TPU v7x, 32 devices: a whole 2x2x4 slice. The times are simulated.
32 devices in a mesh: seq: 16 (over z, y, core), tensor: 2 (over x).
Axes of the slice: x: 2, y: 2, z: 4, core: 2. Of those that a mesh axis runs over, the one named last changes fastest.
Arguments:
- hidden_in: bfloat16 [4096, 8192], P('seq', 'tensor'), may hold values from -6 to 6
- frozen_query: bfloat16 [4096, 8192], P('seq', 'tensor'), may hold values from -48 to 48
- key_base: bfloat16 [4096, 1024], P('seq', 'tensor'), may hold values from -6 to 6
- frozen_value: bfloat16 [4096, 1024], P('seq', 'tensor'), may hold values from -6 to 6
- down_query: bfloat16 [8192, 16], P('tensor'), may hold values from -0.0625 to 0.0625
- query_upper_factor: bfloat16 [16, 8192], P(None, 'tensor'), may hold values from -1.5 to 1.5
- down_value: bfloat16 [8192, 16], P('tensor'), may hold values from -0.0625 to 0.0625
- value_upper_factor: bfloat16 [16, 1024], P(None, 'tensor'), may hold values from -1.5 to 1.5
- grad_output: bfloat16 [4096, 8192], P('seq', 'tensor'), may hold values from -6 to 6
Outputs:
- attention: bfloat16 [4096, 8192], P('seq', 'tensor')
- grad_down_query: float32 [8192, 16], P('tensor')
- gradient_query_upper: float32 [16, 8192], P(None, 'tensor')
- grad_down_value: float32 [8192, 16], P('tensor')
- gradient_value_upper: float32 [16, 1024], P(None, 'tensor')
All inputs are finite; a program needn't handle non-finite values.
Results may differ from a plain program's by a relative error of at most 0.024.
Values may be sent and summed in bfloat16 or wider, within the bound.
No kernel may reach another device: no remote copies, remote signals or barrier semaphores. Data moves between devices by JAX's collectives and lax.ppermute only.
A program may use at most 192 MiB of HBM per device.

v0:
```python
import jax
import jax.numpy as jnp
from jax import lax
from jax.sharding import PartitionSpec as P

HD = 128
GROUP = 2048


ADAPTER_SCALE = 0.5


def passed_along(block, axis, distance):
    devices = range(lax.axis_size(axis))
    route = [((i - distance) % len(devices), i) for i in devices]
    return lax.ppermute(block, axis, route)


def per_device(
    hidden_in,
    frozen_query,
    key_base,
    frozen_value,
    down_query,
    query_upper_factor,
    down_value,
    value_upper_factor,
    grad_output,
):
    rows_here = hidden_in.shape[0]
    seq_count = lax.axis_size("seq")
    heads_here = frozen_query.shape[1] // HD
    kv_here = key_base.shape[1] // HD
    per_head = heads_here // kv_here
    width_q = heads_here * HD
    width_kv = kv_here * HD
    scale_inv = float(HD) ** (-0.5)
    group_blocks = GROUP // rows_here
    half_blocks = group_blocks // 2
    part_q = jnp.dot(hidden_in, down_query, preferred_element_type=jnp.float32)
    part_v = jnp.dot(hidden_in, down_value, preferred_element_type=jnp.float32)
    sum_q, sum_v = lax.psum((part_q, part_v), "tensor")
    reduced_query = sum_q.astype(jnp.bfloat16)
    reduced_value = sum_v.astype(jnp.bfloat16)
    query_matrix = (
        frozen_query.astype(jnp.float32)
        + ADAPTER_SCALE
        * jnp.dot(reduced_query, query_upper_factor, preferred_element_type=jnp.float32)
    ).astype(jnp.bfloat16)
    value_rows = (
        frozen_value.astype(jnp.float32)
        + ADAPTER_SCALE
        * jnp.dot(reduced_value, value_upper_factor, preferred_element_type=jnp.float32)
    ).astype(jnp.bfloat16)
    shifted = lax.axis_index("tensor") >= lax.axis_size("tensor") // 2
    offset_blocks = jnp.where(shifted, half_blocks, 0).astype(jnp.int32)
    frame_block = (lax.axis_index("seq") - offset_blocks) % seq_count
    place_in_group = frame_block % group_blocks
    own_pair = jnp.concatenate((key_base, value_rows), axis=1)
    pair_blocks = [own_pair]
    for distance in range(1, group_blocks):
        pair_blocks.append(passed_along(own_pair, "seq", distance))
    query_rows = query_matrix.reshape(rows_here, kv_here, per_head, HD)
    upstream_rows = grad_output.reshape(rows_here, kv_here, per_head, HD)
    causal = jnp.arange(rows_here)[:, None] >= jnp.arange(rows_here)[None, :]
    key_list = []
    value_list = []
    kept_scores = []
    for distance in range(group_blocks):
        piece = pair_blocks[distance]
        block_keys = piece[:, :width_kv].reshape(rows_here, kv_here, HD)
        block_values = piece[:, width_kv:].reshape(rows_here, kv_here, HD)
        key_list.append(block_keys)
        value_list.append(block_values)
        scores = (
            jnp.einsum("tgpd,sgd->gpts", query_rows, block_keys, preferred_element_type=jnp.float32)
            * scale_inv
        )
        allow = causal if distance == 0 else place_in_group >= distance
        kept_scores.append(jnp.where(allow, scores, -jnp.inf))
    row_max = jnp.max(kept_scores[0], axis=-1, keepdims=True)
    for distance in range(1, group_blocks):
        row_max = jnp.maximum(row_max, jnp.max(kept_scores[distance], axis=-1, keepdims=True))
    row_total = jnp.sum(jnp.exp(kept_scores[0] - row_max), axis=-1, keepdims=True)
    for distance in range(1, group_blocks):
        row_total = row_total + jnp.sum(
            jnp.exp(kept_scores[distance] - row_max), axis=-1, keepdims=True
        )
    lse = row_max + jnp.log(row_total)
    prob_list = []
    prob_bf_list = []
    out_sum = jnp.zeros((rows_here, kv_here, per_head, HD), jnp.float32)
    for distance in range(group_blocks):
        probs = jnp.exp(kept_scores[distance] - lse)
        kept_scores[distance] = None
        probs_bf = probs.astype(jnp.bfloat16)
        prob_list.append(probs)
        prob_bf_list.append(probs_bf)
        out_sum = out_sum + jnp.einsum(
            "gpts,sgd->tgpd", probs_bf, value_list[distance], preferred_element_type=jnp.float32
        )
    output_bf = out_sum.astype(jnp.bfloat16)
    row_delta = jnp.sum(upstream_rows.astype(jnp.float32) * output_bf.astype(jnp.float32), axis=-1)
    delta_cols = jnp.transpose(row_delta, (1, 2, 0))[..., None]
    grad_query_sum = jnp.zeros((rows_here, kv_here, per_head, HD), jnp.float32)
    value_parts = []
    for distance in range(group_blocks):
        grad_probs = jnp.einsum(
            "tgpd,sgd->gpts",
            upstream_rows,
            value_list[distance],
            preferred_element_type=jnp.float32,
        )
        grad_scores = (prob_list[distance] * (grad_probs - delta_cols) * scale_inv).astype(
            jnp.bfloat16
        )
        grad_query_sum = grad_query_sum + jnp.einsum(
            "gpts,sgd->tgpd", grad_scores, key_list[distance], preferred_element_type=jnp.float32
        )
        value_parts.append(
            jnp.einsum(
                "gpts,tgpd->sgd",
                prob_bf_list[distance],
                upstream_rows,
                preferred_element_type=jnp.float32,
            )
        )
    grad_value_sum = value_parts[0]
    for distance in range(1, group_blocks):
        grad_value_sum = grad_value_sum + passed_along(
            value_parts[distance], "seq", seq_count - distance
        )
    attention = output_bf.reshape(rows_here, width_q)
    query_gradient_rows = grad_query_sum.reshape(rows_here, width_q).astype(jnp.bfloat16)
    value_gradient_rows = grad_value_sum.reshape(rows_here, width_kv).astype(jnp.bfloat16)
    head_q = jnp.dot(query_gradient_rows, query_upper_factor.T, preferred_element_type=jnp.float32)
    head_v = jnp.dot(value_gradient_rows, value_upper_factor.T, preferred_element_type=jnp.float32)
    returned_query_rows, returned_value_rows = lax.psum((head_q, head_v), "tensor")
    restored_query = (ADAPTER_SCALE * returned_query_rows).astype(jnp.bfloat16)
    restored_value = (ADAPTER_SCALE * returned_value_rows).astype(jnp.bfloat16)
    resident_query_upper = (
        jnp.dot(reduced_query.T, query_gradient_rows, preferred_element_type=jnp.float32)
        * ADAPTER_SCALE
    )
    resident_value_upper = (
        jnp.dot(reduced_value.T, value_gradient_rows, preferred_element_type=jnp.float32)
        * ADAPTER_SCALE
    )
    local_down_q = jnp.dot(hidden_in.T, restored_query, preferred_element_type=jnp.float32)
    local_down_v = jnp.dot(hidden_in.T, restored_value, preferred_element_type=jnp.float32)
    gradient_query_upper, gradient_value_upper, grad_down_query, grad_down_value = (
        lax.psum(resident_query_upper.astype(jnp.bfloat16), "seq").astype(jnp.float32),
        lax.psum(resident_value_upper.astype(jnp.bfloat16), "seq").astype(jnp.float32),
        lax.psum(local_down_q.astype(jnp.bfloat16), "seq").astype(jnp.float32),
        lax.psum(local_down_v.astype(jnp.bfloat16), "seq").astype(jnp.float32),
    )
    return (attention, grad_down_query, gradient_query_upper, grad_down_value, gradient_value_upper)


def solution(mesh):
    placed = (
        P("seq", "tensor"),
        P("seq", "tensor"),
        P("seq", "tensor"),
        P("seq", "tensor"),
        P("tensor", None),
        P(None, "tensor"),
        P("tensor", None),
        P(None, "tensor"),
        P("seq", "tensor"),
    )
    return jax.shard_map(
        per_device,
        mesh=mesh,
        in_specs=placed,
        out_specs=(
            P("seq", "tensor"),
            P("tensor", None),
            P(None, "tensor"),
            P("tensor", None),
            P(None, "tensor"),
        ),
        check_vma=False,
    )
```

profile of v0, /device:TPU:0, one launch (start us, length us, event | category | flops | bytes accessed | tf_op | source)
XLA Modules:
  0.0 582.3 jit_solution(1124220365772324580)
XLA Ops:
  11.9 9.9 %all-reduce.1 = (bf16[256,16]{0,1:T(8,128)(2,1)S(1)}, bf16[256,16]{0,1:T(8,128)(2,1)S(1)}) all-reduce(f32[256,16]{0,1:T(8,128)S(1)} %fusion.242, f32[256,16]{0,1:T(8,128)S(1)} %fusion.243), channel_id=1, replica_groups=mesh['seq'=16,'tensor'=2] {'tensor'}, use_global_device_ids=true, to_apply=%region_0.0 | all-reduce | flops 8192 | bytes 49152 | tf_op jit(solution)/shard_map/psum | solution.py:42
  38.5 6.9 %bitcast_reduce_fusion.7 = (f32[4,8,256]{2,1,0:T(8,128)S(1)}, f32[4,256,8,256]{1,3,2,0:T(8,128)}) fusion(pred[256,256]{0,1:T(8,128)(4,1)S(1)} %iota_compare_fusion, bf16[256,4,128,1]{0,2,3,1:T(8,128)(2,1)S(1)} %copy.105, bf16[256,4,8,128]{3,2,1,0:T(8,128)(2,1)} %bitcast.384), kind=kOutput, calls=%fused_computation.76 | convolution fusion | flops 543154176 | bytes 10846208 | tf_op jit(solution)/shard_map/tgpd,sgd->gpts/dot_general | solution.py:76
  51.1 57.7 %collective-permute-done.5 = bf16[256,1024]{1,0:T(8,128)(2,1)} collective-permute-done((bf16[256,1024]{1,0:T(8,128)(2,1)}, bf16[256,1024]{1,0:T(8,128)(2,1)}, u32[]{:S(2)}, u32[]{:S(2)}) %collective-permute-start.5) | collective-permute-done | bytes 524320 | tf_op jit(solution)/shard_map/ppermute | solution.py:16
  110.6 14.8 %collective-permute-done.4 = bf16[256,1024]{1,0:T(8,128)(2,1)} collective-permute-done((bf16[256,1024]{1,0:T(8,128)(2,1)}, bf16[256,1024]{1,0:T(8,128)(2,1)}, u32[]{:S(2)}, u32[]{:S(2)}) %collective-permute-start.4) | collective-permute-done | bytes 524320 | tf_op jit(solution)/shard_map/ppermute | solution.py:16
  188.1 24.5 %fusion.43 = (f32[4,8,256]{2,1,0:T(8,128)S(1)}, f32[4,8,256]{2,1,0:T(8,128)S(1)}, f32[4,8,256]{2,1,0:T(8,128)S(1)}, f32[4,8,256]{2,1,0:T(8,128)S(1)}, f32[4,8,25...) fusion(f32[4,256,256,8]{2,1,3,0:T(8,128)S(1)} %get-tuple-element.54, ...), kind=kLoop, calls=%fused_computation.72 | loop fusion | flops 67043328 | bytes 67469320 | tf_op jit(solution)/shard_map/reduce_sum | solution.py:86
  230.4 6.3 %convolution_bitcast_fusion.3 = f32[256,4,128]{0,2,1:T(8,128)} fusion(bf16[256,4,8,128]{0,3,2,1:T(8,128)(2,1)S(1)} %bitcast.412, f32[4,256,256,8]{2,1,3,0:T(8,128)} %get-tuple-element.46, f32[4,8,256]{2,1,0:T(8,128)S(1)} %log_add_fusion, pred[]{:T(512)S(6)} %ge.44), kind=kOutput, calls=%fused_computation.143 | convolution fusion | flops 545259520 | bytes 11042817 | tf_op jit(solution)/shard_map/gpts,tgpd->sgd/dot_general | solution.py:121
  236.7 6.3 %convolution_bitcast_fusion.4 = f32[256,4,128]{0,2,1:T(8,128)} fusion(bf16[256,4,8,128]{0,3,2,1:T(8,128)(2,1)S(1)} %bitcast.413, f32[4,256,256,8]{2,1,3,0:T(8,128)} %get-tuple-element.48, f32[4,8,256]{2,1,0:T(8,128)S(1)} %log_add_fusion, pred[]{:T(512)S(6)} %ge.43), kind=kOutput, calls=%fused_computation.144 | convolution fusion | flops 545259520 | bytes 11042817 | tf_op jit(solution)/shard_map/gpts,tgpd->sgd/dot_general | solution.py:121
  245.8 7.5 %fusion.133 = f32[4,128,8,256]{3,1,2,0:T(8,128)} fusion(bf16[256,4,128,1]{2,1,0,3:T(4,128)(2,1)S(1)} %bitcast.421, f32[4,256,256,8]{2,1,3,0:T(8,128)} %get-tuple-element.42, f32[4,8,256]{2,1,0:T(8,128)S(1)} %log_add_fusion, pred[]{:T(512)S(6)} %ge.46), kind=kOutput, calls=%fused_computation.179 | convolution fusion | flops 545259520 | bytes 12877825 | tf_op jit(solution)/shard_map/gpts,sgd->tgpd/dot_general | solution.py:99
  253.2 7.9 %fusion.135 = f32[4,128,8,256]{3,1,2,0:T(8,128)} fusion(bf16[256,4,128,1]{2,1,0,3:T(4,128)(2,1)S(1)} %bitcast.422, f32[4,256,256,8]{2,1,3,0:T(8,128)} %get-tuple-element.44, f32[4,8,256]{2,1,0:T(8,128)S(1)} %log_add_fusion, pred[]{:T(512)S(6)} %ge.45), kind=kOutput, calls=%fused_computation.181 | convolution fusion | flops 545259520 | bytes 12877825 | tf_op jit(solution)/shard_map/gpts,sgd->tgpd/dot_general | solution.py:99
  281.1 16.7 %multiply_reduce_fusion = (f32[256,4,8]{0,2,1:T(8,128)S(1)}, bf16[4,128,8,256]{3,1,2,0:T(8,128)(2,1)}) fusion(bf16[256,4096]{0,1:T(8,128)(2,1)S(1)} %copy-done.5, f32[4,256,256,8]{2,1,3,0:T(8,128)} %copy-done.1, f32[4,8,256]{2,1,0:T(8,128)S(1)} %log_add_fusion, pred[]{:T(512)S(6)} %ge.47, bf16[256,4,128,1]{2,1,0,3:T(4,128)(2,1)S(1)} %bitcast.419, ...), kind=kOutput, calls=%fused_computation.114 | convolution fusion | flops 557834240 | bytes 42270720 | tf_op jit(solution)/shard_map/gpts,sgd->tgpd/dot_general | solution.py:99
  301.9 9.6 %fusion.74 = f32[4,128,8,256]{3,1,2,0:T(8,128)} fusion(bf16[256,4,128,1]{0,2,3,1:T(8,128)(2,1)} %copy.122, f32[4,256,256,8]{2,1,3,0:T(8,128)} %get-tuple-element.42, f32[4,8,256]{2,1,0:T(8,128)S(1)} %bitcast.437, f32[4,8,256]{2,1,0:T(8,128)S(1)} %log_add_fusion, pred[]{:T(512)S(6)} %ge.46, bf16[256,4,8,128]{0,3,2,1:T(8,128)(2,1)} %bitcast.401, ...), kind=kOutput, calls=%fused_computation.121 | convolution fusion | flops 1088421888 | bytes 15269889 | tf_op jit(solution)/shard_map/gpts,sgd->tgpd/dot_general | solution.py:117
  311.5 9.4 %fusion.72 = f32[4,128,8,256]{3,1,2,0:T(8,128)} fusion(bf16[256,4,128,1]{0,2,3,1:T(8,128)(2,1)S(1)} %copy-done.19, f32[4,256,256,8]{2,1,3,0:T(8,128)} %get-tuple-element.44, f32[4,8,256]{2,1,0:T(8,128)S(1)} %bitcast.438, f32[4,8,256]{2,1,0:T(8,128)S(1)} %log_add_fusion, pred[]{:T(512)S(6)} %ge.45, bf16[256,4,8,128]{0,3,2,1:T(8,128)(2,1)} %bitcast.402, ...), kind=kOutput, calls=%fused_computation.120 | convolution fusion | flops 1088421888 | bytes 15269889 | tf_op jit(solution)/shard_map/gpts,sgd->tgpd/dot_general | solution.py:117
  320.9 9.5 %fusion.70 = f32[4,128,8,256]{3,1,2,0:T(8,128)} fusion(bf16[256,4,128,1]{0,2,3,1:T(8,128)(2,1)S(1)} %copy-done.21, f32[4,256,256,8]{2,1,3,0:T(8,128)} %get-tuple-element.46, f32[4,8,256]{2,1,0:T(8,128)S(1)} %bitcast.439, f32[4,8,256]{2,1,0:T(8,128)S(1)} %log_add_fusion, pred[]{:T(512)S(6)} %ge.44, bf16[256,4,8,128]{0,3,2,1:T(8,128)(2,1)} %bitcast.403, ...), kind=kOutput, calls=%fused_computation.119 | convolution fusion | flops 1088421888 | bytes 15269889 | tf_op jit(solution)/shard_map/gpts,sgd->tgpd/dot_general | solution.py:117
  330.5 9.6 %fusion.68 = f32[4,128,8,256]{3,1,2,0:T(8,128)} fusion(bf16[256,4,128,1]{0,2,3,1:T(8,128)(2,1)S(1)} %copy-done.23, f32[4,256,256,8]{2,1,3,0:T(8,128)} %get-tuple-element.48, f32[4,8,256]{2,1,0:T(8,128)S(1)} %bitcast.440, f32[4,8,256]{2,1,0:T(8,128)S(1)} %log_add_fusion, pred[]{:T(512)S(6)} %ge.43, bf16[256,4,8,128]{0,3,2,1:T(8,128)(2,1)} %bitcast.404, ...), kind=kOutput, calls=%fused_computation.118 | convolution fusion | flops 1088421888 | bytes 15269889 | tf_op jit(solution)/shard_map/gpts,sgd->tgpd/dot_general | solution.py:117
  340.1 9.6 %fusion.66 = f32[4,128,8,256]{3,1,2,0:T(8,128)} fusion(bf16[256,4,128,1]{0,2,3,1:T(8,128)(2,1)S(1)} %copy-done.25, f32[4,256,256,8]{2,1,3,0:T(8,128)} %get-tuple-element.50, f32[4,8,256]{2,1,0:T(8,128)S(1)} %bitcast.441, f32[4,8,256]{2,1,0:T(8,128)S(1)} %log_add_fusion, pred[]{:T(512)S(6)} %ge.42, bf16[256,4,8,128]{0,3,2,1:T(8,128)(2,1)} %bitcast.405, ...), kind=kOutput, calls=%fused_computation.117 | convolution fusion | flops 1088421888 | bytes 15269889 | tf_op jit(solution)/shard_map/gpts,sgd->tgpd/dot_general | solution.py:117
  349.6 9.5 %fusion.64 = f32[4,128,8,256]{3,1,2,0:T(8,128)} fusion(bf16[256,4,128,1]{0,2,3,1:T(8,128)(2,1)S(1)} %copy-done.27, f32[4,256,256,8]{2,1,3,0:T(8,128)} %copy-done.3, f32[4,8,256]{2,1,0:T(8,128)S(1)} %bitcast.442, f32[4,8,256]{2,1,0:T(8,128)S(1)} %log_add_fusion, pred[]{:T(512)S(6)} %ge.41, bf16[256,4,8,128]{0,3,2,1:T(8,128)(2,1)} %bitcast.406, ...), kind=kOutput, calls=%fused_computation.116 | convolution fusion | flops 1088421888 | bytes 15269889 | tf_op jit(solution)/shard_map/gpts,sgd->tgpd/dot_general | solution.py:117
  359.2 9.6 %fusion.62 = f32[4,8,256,128]{2,3,1,0:T(8,128)} fusion(bf16[256,4,128,1]{0,2,3,1:T(8,128)(2,1)S(1)} %copy-done.32, f32[4,256,8,256]{1,3,2,0:T(8,128)} %get-tuple-element.52, f32[4,8,256]{2,1,0:T(8,128)S(1)} %bitcast.443, f32[4,8,256]{2,1,0:T(8,128)S(1)} %log_add_fusion, pred[256,256]{0,1:T(8,128)(4,1)S(1)} %iota_compare_fusion, ...), kind=kOutput, calls=%fused_computation.115 | convolution fusion | flops 1088421888 | bytes 15335424 | tf_op jit(solution)/shard_map/gpts,sgd->tgpd/dot_general | solution.py:117
  368.8 7.4 %collective-permute-start.10 = (f32[256,4,128]{0,2,1:T(8,128)}, f32[256,4,128]{0,2,1:T(8,128)}, u32[]{:S(2)}, u32[]{:S(2)}) collective-permute-start(f32[256,4,128]{0,2,1:T(8,128)} %convolution_bitcast_fusion.3), channel_id=1, source_target_pairs={{8,0},{10,2},{12,4},{14,6},{16,8},{18,10},{20,12},{22,14},{24,16},... | collective-permute-start | bytes 1572872 | tf_op jit(solution)/shard_map/ppermute | solution.py:16
  376.2 16.3 %fusion.61 = bf16[256,4,8,128]{0,3,2,1:T(8,128)(2,1)} fusion(f32[4,128,8,256]{3,1,2,0:T(8,128)} %fusion.74, f32[4,128,8,256]{3,1,2,0:T(8,128)} %fusion.72, f32[4,128,8,256]{3,1,2,0:T(8,128)} %fusion.70, f32[4,128,8,256]{3,1,2,0:T(8,128)} %fusion.68, f32[4,128,8,256]{3,1,2,0:T(8,128)} %fusion.66, f32[4,128,8,256]{3,1,2,0:T(8,128)} %fusion.64, ...), kind=kOutput, calls=%fused_computation.106 | convolution fusion | flops 1096810496 | bytes 42532864 | tf_op jit(solution)/shard_map/gpts,sgd->tgpd/dot_general | solution.py:117
  398.6 37.5 %collective-permute-start.8 = (f32[256,4,128]{0,2,1:T(8,128)S(1)}, f32[256,4,128]{0,2,1:T(8,128)S(1)}, u32[]{:S(2)}, u32[]{:S(2)}) collective-permute-start(f32[256,4,128]{0,2,1:T(8,128)S(1)} %copy-done.42), channel_id=1, source_target_pairs={{4,0},{6,2},{8,4},{10,6},{12,8},{14,10},{16,12},{18,14},{20,16},{2... | collective-permute-start | bytes 1572872 | tf_op jit(solution)/shard_map/ppermute | solution.py:16
  436.1 16.7 %collective-permute-start.7 = (f32[256,4,128]{0,2,1:T(8,128)S(1)}, f32[256,4,128]{0,2,1:T(8,128)S(1)}, u32[]{:S(2)}, u32[]{:S(2)}) collective-permute-start(f32[256,4,128]{0,2,1:T(8,128)S(1)} %convolution_bitcast_fusion.6), channel_id=1, source_target_pairs={{2,0},{4,2},{6,4},{8,6},{10,8},{12,10},{14,12},{16,14},{18,16},{20... | collective-permute-start | bytes 1572872 | tf_op jit(solution)/shard_map/ppermute | solution.py:16
  465.9 10.2 %all-reduce = (f32[256,16]{1,0:T(8,128)S(1)}, f32[256,16]{1,0:T(8,128)S(1)}) all-reduce(f32[256,16]{1,0:T(8,128)S(1)} %fusion.244, f32[256,16]{1,0:T(8,128)S(1)} %fusion.245), channel_id=1, replica_groups=mesh['seq'=16,'tensor'=2] {'tensor'}, use_global_device_ids=true, to_apply=%region_19.20 | all-reduce | flops 8192 | bytes 65536 | tf_op jit(solution)/shard_map/psum | solution.py:138
  478.4 61.2 %psum.63 = bf16[16,512]{1,0:T(8,128)(2,1)S(1)} all-reduce(bf16[16,512]{1,0:T(8,128)(2,1)S(1)} %fusion.115), channel_id=1, replica_groups=mesh['seq'=16,'tensor'=2] {'seq'}, use_global_device_ids=true, to_apply=%region_24.25 | all-reduce | flops 8192 | bytes 32768 | tf_op jit(solution)/shard_map/psum | solution.py:153
  540.2 30.0 %all-reduce.5.cloned.1.call-done = (bf16[4096,16]{0,1:T(8,128)(2,1)}, bf16[16,4096]{1,0:T(8,128)(2,1)}, bf16[4096,16]{0,1:T(8,128)(2,1)}) async-done(((bf16[4096,16]{0,1:T(8,128)(2,1)}, bf16[16,4096]{1,0:T(8,128)(2,1)}, bf16[4096,16]{0,1:T(8,128)(2,1)}), (bf16[4096,16]{0,1:T(8,128)(2,1)}, bf16[16,4096]{1,0:T(8,128)(2,1)}, bf16[4096,16]{0,1:T(8,128)(2,1)})) %all-reduce.5.cloned.1.call-update) | async-done | bytes 393232 | tf_op jit(solution)/shard_map/psum | solution.py:154
  (209 shorter events, 162.9 us)
Async XLA Ops:
  7.2 27.6 %copy-start.28 = (bf16[256,512]{1,0:T(8,128)(2,1)S(1)}, bf16[256,512]{1,0:T(8,128)(2,1)}, u32[]{:S(2)}) copy-start(bf16[256,512]{1,0:T(8,128)(2,1)} %param.11) | copy-start | bytes 786436
  7.2 563.0 %all-reduce.5.cloned.1.call-start = ((), (), s32[]{:S(2)}) async-start(), calls=%async_computation | async-start | bytes 786432 | tf_op jit(solution)/shard_map/psum | solution.py:154
  24.9 118.8 %collective-permute-start.6 = (bf16[256,1024]{1,0:T(8,128)(2,1)}, bf16[256,1024]{1,0:T(8,128)(2,1)}, u32[]{:S(2)}, u32[]{:S(2)}) collective-permute-start(bf16[256,1024]{1,0:T(8,128)(2,1)} %pad_maximum_fusion), channel_id=1, source_target_pairs={{18,0},{20,2},{22,4},{24,6},{26,8},{28,10},{30,12},{0,14},{2,16},{... | collective-permute-start | bytes 1572872 | tf_op jit(solution)/shard_map/ppermute | solution.py:16
  24.9 83.9 %collective-permute-start.5 = (bf16[256,1024]{1,0:T(8,128)(2,1)}, bf16[256,1024]{1,0:T(8,128)(2,1)}, u32[]{:S(2)}, u32[]{:S(2)}) collective-permute-start(bf16[256,1024]{1,0:T(8,128)(2,1)} %pad_maximum_fusion), channel_id=1, source_target_pairs={{20,0},{22,2},{24,4},{26,6},{28,8},{30,10},{0,12},{2,14},{4,16},{6... | collective-permute-start | bytes 1572872 | tf_op jit(solution)/shard_map/ppermute | solution.py:16
  27.3 98.1 %collective-permute-start.4 = (bf16[256,1024]{1,0:T(8,128)(2,1)}, bf16[256,1024]{1,0:T(8,128)(2,1)}, u32[]{:S(2)}, u32[]{:S(2)}) collective-permute-start(bf16[256,1024]{1,0:T(8,128)(2,1)} %pad_maximum_fusion), channel_id=1, source_target_pairs={{22,0},{24,2},{26,4},{28,6},{30,8},{0,10},{2,12},{4,14},{6,16},{8,... | collective-permute-start | bytes 1572872 | tf_op jit(solution)/shard_map/ppermute | solution.py:16
  28.6 98.7 %collective-permute-start.3 = (bf16[256,1024]{1,0:T(8,128)(2,1)}, bf16[256,1024]{1,0:T(8,128)(2,1)}, u32[]{:S(2)}, u32[]{:S(2)}) collective-permute-start(bf16[256,1024]{1,0:T(8,128)(2,1)} %pad_maximum_fusion), channel_id=1, source_target_pairs={{24,0},{26,2},{28,4},{30,6},{0,8},{2,10},{4,12},{6,14},{8,16},{10,... | collective-permute-start | bytes 1572872 | tf_op jit(solution)/shard_map/ppermute | solution.py:16
  30.2 98.9 %collective-permute-start.2 = (bf16[256,1024]{1,0:T(8,128)(2,1)}, bf16[256,1024]{1,0:T(8,128)(2,1)}, u32[]{:S(2)}, u32[]{:S(2)}) collective-permute-start(bf16[256,1024]{1,0:T(8,128)(2,1)} %pad_maximum_fusion), channel_id=1, source_target_pairs={{26,0},{28,2},{30,4},{0,6},{2,8},{4,10},{6,12},{8,14},{10,16},{12,... | collective-permute-start | bytes 1572872 | tf_op jit(solution)/shard_map/ppermute | solution.py:16
  108.8 28.3 %collective-permute-start.1 = (bf16[256,1024]{1,0:T(8,128)(2,1)}, bf16[256,1024]{1,0:T(8,128)(2,1)}, u32[]{:S(2)}, u32[]{:S(2)}) collective-permute-start(bf16[256,1024]{1,0:T(8,128)(2,1)} %pad_maximum_fusion), channel_id=1, source_target_pairs={{28,0},{30,2},{0,4},{2,6},{4,8},{6,10},{8,12},{10,14},{12,16},{14,... | collective-permute-start | bytes 1572872 | tf_op jit(solution)/shard_map/ppermute | solution.py:16
  125.4 15.0 %collective-permute-start = (bf16[256,1024]{1,0:T(8,128)(2,1)}, bf16[256,1024]{1,0:T(8,128)(2,1)}, u32[]{:S(2)}, u32[]{:S(2)}) collective-permute-start(bf16[256,1024]{1,0:T(8,128)(2,1)} %pad_maximum_fusion), channel_id=1, source_target_pairs={{30,0},{0,2},{2,4},{4,6},{6,8},{8,10},{10,12},{12,14},{14,16},{16,... | collective-permute-start | bytes 1572872 | tf_op jit(solution)/shard_map/ppermute | solution.py:16
  159.7 53.9 %copy-start.1 = (f32[4,256,256,8]{2,1,3,0:T(8,128)}, f32[4,256,256,8]{2,1,3,0:T(8,128)S(1)}, u32[]{:S(2)}) copy-start(f32[4,256,256,8]{2,1,3,0:T(8,128)S(1)} %get-tuple-element.40) | copy-start | bytes 25165828
  188.1 89.0 %copy-start.3 = (f32[4,256,256,8]{2,1,3,0:T(8,128)}, f32[4,256,256,8]{2,1,3,0:T(8,128)S(1)}, u32[]{:S(2)}) copy-start(f32[4,256,256,8]{2,1,3,0:T(8,128)S(1)} %get-tuple-element.54) | copy-start | bytes 25165828
  359.2 17.0 %copy-start.8 = (bf16[256,4,128,1]{2,1,0,3:T(4,128)(2,1)S(1)}, bf16[256,4,128,1]{2,1,0,3:T(4,128)(2,1)}, u32[]{:S(2)}) copy-start(bf16[256,4,128,1]{2,1,0,3:T(4,128)(2,1)} %reshape.201) | copy-start | bytes 786436
  368.8 29.8 %collective-permute-start.13 = (f32[256,4,128]{0,2,1:T(8,128)}, f32[256,4,128]{0,2,1:T(8,128)S(1)}, u32[]{:S(2)}, u32[]{:S(2)}) collective-permute-start(f32[256,4,128]{0,2,1:T(8,128)} %convolution_bitcast_fusion), channel_id=1, source_target_pairs={{14,0},{16,2},{18,4},{20,6},{22,8},{24,10},{26,12},{28,14},{30,16}... | collective-permute-start | bytes 1572872 | tf_op jit(solution)/shard_map/ppermute | solution.py:16
  368.8 67.3 %collective-permute-start.12 = (f32[256,4,128]{0,2,1:T(8,128)}, f32[256,4,128]{0,2,1:T(8,128)}, u32[]{:S(2)}, u32[]{:S(2)}) collective-permute-start(f32[256,4,128]{0,2,1:T(8,128)} %convolution_bitcast_fusion.1), channel_id=1, source_target_pairs={{12,0},{14,2},{16,4},{18,6},{20,8},{22,10},{24,12},{26,14},{28,16}... | collective-permute-start | bytes 1572872 | tf_op jit(solution)/shard_map/ppermute | solution.py:16
  368.8 86.1 %collective-permute-start.11 = (f32[256,4,128]{0,2,1:T(8,128)}, f32[256,4,128]{0,2,1:T(8,128)}, u32[]{:S(2)}, u32[]{:S(2)}) collective-permute-start(f32[256,4,128]{0,2,1:T(8,128)} %convolution_bitcast_fusion.2), channel_id=1, source_target_pairs={{10,0},{12,2},{14,4},{16,6},{18,8},{20,10},{22,12},{24,14},{26,16}... | collective-permute-start | bytes 1572872 | tf_op jit(solution)/shard_map/ppermute | solution.py:16
  368.8 86.1 %collective-permute-start.10 = (f32[256,4,128]{0,2,1:T(8,128)}, f32[256,4,128]{0,2,1:T(8,128)}, u32[]{:S(2)}, u32[]{:S(2)}) collective-permute-start(f32[256,4,128]{0,2,1:T(8,128)} %convolution_bitcast_fusion.3), channel_id=1, source_target_pairs={{8,0},{10,2},{12,4},{14,6},{16,8},{18,10},{20,12},{22,14},{24,16},... | collective-permute-start | bytes 1572872 | tf_op jit(solution)/shard_map/ppermute | solution.py:16
  376.1 78.7 %collective-permute-start.9 = (f32[256,4,128]{0,2,1:T(8,128)}, f32[256,4,128]{0,2,1:T(8,128)}, u32[]{:S(2)}, u32[]{:S(2)}) collective-permute-start(f32[256,4,128]{0,2,1:T(8,128)} %convolution_bitcast_fusion.4), channel_id=1, source_target_pairs={{6,0},{8,2},{10,4},{12,6},{14,8},{16,10},{18,12},{20,14},{22,16},{... | collective-permute-start | bytes 1572872 | tf_op jit(solution)/shard_map/ppermute | solution.py:16
  392.4 60.3 %copy-start.7 = (bf16[256,4,8,128]{0,3,2,1:T(8,128)(2,1)S(1)}, bf16[256,4,8,128]{0,3,2,1:T(8,128)(2,1)}, u32[]{:S(2)}) copy-start(bf16[256,4,8,128]{0,3,2,1:T(8,128)(2,1)} %fusion.61) | copy-start | bytes 6291460
  392.4 60.3 %copy-start.39 = (bf16[256,16]{0,1:T(8,128)(2,1)S(1)}, bf16[256,16]{0,1:T(8,128)(2,1)}, u32[]{:S(2)}) copy-start(bf16[256,16]{0,1:T(8,128)(2,1)} %copy-done.38) | copy-start | bytes 24580
  392.4 61.6 %copy-start.36 = (bf16[16,4096]{1,0:T(8,128)(2,1)S(1)}, bf16[16,4096]{1,0:T(8,128)(2,1)}, u32[]{:S(2)}) copy-start(bf16[16,4096]{1,0:T(8,128)(2,1)} %param.14) | copy-start | bytes 393220
  392.5 67.0 %copy-start.6 = (bf16[256,4096]{0,1:T(8,128)(2,1)S(1)}, bf16[256,4096]{0,1:T(8,128)(2,1)}, u32[]{:S(2)}) copy-start(bf16[256,4096]{0,1:T(8,128)(2,1)} %copy.46) | copy-start | bytes 6291460
  398.6 56.3 %collective-permute-start.8 = (f32[256,4,128]{0,2,1:T(8,128)S(1)}, f32[256,4,128]{0,2,1:T(8,128)S(1)}, u32[]{:S(2)}, u32[]{:S(2)}) collective-permute-start(f32[256,4,128]{0,2,1:T(8,128)S(1)} %copy-done.42), channel_id=1, source_target_pairs={{4,0},{6,2},{8,4},{10,6},{12,8},{14,10},{16,12},{18,14},{20,16},{2... | collective-permute-start | bytes 1572872 | tf_op jit(solution)/shard_map/ppermute | solution.py:16
  436.1 23.4 %collective-permute-start.7 = (f32[256,4,128]{0,2,1:T(8,128)S(1)}, f32[256,4,128]{0,2,1:T(8,128)S(1)}, u32[]{:S(2)}, u32[]{:S(2)}) collective-permute-start(f32[256,4,128]{0,2,1:T(8,128)S(1)} %convolution_bitcast_fusion.6), channel_id=1, source_target_pairs={{2,0},{4,2},{6,4},{8,6},{10,8},{12,10},{14,12},{16,14},{18,16},{20... | collective-permute-start | bytes 1572872 | tf_op jit(solution)/shard_map/ppermute | solution.py:16
  454.8 23.4 %copy-start.41 = (bf16[256,16]{0,1:T(8,128)(2,1)S(1)}, bf16[256,16]{0,1:T(8,128)(2,1)}, u32[]{:S(2)}) copy-start(bf16[256,16]{0,1:T(8,128)(2,1)} %copy-done.40) | copy-start | bytes 24580
  (42 other events, 338.5 us)
Sparse Core Ops, SparseCore 0:
  478.4 91.7 all-reduce.4
where the time goes:
time: 588 us; the launch traced here: 582 us
  matrix products  231 us (39%)
  waiting for transfers between devices  107 us (18%)
  blocking collectives  81.3 us (14%)
  starting transfers between devices  68 us (12%)
  local copies, waits for them, and re-layouts  47.3 us (8%)
  other arithmetic  32.9 us (6%)
  between operations  15 us (3%)
    dot_general x8, matrix products, per_device(): jnp.einsum('gpts,sgd->tgpd', grad_scores, key_list[distance], preferred_e...  83.1 us
    ppermute x14, waiting for transfers between devices, passed_along(): return lax.ppermute(block, axis, route)  77.2 us
    ppermute x14, starting transfers between devices, passed_along(): return lax.ppermute(block, axis, route)  67.9 us
    psum x1, blocking collectives, per_device(): lax.psum(resident_value_upper.astype(jnp.bfloat16), 'seq')  61.2 us
    dot_general x8, matrix products, per_device(): jnp.einsum('gpts,sgd->tgpd', probs_bf, value_list[distance], preferred_el...  51.9 us
    dot_general x8, matrix products, per_device(): jnp.einsum('gpts,tgpd->sgd', prob_bf_list[distance], upstream_rows, prefe...  44.4 us
    dot_general x8, matrix products, per_device(): jnp.einsum('tgpd,sgd->gpts', query_rows, block_keys, preferred_element_ty...  38.8 us
    psum x1, waiting for transfers between devices, per_device(): lax.psum(local_down_q.astype(jnp.bfloat16), 'seq').astype(jnp.float32)  30 us
  transfers between devices with their start and end apart: 15, of which 4 were waited for; matrix products, arithmetic and copies ran while one was open for 11% of the time, Pallas kernels for 0%

commit v1 on v0

v1 whole, which is shorter than its diff:
```python
import functools

import jax
import jax.numpy as jnp
from jax import lax
from jax.experimental import pallas as pl
from jax.experimental.pallas import tpu as pltpu
from jax.sharding import PartitionSpec as P

HD = 128
GROUP = 2048
ADAPTER_SCALE = 0.5
LOG2E = 1.4426950408889634
MASKED = -1e30

F32 = jnp.float32
BF16 = jnp.bfloat16
NN = (((1,), (0,)), ((), ()))
NT = (((1,), (1,)), ((), ()))

AXES = ("seq", "tensor")


def dot(a, b, dims):
    return lax.dot_general(a, b, dims, preferred_element_type=F32)


def attention_body(rows, per_head, pieces, where, *refs):
    frozen, low_q, low_q_t, up_q, up_v, low_v, grad_out = refs[:7]
    keys = refs[7 : 7 + pieces]
    values = refs[7 + pieces : 7 + 2 * pieces]
    out, grad_up_q, back_q, back_v, grad_up_v = refs[7 + 2 * pieces : 12 + 2 * pieces]
    scores, probs, wide_v, grad_v = refs[12 + 2 * pieces :]
    scale = float(HD) ** -0.5
    place, y_bit, z_bit = where[0], where[1], where[2]
    for j in range(pieces):
        wide_v[j * rows : (j + 1) * rows, :HD] = values[j][...]
        wide_v[j * rows : (j + 1) * rows, HD:] = jnp.ones((rows, HD), BF16)
    grad_v[...] = jnp.zeros_like(grad_v)

    @pl.when(pl.program_id(0) == 0)
    def _():
        back_q[...] = jnp.zeros_like(back_q)
        back_v[...] = jnp.zeros_like(back_v)

    row_at = lax.broadcasted_iota(jnp.int32, (rows, rows), 0)
    col_at = lax.broadcasted_iota(jnp.int32, (rows, rows), 1)

    def heads_over(blocks):
        def one_head(h, carry):
            cols = pl.ds(pl.multiple_of(h * HD, HD), HD)
            up = up_q[:, cols]
            query = (frozen[:, cols].astype(F32) + ADAPTER_SCALE * dot(low_q[...], up, NN)).astype(BF16)
            top = None
            for j in blocks:
                s = dot(query, keys[j][...], NT) * (scale * LOG2E)
                if j == 0:
                    s = jnp.where(row_at >= col_at, s, MASKED)
                if j == 1:
                    s = jnp.where(place > 0, s, MASKED)
                scores[:, j * rows : (j + 1) * rows] = s
                top = s if top is None else jnp.maximum(top, s)
            row_max = jnp.max(top, axis=1, keepdims=True)
            total = jnp.zeros((rows, 2 * HD), F32)
            for j in blocks:
                e = jnp.exp2(scores[:, j * rows : (j + 1) * rows] - row_max).astype(BF16)
                probs[:, j * rows : (j + 1) * rows] = e
                total = total + dot(e, wide_v[j * rows : (j + 1) * rows, :], NN)
            inverse = 1.0 / total[:, HD:]
            attended = (total[:, :HD] * inverse).astype(BF16)
            out[:, cols] = attended
            upstream = grad_out[:, cols]
            upstream_f = upstream.astype(F32)
            delta = jnp.sum(upstream_f * attended.astype(F32), axis=1, keepdims=True)
            normed_t = (upstream_f * inverse).astype(BF16).T
            grad_query = jnp.zeros((rows, HD), F32)
            for j in blocks:
                grad_probs = dot(upstream, values[j][...], NT)
                e = probs[:, j * rows : (j + 1) * rows]
                grad_s = (e.astype(F32) * (grad_probs - delta)).astype(BF16)
                grad_query = grad_query + dot(grad_s, keys[j][...], NN)
                grad_v[:, j * rows : (j + 1) * rows] += dot(normed_t, e, NN)
            grad_query = (grad_query * (inverse * scale)).astype(BF16)
            grad_up_q[:, cols] = ADAPTER_SCALE * dot(low_q_t[...], grad_query, NN)
            back_q[...] += ADAPTER_SCALE * dot(up, grad_query, NT)
            return carry

        lax.fori_loop(0, per_head, one_head, 0, unroll=2)

    for y in (0, 1):
        for z in (0, 1):

            @pl.when((y_bit == y) & (z_bit == z))
            def _():
                blocks = [0, 1]
                if y:
                    blocks += [2, 3]
                if z:
                    blocks += [4, 5, 6, 7]
                heads_over(blocks)

    rounded = grad_v[...].astype(BF16)
    back_v[...] += ADAPTER_SCALE * dot(up_v[...], rounded, NN)
    grad_up_v[...] = ADAPTER_SCALE * dot(low_v[...], rounded, NT)


def attention_call(where, frozen, low_q, low_q_t, up_q, up_v, low_v, grad_out, keys, values):
    rows, width = frozen.shape
    kv = keys[0].shape[1] // HD
    rank = up_q.shape[0]
    pieces = len(keys)
    wide = width // kv
    per_head = wide // HD

    def columns(height, wide_of):
        return pl.BlockSpec((height, wide_of), lambda g, w: (0, g))

    def whole(shape):
        return pl.BlockSpec(shape, lambda g, w: (0, 0))

    pairs = rows * rows * per_head * kv * pieces
    return pl.pallas_call(
        functools.partial(attention_body, rows, per_head, pieces),
        grid_spec=pltpu.PrefetchScalarGridSpec(
            num_scalar_prefetch=1,
            grid=(kv,),
            in_specs=[
                columns(rows, wide),
                whole((rows, rank)),
                whole((rank, rows)),
                columns(rank, wide),
                columns(rank, HD),
                whole((rank, pieces * rows)),
                columns(rows, wide),
            ]
            + [columns(rows, HD)] * (2 * pieces),
            out_specs=[
                columns(rows, wide),
                columns(rank, wide),
                whole((rank, rows)),
                whole((rank, pieces * rows)),
                columns(rank, HD),
            ],
            scratch_shapes=[
                pltpu.VMEM((rows, pieces * rows), F32),
                pltpu.VMEM((rows, pieces * rows), BF16),
                pltpu.VMEM((pieces * rows, 2 * HD), BF16),
                pltpu.VMEM((HD, pieces * rows), F32),
            ],
        ),
        out_shape=[
            jax.ShapeDtypeStruct((rows, width), BF16),
            jax.ShapeDtypeStruct((rank, width), F32),
            jax.ShapeDtypeStruct((rank, rows), F32),
            jax.ShapeDtypeStruct((rank, pieces * rows), F32),
            jax.ShapeDtypeStruct((rank, kv * HD), F32),
        ],
        compiler_params=pltpu.CompilerParams(vmem_limit_bytes=50 * 2**20),
        cost_estimate=pl.CostEstimate(
            flops=10 * pairs * HD, bytes_accessed=16 * rows * width, transcendentals=pairs
        ),
    )(where, frozen, low_q, low_q_t, up_q, up_v, low_v, grad_out, *keys, *values)


class Routes:
    def __init__(self, blocks):
        self.seq = lax.axis_size("seq")
        self.tensor = lax.axis_size("tensor")
        self.half = blocks // 2
        self.y = blocks // 4

    def upper(self, s, t):
        offset = self.half if t >= self.tensor // 2 else 0
        return ((s - offset) // self.half) % 2 == 1

    def send(self, block, target):
        route = []
        for s in range(self.seq):
            for t in range(self.tensor):
                to = target(s, t)
                if to is not None:
                    route.append((s * self.tensor + t, to % self.seq * self.tensor + t))
        return lax.ppermute(block, AXES, route)

    def core(self, block):
        return self.send(block, lambda s, t: s ^ 1)

    def across_y(self, block):
        return self.send(block, lambda s, t: s ^ self.y)

    def own_across_y(self, block):
        return self.send(
            block, lambda s, t: None if self.upper(s, t) and s & self.y else s ^ self.y
        )

    def up(self, block):
        return self.send(block, lambda s, t: None if self.upper(s, t) else s + self.half)

    def within_upper(self, block):
        return self.send(block, lambda s, t: s ^ self.y if self.upper(s, t) else None)

    def down(self, block):
        return self.send(block, lambda s, t: s - self.half if self.upper(s, t) else None)


def gather_blocks(routes, own):
    cut = own.shape[0] // 2 // 16 * 16
    from_y = routes.own_across_y(own)
    from_z = routes.up(own)
    first = routes.up(from_y[:cut])
    second = routes.within_upper(from_z[cut:])
    from_both = jnp.concatenate((first, second), axis=0)
    mine = (own, from_y, from_z, from_both)
    found = []
    for block in mine:
        found += [block, routes.core(block)]
    return found


def sum_over_tensor(part):
    size = lax.axis_size("tensor")
    step = 1
    while step < size:
        part = part + lax.ppermute(part, "tensor", [(i, i ^ step) for i in range(size)])
        step *= 2
    return part


def sum_over_seq(part):
    size = lax.axis_size("seq")
    odd = lax.axis_index("seq") % 2 == 1
    half = part.shape[1] // 2
    low, high = part[:, :half], part[:, half:]
    got = lax.ppermute(jnp.where(odd, low, high), "seq", [(i, i ^ 1) for i in range(size)])
    total = jnp.where(odd, high, low).astype(F32) + got.astype(F32)
    step = 2
    while step < size:
        sent = total.astype(BF16)
        got = lax.ppermute(sent, "seq", [(i, i ^ step) for i in range(size)])
        total = sent.astype(F32) + got.astype(F32)
        step *= 2
    total = total.astype(BF16)
    got = lax.ppermute(total, "seq", [(i, i ^ 1) for i in range(size)])
    return jnp.concatenate((jnp.where(odd, got, total), jnp.where(odd, total, got)), axis=1)


def per_device(
    hidden_in,
    frozen_query,
    key_base,
    frozen_value,
    down_query,
    query_upper_factor,
    down_value,
    value_upper_factor,
    grad_output,
):
    rows = hidden_in.shape[0]
    rank = down_query.shape[1]
    width_here = hidden_in.shape[1]
    kv_width = key_base.shape[1]
    blocks = GROUP // rows
    assert blocks == 8 and rows % 32 == 0
    routes = Routes(blocks)
    seq_at, tensor_at = lax.axis_index("seq"), lax.axis_index("tensor")
    offset = jnp.where(tensor_at >= lax.axis_size("tensor") // 2, routes.half, 0)
    place = (seq_at - offset) % blocks
    where = jnp.stack([place % 2, place // routes.y % 2, place // routes.half]).astype(jnp.int32)

    keys = gather_blocks(routes, key_base)
    down = jnp.concatenate((down_query, down_value), axis=1)
    part_t = lax.dot_general(down, hidden_in, (((0,), (1,)), ((), ())), preferred_element_type=F32)
    low_t = sum_over_tensor(part_t).astype(BF16)
    low_q_t, low_v_t = low_t[:rank], low_t[rank:]
    low_q = low_q_t.T
    value_rows = (
        frozen_value.astype(F32)
        + ADAPTER_SCALE
        * lax.dot_general(
            low_v_t, value_upper_factor, (((0,), (0,)), ((), ())), preferred_element_type=F32
        )
    ).astype(BF16)
    low_rows = low_v_t.reshape(rank * rows // kv_width, kv_width)
    extra = -(-low_rows.shape[0] // 16) * 16
    low_rows = jnp.pad(low_rows, ((0, extra - low_rows.shape[0]), (0, 0)))
    packed = gather_blocks(routes, jnp.concatenate((value_rows, low_rows), axis=0))
    low_v = jnp.concatenate(
        [p[rows : rows + rank * rows // kv_width].reshape(rank, rows) for p in packed], axis=1
    )

    attention, grad_up_q, back_q, back_v, grad_up_v = attention_call(
        where,
        frozen_query,
        low_q,
        low_q_t,
        query_upper_factor,
        value_upper_factor,
        low_v,
        grad_output,
        keys,
        packed,
    )

    back_v = back_v.reshape(rank, 4, 2, rows)
    mine = back_v[:, :, 0] + routes.core(back_v[:, :, 1])
    mine = mine[:, 0::2] + routes.across_y(mine[:, 1::2])
    mine = mine[:, 0] + routes.down(mine[:, 1])
    back = sum_over_tensor(jnp.concatenate((back_q, mine), axis=0)).astype(BF16)
    grad_down = dot(back, hidden_in, NN)

    summed = sum_over_seq(
        jnp.concatenate(
            (grad_down[:rank], grad_down[rank:], grad_up_q, grad_up_v), axis=1
        ).astype(BF16)
    ).astype(F32)
    grad_down_query = summed[:, :width_here].T
    grad_down_value = summed[:, width_here : 2 * width_here].T
    grad_up_query = summed[:, 2 * width_here : -kv_width]
    grad_up_value = summed[:, -kv_width:]
    return attention, grad_down_query, grad_up_query, grad_down_value, grad_up_value


def solution(mesh):
    placed = (
        P("seq", "tensor"),
        P("seq", "tensor"),
        P("seq", "tensor"),
        P("seq", "tensor"),
        P("tensor", None),
        P(None, "tensor"),
        P("tensor", None),
        P(None, "tensor"),
        P("seq", "tensor"),
    )
    return jax.shard_map(
        per_device,
        mesh=mesh,
        in_specs=placed,
        out_specs=(
            P("seq", "tensor"),
            P("tensor", None),
            P(None, "tensor"),
            P("tensor", None),
            P(None, "tensor"),
        ),
        check_vma=False,
    )
```

time: 588 us -> 196 us (0.33)
  matrix products: 231 us -> 2.42 us
  blocking collectives: 81.3 us -> 0 us
  Pallas kernels: 0 us -> 38.1 us
  waiting for transfers between devices: 107 us -> 75.2 us
  other arithmetic: 32.9 us -> 1.14 us
  local copies, waits for them, and re-layouts: 47.3 us -> 23.1 us
  starting transfers between devices: 68 us -> 53.9 us
  between operations: 15 us -> 1.14 us
    dot_general x42 -> x3, matrix products: 231 us -> 2.42 us  [the longest x1 1.7 us: per_device(): lax.dot_general(down, hidden_in, (((0,), (1,)), ((), ())), preferred_elem...]
    psum x3 -> x0, blocking collectives: 81.3 us -> none  [the longest x1 61.2 us: per_device(): lax.psum(resident_value_upper.astype(jnp.bfloat16), 'seq')]
    pallas_call x0 -> x1, Pallas kernels: none -> 38.1 us  [attention_call(): pl.pallas_call(functools.partial(attention_body, rows, per_head, pieces),...]
    psum x1 -> x0, waiting for transfers between devices: 30 us -> none  [per_device(): lax.psum(local_down_q.astype(jnp.bfloat16), 'seq').astype(jnp.float32)]
    reduce_sum x1 -> x0, other arithmetic: 24.5 us -> none  [per_device(): jnp.sum(jnp.exp(kept_scores[distance] - row_max), axis=-1, keepdims=True)]
    reshape x32 -> x9, local copies, waits for them, and re-layouts: 22.3 us -> 2.88 us  [the longest x7 2.76 us: per_device(): p[rows:rows + rank * rows // kv_width].reshape(rank, rows)]
    ppermute x14 -> x26, starting transfers between devices: 67.9 us -> 53.9 us  [the longest x19 42.5 us: send(): return lax.ppermute(block, AXES, route)]
    unnamed x105 -> x29, local copies, waits for them, and re-layouts: 13.3 us -> 9.94 us
  transfers between devices with their start and end apart: 15 -> 26, of which waited for: 4 -> 12; matrix products, arithmetic and copies ran while one was open for 11% -> 9% of each run, Pallas kernels for 0% -> 0%
where the time goes in v1:
time: 196 us; the launch traced here: 195 us
  waiting for transfers between devices  75.2 us (38%)
  starting transfers between devices  53.9 us (28%)
  Pallas kernels  38.1 us (19%)
  local copies, waits for them, and re-layouts  23.1 us (12%)
  matrix products  2.42 us (1%)
    ppermute x19, waiting for transfers between devices, send(): return lax.ppermute(block, AXES, route)  48.1 us
    ppermute x19, starting transfers between devices, send(): return lax.ppermute(block, AXES, route)  42.5 us
    pallas_call x1, Pallas kernels, attention_call(): pl.pallas_call(functools.partial(attention_body, rows, per_head, pieces),...  38.1 us
    ppermute x3, waiting for transfers between devices, sum_over_seq(): got = lax.ppermute(sent, 'seq', [(i, i ^ step) for i in range(size)])  20.5 us
    unnamed x29, local copies, waits for them, and re-layouts  9.94 us
    ppermute x2, starting transfers between devices, sum_over_tensor(): lax.ppermute(part, 'tensor', [(i, i ^ step) for i in range(size)])  5.93 us
    ppermute x3, starting transfers between devices, sum_over_seq(): got = lax.ppermute(sent, 'seq', [(i, i ^ step) for i in range(size)])  5.35 us
    slice x7, local copies, waits for them, and re-layouts, per_device(): p[rows:rows + rank * rows // kv_width].reshape(rank, rows)  5.31 us
  transfers between devices with their start and end apart: 26, of which 12 were waited for; matrix products, arithmetic and copies ran while one was open for 9% of the time, Pallas kernels for 0%

profile of v1, /device:TPU:0, one launch (start us, length us, event | category | flops | bytes accessed | tf_op | source)
XLA Modules:
  0.0 195.0 jit_solution(908729773603013836)
XLA Ops:
  0.7 1.6 copy-done
  2.2 1.7 fusion.4
  3.9 3.0 %collective-permute-start = (f32[32,256]{1,0:T(8,128)S(1)}, f32[32,256]{1,0:T(8,128)S(1)}, u32[]{:S(2)}, u32[]{:S(2)}) collective-permute-start(f32[32,256]{1,0:T(8,128)S(1)} %fusion.4), channel_id=1, source_target_pairs={{0,1},{1,0},{2,3},{3,2},{4,5},{5,4},{6,7},{7,6},{8,9},{9,8},{10,11... | collective-permute-start | bytes 98312 | tf_op jit(solution)/shard_map/ppermute | solution.py:224
  6.9 1.9 collective-permute-done
  9.3 4.0 %collective-permute-start.10 = (bf16[256,512]{1,0:T(8,128)(2,1)}, bf16[256,512]{1,0:T(8,128)(2,1)S(1)}, u32[]{:S(2)}, u32[]{:S(2)}) collective-permute-start(bf16[256,512]{1,0:T(8,128)(2,1)} %refs_7_.1), channel_id=1, source_target_pairs={{0,4},{1,5},{2,6},{3,7},{4,0},{6,2},{8,12},{9,13},{10,14},{11,15},... | collective-permute-start | bytes 786440 | tf_op jit(solution)/shard_map/ppermute | solution.py:183
  13.2 3.5 %collective-permute-start.12 = (bf16[256,512]{1,0:T(8,128)(2,1)}, bf16[256,512]{1,0:T(8,128)(2,1)S(1)}, u32[]{:S(2)}, u32[]{:S(2)}) collective-permute-start(bf16[256,512]{1,0:T(8,128)(2,1)} %refs_7_.1), channel_id=1, source_target_pairs={{0,8},{2,10},{4,12},{6,14},{9,17},{11,19},{13,21},{15,23},{16,24},... | collective-permute-start | bytes 786440 | tf_op jit(solution)/shard_map/ppermute | solution.py:183
  16.7 1.9 collective-permute-start.2
  18.7 2.0 %collective-permute-start.4 = (bf16[272,512]{1,0:T(8,128)(2,1)S(1)}, bf16[272,512]{1,0:T(8,128)(2,1)}, u32[]{:S(2)}, u32[]{:S(2)}) collective-permute-start(bf16[272,512]{1,0:T(8,128)(2,1)S(1)} %fusion.3.refs_15_), channel_id=1, source_target_pairs={{0,8},{2,10},{4,12},{6,14},{9,17},{11,19},{13,21},{15,23},{16,24},... | collective-permute-start | bytes 835592 | tf_op jit(solution)/shard_map/ppermute | solution.py:183
  21.1 2.6 %collective-permute-done.12.refs_11_ = bf16[256,512]{1,0:T(8,128)(2,1)S(1)} collective-permute-done((bf16[256,512]{1,0:T(8,128)(2,1)}, bf16[256,512]{1,0:T(8,128)(2,1)S(1)}, u32[]{:S(2)}, u32[]{:S(2)}) %collective-permute-start.12) | collective-permute-done | bytes 262176 | tf_op jit(solution)/shard_map/ppermute | solution.py:183
  23.7 4.9 %collective-permute-start.14 = (bf16[128,512]{1,0:T(8,128)(2,1)S(1)}, bf16[128,512]{1,0:T(8,128)(2,1)}, u32[]{:S(2)}, u32[]{:S(2)}) collective-permute-start(bf16[128,512]{1,0:T(8,128)(2,1)S(1)} %slice.124), channel_id=1, source_target_pairs={{0,8},{2,10},{4,12},{6,14},{9,17},{11,19},{13,21},{15,23},{16,24},... | collective-permute-start | bytes 393224 | tf_op jit(solution)/shard_map/ppermute | solution.py:183
  33.8 4.5 %collective-permute-start.7 = (bf16[128,512]{1,0:T(8,128)(2,1)S(1)}, bf16[128,512]{1,0:T(8,128)(2,1)S(1)}, u32[]{:S(2)}, u32[]{:S(2)}) collective-permute-start(bf16[128,512]{1,0:T(8,128)(2,1)S(1)} %slice.122), channel_id=1, source_target_pairs={{0,8},{2,10},{4,12},{6,14},{9,17},{11,19},{13,21},{15,23},{16,24},... | collective-permute-start | bytes 393224 | tf_op jit(solution)/shard_map/ppermute | solution.py:183
  57.9 38.1 %shard_map.128 = (bf16[256,4096]{1,0:T(8,128)(2,1)}, f32[16,4096]{1,0:T(8,128)S(1)}, f32[16,256]{1,0:T(8,128)S(1)}, f32[16,2048]{1,0:T(8,128)S(1)}, f32[16,512]{1,0:T(8,128)S(1)}) custom-call(s32[3]{0:T(128)S(1)} %pad_add_fusion.where, bf16[256,4096]{1,0:T(8,128)(2,1)} %refs_0_.1, bf16[256,16]{1,0:T(8,128)(2,1)S(1)} %copy.14.refs_1_, ...), custom_call_target="tpu_custom_call" | custom-call | flops 21474836480 | bytes 16777216 | tf_op jit(solution)/shard_map/pallas_call | solution.py:122
  97.7 17.0 %collective-permute-start.18 = (f32[16,2,256]{2,0,1:T(8,128)S(1)}, f32[16,2,256]{2,0,1:T(8,128)S(1)}, u32[]{:S(2)}, u32[]{:S(2)}) collective-permute-start(f32[16,2,256]{2,0,1:T(8,128)S(1)} %slice.102), channel_id=1, source_target_pairs={{0,4},{1,5},{2,6},{3,7},{4,0},{5,1},{6,2},{7,3},{8,12},{9,13},{10,... | collective-permute-start | bytes 98312 | tf_op jit(solution)/shard_map/ppermute | solution.py:183
  114.6 1.9 collective-permute-done.18
  117.8 41.1 %collective-permute-done.19 = f32[16,256]{1,0:T(8,128)S(1)} collective-permute-done((f32[16,256]{1,0:T(8,128)S(1)}, f32[16,256]{1,0:T(8,128)S(1)}, u32[]{:S(2)}, u32[]{:S(2)}) %collective-permute-start.19) | collective-permute-done | bytes 16416 | tf_op jit(solution)/shard_map/ppermute | solution.py:183
  159.0 2.9 %collective-permute-start.20 = (f32[32,256]{1,0:T(8,128)S(1)}, f32[32,256]{1,0:T(8,128)S(1)}, u32[]{:S(2)}, u32[]{:S(2)}) collective-permute-start(f32[32,256]{1,0:T(8,128)S(1)} %pad_maximum_fusion.3), channel_id=1, source_target_pairs={{0,1},{1,0},{2,3},{3,2},{4,5},{5,4},{6,7},{7,6},{8,9},{9,8},{10,11... | collective-permute-start | bytes 98312 | tf_op jit(solution)/shard_map/ppermute | solution.py:224
  161.9 1.9 collective-permute-done.20
  164.4 1.4 collective-permute-done.21
  165.9 2.1 %collective-permute-start.22 = (bf16[16,6400]{1,0:T(8,128)(2,1)S(1)}, bf16[16,6400]{1,0:T(8,128)(2,1)S(1)}, u32[]{:S(2)}, u32[]{:S(2)}) collective-permute-start(bf16[16,6400]{1,0:T(8,128)(2,1)S(1)} %add_convert_fusion.3), channel_id=1, source_target_pairs={{0,4},{2,6},{4,0},{6,2},{8,12},{10,14},{12,8},{14,10},{16,20},{18,... | collective-permute-start | bytes 614408 | tf_op jit(solution)/shard_map/ppermute | solution.py:239
  168.0 5.4 %collective-permute-done.22 = bf16[16,6400]{1,0:T(8,128)(2,1)S(1)} collective-permute-done((bf16[16,6400]{1,0:T(8,128)(2,1)S(1)}, bf16[16,6400]{1,0:T(8,128)(2,1)S(1)}, u32[]{:S(2)}, u32[]{:S(2)}) %collective-permute-start.22) | collective-permute-done | bytes 204832 | tf_op jit(solution)/shard_map/ppermute | solution.py:239
  173.7 6.4 %collective-permute-done.23 = bf16[16,6400]{1,0:T(8,128)(2,1)S(1)} collective-permute-done((bf16[16,6400]{1,0:T(8,128)(2,1)S(1)}, bf16[16,6400]{1,0:T(8,128)(2,1)S(1)}, u32[]{:S(2)}, u32[]{:S(2)}) %collective-permute-start.23) | collective-permute-done | bytes 204832 | tf_op jit(solution)/shard_map/ppermute | solution.py:239
  180.2 3.0 %collective-permute-start.24 = (bf16[16,6400]{1,0:T(8,128)(2,1)S(1)}, bf16[16,6400]{1,0:T(8,128)(2,1)S(1)}, u32[]{:S(2)}, u32[]{:S(2)}) collective-permute-start(bf16[16,6400]{1,0:T(8,128)(2,1)S(1)} %add_convert_fusion.1), channel_id=1, source_target_pairs={{0,16},{2,18},{4,20},{6,22},{8,24},{10,26},{12,28},{14,30},{16,0},... | collective-permute-start | bytes 614408 | tf_op jit(solution)/shard_map/ppermute | solution.py:239
  183.2 8.7 %collective-permute-done.24 = bf16[16,6400]{1,0:T(8,128)(2,1)S(1)} collective-permute-done((bf16[16,6400]{1,0:T(8,128)(2,1)S(1)}, bf16[16,6400]{1,0:T(8,128)(2,1)S(1)}, u32[]{:S(2)}, u32[]{:S(2)}) %collective-permute-start.24) | collective-permute-done | bytes 204832 | tf_op jit(solution)/shard_map/ppermute | solution.py:239
  192.0 1.4 collective-permute-done.25
  (108 shorter events, 30.9 us)
Async XLA Ops:
  3.9 4.9 %collective-permute-start = (f32[32,256]{1,0:T(8,128)S(1)}, f32[32,256]{1,0:T(8,128)S(1)}, u32[]{:S(2)}, u32[]{:S(2)}) collective-permute-start(f32[32,256]{1,0:T(8,128)S(1)} %fusion.4), channel_id=1, source_target_pairs={{0,1},{1,0},{2,3},{3,2},{4,5},{5,4},{6,7},{7,6},{8,9},{9,8},{10,11... | collective-permute-start | bytes 98312 | tf_op jit(solution)/shard_map/ppermute | solution.py:224
  9.2 20.1 %collective-permute-start.1 = (bf16[272,512]{1,0:T(8,128)(2,1)S(1)}, bf16[272,512]{1,0:T(8,128)(2,1)}, u32[]{:S(2)}, u32[]{:S(2)}) collective-permute-start(bf16[272,512]{1,0:T(8,128)(2,1)S(1)} %fusion.3.refs_15_), channel_id=1, source_target_pairs={{0,2},{1,3},{2,0},{3,1},{4,6},{5,7},{6,4},{7,5},{8,10},{9,11},{10,... | collective-permute-start | bytes 835592 | tf_op jit(solution)/shard_map/ppermute | solution.py:183
  9.3 11.7 %collective-permute-start.10 = (bf16[256,512]{1,0:T(8,128)(2,1)}, bf16[256,512]{1,0:T(8,128)(2,1)S(1)}, u32[]{:S(2)}, u32[]{:S(2)}) collective-permute-start(bf16[256,512]{1,0:T(8,128)(2,1)} %refs_7_.1), channel_id=1, source_target_pairs={{0,4},{1,5},{2,6},{3,7},{4,0},{6,2},{8,12},{9,13},{10,14},{11,15},... | collective-permute-start | bytes 786440 | tf_op jit(solution)/shard_map/ppermute | solution.py:183
  13.2 10.5 %collective-permute-start.12 = (bf16[256,512]{1,0:T(8,128)(2,1)}, bf16[256,512]{1,0:T(8,128)(2,1)S(1)}, u32[]{:S(2)}, u32[]{:S(2)}) collective-permute-start(bf16[256,512]{1,0:T(8,128)(2,1)} %refs_7_.1), channel_id=1, source_target_pairs={{0,8},{2,10},{4,12},{6,14},{9,17},{11,19},{13,21},{15,23},{16,24},... | collective-permute-start | bytes 786440 | tf_op jit(solution)/shard_map/ppermute | solution.py:183
  16.7 14.6 %collective-permute-start.2 = (bf16[272,512]{1,0:T(8,128)(2,1)S(1)}, bf16[272,512]{1,0:T(8,128)(2,1)S(1)}, u32[]{:S(2)}, u32[]{:S(2)}) collective-permute-start(bf16[272,512]{1,0:T(8,128)(2,1)S(1)} %fusion.3.refs_15_), channel_id=1, source_target_pairs={{0,4},{1,5},{2,6},{3,7},{4,0},{6,2},{8,12},{9,13},{10,14},{11,15},... | collective-permute-start | bytes 835592 | tf_op jit(solution)/shard_map/ppermute | solution.py:183
  18.7 12.7 %collective-permute-start.4 = (bf16[272,512]{1,0:T(8,128)(2,1)S(1)}, bf16[272,512]{1,0:T(8,128)(2,1)}, u32[]{:S(2)}, u32[]{:S(2)}) collective-permute-start(bf16[272,512]{1,0:T(8,128)(2,1)S(1)} %fusion.3.refs_15_), channel_id=1, source_target_pairs={{0,8},{2,10},{4,12},{6,14},{9,17},{11,19},{13,21},{15,23},{16,24},... | collective-permute-start | bytes 835592 | tf_op jit(solution)/shard_map/ppermute | solution.py:183
  21.0 33.3 %collective-permute-start.9 = (bf16[256,512]{1,0:T(8,128)(2,1)}, bf16[256,512]{1,0:T(8,128)(2,1)}, u32[]{:S(2)}, u32[]{:S(2)}) collective-permute-start(bf16[256,512]{1,0:T(8,128)(2,1)} %refs_7_.1), channel_id=1, source_target_pairs={{0,2},{1,3},{2,0},{3,1},{4,6},{5,7},{6,4},{7,5},{8,10},{9,11},{10,... | collective-permute-start | bytes 786440 | tf_op jit(solution)/shard_map/ppermute | solution.py:183
  23.7 10.1 %collective-permute-start.14 = (bf16[128,512]{1,0:T(8,128)(2,1)S(1)}, bf16[128,512]{1,0:T(8,128)(2,1)}, u32[]{:S(2)}, u32[]{:S(2)}) collective-permute-start(bf16[128,512]{1,0:T(8,128)(2,1)S(1)} %slice.124), channel_id=1, source_target_pairs={{0,8},{2,10},{4,12},{6,14},{9,17},{11,19},{13,21},{15,23},{16,24},... | collective-permute-start | bytes 393224 | tf_op jit(solution)/shard_map/ppermute | solution.py:183
  29.3 10.0 %collective-permute-start.15 = (bf16[128,512]{1,0:T(8,128)(2,1)}, bf16[128,512]{1,0:T(8,128)(2,1)}, u32[]{:S(2)}, u32[]{:S(2)}) collective-permute-start(bf16[128,512]{1,0:T(8,128)(2,1)} %slice.125), channel_id=1, source_target_pairs={{1,5},{3,7},{5,1},{7,3},{8,12},{10,14},{12,8},{14,10},{17,21},{19,... | collective-permute-start | bytes 393224 | tf_op jit(solution)/shard_map/ppermute | solution.py:183
  31.3 22.9 %collective-permute-start.11 = (bf16[256,512]{1,0:T(8,128)(2,1)S(1)}, bf16[256,512]{1,0:T(8,128)(2,1)}, u32[]{:S(2)}, u32[]{:S(2)}) collective-permute-start(bf16[256,512]{1,0:T(8,128)(2,1)S(1)} %collective-permute-done.10.refs_9_), channel_id=1, source_target_pairs={{0,2},{1,3},{2,0},{3,1},{4,6},{5,7},{6,4},{7,5},{8,10},{9,11},{10,... | collective-permute-start | bytes 786440 | tf_op jit(solution)/shard_map/ppermute | solution.py:183
  33.1 9.0 %collective-permute-start.6 = (bf16[144,512]{1,0:T(8,128)(2,1)S(1)}, bf16[144,512]{1,0:T(8,128)(2,1)S(1)}, u32[]{:S(2)}, u32[]{:S(2)}) collective-permute-start(bf16[144,512]{1,0:T(8,128)(2,1)S(1)} %slice.120), channel_id=1, source_target_pairs={{1,5},{3,7},{5,1},{7,3},{8,12},{10,14},{12,8},{14,10},{17,21},{19,... | collective-permute-start | bytes 442376 | tf_op jit(solution)/shard_map/ppermute | solution.py:183
  33.8 7.6 %collective-permute-start.7 = (bf16[128,512]{1,0:T(8,128)(2,1)S(1)}, bf16[128,512]{1,0:T(8,128)(2,1)S(1)}, u32[]{:S(2)}, u32[]{:S(2)}) collective-permute-start(bf16[128,512]{1,0:T(8,128)(2,1)S(1)} %slice.122), channel_id=1, source_target_pairs={{0,8},{2,10},{4,12},{6,14},{9,17},{11,19},{13,21},{15,23},{16,24},... | collective-permute-start | bytes 393224 | tf_op jit(solution)/shard_map/ppermute | solution.py:183
  39.3 5.3 %collective-permute-start.3 = (bf16[272,512]{1,0:T(8,128)(2,1)S(1)}, bf16[272,512]{1,0:T(8,128)(2,1)}, u32[]{:S(2)}, u32[]{:S(2)}) collective-permute-start(bf16[272,512]{1,0:T(8,128)(2,1)S(1)} %collective-permute-done.2.refs_17_), channel_id=1, source_target_pairs={{0,2},{1,3},{2,0},{3,1},{4,6},{5,7},{6,4},{7,5},{8,10},{9,11},{10,... | collective-permute-start | bytes 835592 | tf_op jit(solution)/shard_map/ppermute | solution.py:183
  41.5 12.8 %collective-permute-start.13 = (bf16[256,512]{1,0:T(8,128)(2,1)S(1)}, bf16[256,512]{1,0:T(8,128)(2,1)}, u32[]{:S(2)}, u32[]{:S(2)}) collective-permute-start(bf16[256,512]{1,0:T(8,128)(2,1)S(1)} %collective-permute-done.12.refs_11_), channel_id=1, source_target_pairs={{0,2},{1,3},{2,0},{3,1},{4,6},{5,7},{6,4},{7,5},{8,10},{9,11},{10,... | collective-permute-start | bytes 786440 | tf_op jit(solution)/shard_map/ppermute | solution.py:183
  42.1 7.1 %collective-permute-start.5 = (bf16[272,512]{1,0:T(8,128)(2,1)}, bf16[272,512]{1,0:T(8,128)(2,1)}, u32[]{:S(2)}, u32[]{:S(2)}) collective-permute-start(bf16[272,512]{1,0:T(8,128)(2,1)} %collective-permute-done.4.refs_19_), channel_id=1, source_target_pairs={{0,2},{1,3},{2,0},{3,1},{4,6},{5,7},{6,4},{7,5},{8,10},{9,11},{10,... | collective-permute-start | bytes 835592 | tf_op jit(solution)/shard_map/ppermute | solution.py:183
  44.6 8.3 %collective-permute-start.8 = (bf16[272,512]{1,0:T(8,128)(2,1)}, bf16[272,512]{1,0:T(8,128)(2,1)}, u32[]{:S(2)}, u32[]{:S(2)}) collective-permute-start(bf16[272,512]{1,0:T(8,128)(2,1)} %constant_dynamic-update-slice_fusion.refs_21_), channel_id=1, source_target_pairs={{0,2},{1,3},{2,0},{3,1},{4,6},{5,7},{6,4},{7,5},{8,10},{9,11},{10,... | collective-permute-start | bytes 835592 | tf_op jit(solution)/shard_map/ppermute | solution.py:183
  49.2 5.0 %collective-permute-start.16 = (bf16[256,512]{1,0:T(8,128)(2,1)S(1)}, bf16[256,512]{1,0:T(8,128)(2,1)}, u32[]{:S(2)}, u32[]{:S(2)}) collective-permute-start(bf16[256,512]{1,0:T(8,128)(2,1)S(1)} %constant_dynamic-update-slice_fusion.10.refs_13_), channel_id=1, source_target_pairs={{0,2},{1,3},{2,0},{3,1},{4,6},{5,7},{6,4},{7,5},{8,10},{9,11},{10,... | collective-permute-start | bytes 786440 | tf_op jit(solution)/shard_map/ppermute | solution.py:183
  97.7 18.8 %collective-permute-start.18 = (f32[16,2,256]{2,0,1:T(8,128)S(1)}, f32[16,2,256]{2,0,1:T(8,128)S(1)}, u32[]{:S(2)}, u32[]{:S(2)}) collective-permute-start(f32[16,2,256]{2,0,1:T(8,128)S(1)} %slice.102), channel_id=1, source_target_pairs={{0,4},{1,5},{2,6},{3,7},{4,0},{5,1},{6,2},{7,3},{8,12},{9,13},{10,... | collective-permute-start | bytes 98312 | tf_op jit(solution)/shard_map/ppermute | solution.py:183
  116.5 42.4 %collective-permute-start.19 = (f32[16,256]{1,0:T(8,128)S(1)}, f32[16,256]{1,0:T(8,128)S(1)}, u32[]{:S(2)}, u32[]{:S(2)}) collective-permute-start(f32[16,256]{1,0:T(8,128)S(1)} %slice_bitcast_fusion.2), channel_id=1, source_target_pairs={{1,25},{3,27},{5,29},{7,31},{8,0},{10,2},{12,4},{14,6},{17,9},{19,... | collective-permute-start | bytes 49160 | tf_op jit(solution)/shard_map/ppermute | solution.py:183
  159.0 4.8 %collective-permute-start.20 = (f32[32,256]{1,0:T(8,128)S(1)}, f32[32,256]{1,0:T(8,128)S(1)}, u32[]{:S(2)}, u32[]{:S(2)}) collective-permute-start(f32[32,256]{1,0:T(8,128)S(1)} %pad_maximum_fusion.3), channel_id=1, source_target_pairs={{0,1},{1,0},{2,3},{3,2},{4,5},{5,4},{6,7},{7,6},{8,9},{9,8},{10,11... | collective-permute-start | bytes 98312 | tf_op jit(solution)/shard_map/ppermute | solution.py:224
  165.9 7.5 %collective-permute-start.22 = (bf16[16,6400]{1,0:T(8,128)(2,1)S(1)}, bf16[16,6400]{1,0:T(8,128)(2,1)S(1)}, u32[]{:S(2)}, u32[]{:S(2)}) collective-permute-start(bf16[16,6400]{1,0:T(8,128)(2,1)S(1)} %add_convert_fusion.3), channel_id=1, source_target_pairs={{0,4},{2,6},{4,0},{6,2},{8,12},{10,14},{12,8},{14,10},{16,20},{18,... | collective-permute-start | bytes 614408 | tf_op jit(solution)/shard_map/ppermute | solution.py:239
  173.5 6.7 %collective-permute-start.23 = (bf16[16,6400]{1,0:T(8,128)(2,1)S(1)}, bf16[16,6400]{1,0:T(8,128)(2,1)S(1)}, u32[]{:S(2)}, u32[]{:S(2)}) collective-permute-start(bf16[16,6400]{1,0:T(8,128)(2,1)S(1)} %add_convert_fusion.2), channel_id=1, source_target_pairs={{0,8},{2,10},{4,12},{6,14},{8,0},{10,2},{12,4},{14,6},{16,24},{18,... | collective-permute-start | bytes 614408 | tf_op jit(solution)/shard_map/ppermute | solution.py:239
  180.2 11.7 %collective-permute-start.24 = (bf16[16,6400]{1,0:T(8,128)(2,1)S(1)}, bf16[16,6400]{1,0:T(8,128)(2,1)S(1)}, u32[]{:S(2)}, u32[]{:S(2)}) collective-permute-start(bf16[16,6400]{1,0:T(8,128)(2,1)S(1)} %add_convert_fusion.1), channel_id=1, source_target_pairs={{0,16},{2,18},{4,20},{6,22},{8,24},{10,26},{12,28},{14,30},{16,0},... | collective-permute-start | bytes 614408 | tf_op jit(solution)/shard_map/ppermute | solution.py:239
  191.9 1.5 collective-permute-start.25
  (12 other events, 71.4 us)

commit v2 on v1

v2 whole, which is shorter than its diff:
```python
import functools

import jax
import jax.numpy as jnp
from jax import lax
from jax.experimental import pallas as pl
from jax.experimental.pallas import tpu as pltpu
from jax.sharding import PartitionSpec as P

HD = 128
GROUP = 2048
ADAPTER_SCALE = 0.5
LOG2E = 1.4426950408889634
MASKED = -1e30

F32 = jnp.float32
BF16 = jnp.bfloat16
NN = (((1,), (0,)), ((), ()))
NT = (((1,), (1,)), ((), ()))

AXES = ("seq", "tensor")


def dot(a, b, dims):
    return lax.dot_general(a, b, dims, preferred_element_type=F32)


ONES = 16


def attention_body(rows, per_head, kv, stacked, where, *refs):
    frozen, low_q, low_q_t, up_q, up_v, low_v, grad_out = refs[:7]
    given = refs[7:17]
    out, grad_up_q, back_q, back_v, grad_up_v = refs[17:22]
    scores, probs, grad_s, keys, keys_t, values, values_t, grad_v = refs[22:]
    scale = float(HD) ** -0.5
    to_log2 = scale * LOG2E
    core, y_bit, z_bit = where[0], where[1], where[2]
    half = rows // 2
    parts = [(given[j], 0, rows) for j in range(6)]
    parts = [[p] for p in parts]
    parts += [[(given[6], 0, half), (given[7], half, half)], [(given[8], 0, half), (given[9], half, half)]]
    width_kv = kv * HD
    columns = stacked * rows
    steps = kv * per_head // stacked
    steps_per_kv = per_head // stacked
    back_q[...] = jnp.zeros_like(back_q)
    back_v[...] = jnp.zeros_like(back_v)
    key_at = lax.broadcasted_iota(jnp.int32, (rows, columns), 0)
    query_at = lax.broadcasted_iota(jnp.int32, (rows, columns), 1) % rows

    def prepare(blocks):
        for slot, j in enumerate(blocks):
            for ref, first, count in parts[j]:
                at = slice(slot * rows + first, slot * rows + first + count)
                low_at = slice(j * rows + first, j * rows + first + count)
                block = ref[:, :width_kv]
                keys[at, :] = block
                keys_t[:, at] = block.T
                added = lax.dot_general(
                    low_v[:, low_at], up_v[...], (((0,), (0,)), ((), ())), preferred_element_type=F32
                )
                block = (ref[:, width_kv:].astype(F32) + ADAPTER_SCALE * added).astype(BF16)
                values[at, :] = block
                block_t = block.T
                for g in range(kv):
                    values_t[g, :HD, at] = block_t[g * HD : (g + 1) * HD]
                    values_t[g, HD:, at] = jnp.ones((ONES, count), BF16)
                grad_v[at, :] = jnp.zeros((count, width_kv), F32)

    def finish(blocks):
        for g in range(kv):
            cols = slice(g * HD, (g + 1) * HD)
            total = None
            for slot, j in enumerate(blocks):
                rounded = grad_v[slot * rows : (slot + 1) * rows, cols].astype(BF16)
                at = slice(j * rows, (j + 1) * rows)
                back_v[:, at] += ADAPTER_SCALE * dot(up_v[:, cols], rounded, NT)
                term = dot(low_v[:, at], rounded, NN)
                total = term if total is None else total + term
            grad_up_v[:, cols] = ADAPTER_SCALE * total

    def attend(length, pipelined):
        def wide(i):
            return pl.ds(pl.multiple_of(i * (stacked * HD), stacked * HD), stacked * HD)

        def narrow(i, a):
            return pl.ds(pl.multiple_of(i * (stacked * HD) + a * HD, HD), HD)

        def kv_cols(i):
            return pl.ds(pl.multiple_of((i // steps_per_kv) * HD, HD), HD)

        def score(i, slot):
            query = frozen[:, wide(i)].astype(F32) + ADAPTER_SCALE * dot(low_q[...], up_q[:, wide(i)], NN)
            query = query.astype(BF16)
            query = jnp.concatenate([query[:, a * HD : (a + 1) * HD] for a in range(stacked)], axis=0)
            s = dot(keys[:length, kv_cols(i)], query, NT)
            own = jnp.where(key_at <= query_at, s[:rows], MASKED)
            sibling = jnp.where(core > 0, s[rows : 2 * rows], MASKED)
            scores[slot, :rows, :] = own
            scores[slot, rows : 2 * rows, :] = sibling
            top = jnp.max(jnp.maximum(own, sibling), axis=0, keepdims=True)
            if length > 2 * rows:
                rest = s[2 * rows :]
                scores[slot, 2 * rows : length, :] = rest
                top = jnp.maximum(top, jnp.max(rest, axis=0, keepdims=True))
            return top * to_log2

        def follow(i, slot, top):
            probs[:length, :] = jnp.exp2(scores[slot, :length, :] * to_log2 - top).astype(BF16)
            attended = dot(values_t[i // steps_per_kv, :, :length], probs[:length, :], NN)
            inverse = 1.0 / attended[HD : HD + 1, :]
            attended = (attended[:HD] * inverse).astype(BF16)
            for a in range(stacked):
                out[:, narrow(i, a)] = attended[:, a * rows : (a + 1) * rows].T
            upstream = jnp.concatenate([grad_out[:, narrow(i, a)].T for a in range(stacked)], axis=1)
            upstream_f = upstream.astype(F32)
            delta = jnp.sum(upstream_f * attended.astype(F32), axis=0, keepdims=True)
            normed = (upstream_f * inverse).astype(BF16)
            grad_probs = dot(values[:length, kv_cols(i)], upstream, NN)
            grad_s[:length, :] = (probs[:length, :].astype(F32) * (grad_probs - delta)).astype(BF16)
            grad_v[:length, kv_cols(i)] += dot(probs[:length, :], normed, NT)
            grad_query = dot(keys_t[kv_cols(i), :length], grad_s[:length, :], NN)
            grad_query = (grad_query * (inverse * scale)).astype(BF16)
            back = None
            for a in range(stacked):
                one = grad_query[:, a * rows : (a + 1) * rows]
                grad_up_q[:, narrow(i, a)] = ADAPTER_SCALE * dot(low_q_t[...], one, NT)
                term = dot(up_q[:, narrow(i, a)], one, NN)
                back = term if back is None else back + term
            back_q[...] += ADAPTER_SCALE * back

        if pipelined:

            def two_steps(t, top):
                for u in range(2):
                    i = 2 * t + u
                    later = score(jnp.minimum(i + 1, steps - 1), 1 - u)
                    follow(i, u, top)
                    top = later
                return top

            lax.fori_loop(0, steps // 2, two_steps, score(0, 0))
        else:

            def one_step(i, carry):
                follow(i, 0, score(i, 0))
                return carry

            lax.fori_loop(0, steps, one_step, 0)

    for y in (0, 1):
        for z in (0, 1):

            @pl.when((y_bit == y) & (z_bit == z))
            def _():
                blocks = [0, 1] + [2, 3] * y + [4, 5, 6, 7] * z
                prepare(blocks)
                attend(len(blocks) * rows, len(blocks) == 8 and steps % 2 == 0)
                finish(blocks)


def attention_call(where, frozen, low_q, low_q_t, up_q, up_v, low_v, grad_out, given):
    rows, width = frozen.shape
    kv = up_v.shape[1] // HD
    rank = up_q.shape[0]
    per_head = width // HD // kv
    reach = low_v.shape[1]
    stacked = 2
    vmem = pl.BlockSpec(memory_space=pltpu.VMEM)
    pairs = rows * reach * per_head * kv
    return pl.pallas_call(
        functools.partial(attention_body, rows, per_head, kv, stacked),
        in_specs=[pl.BlockSpec(memory_space=pltpu.SMEM)] + [vmem] * (7 + len(given)),
        out_specs=[vmem] * 5,
        scratch_shapes=[
            pltpu.VMEM((2, reach, stacked * rows), F32),
            pltpu.VMEM((reach, stacked * rows), BF16),
            pltpu.VMEM((reach, stacked * rows), BF16),
            pltpu.VMEM((reach, kv * HD), BF16),
            pltpu.VMEM((kv * HD, reach), BF16),
            pltpu.VMEM((reach, kv * HD), BF16),
            pltpu.VMEM((kv, HD + ONES, reach), BF16),
            pltpu.VMEM((reach, kv * HD), F32),
        ],
        out_shape=[
            jax.ShapeDtypeStruct((rows, width), BF16),
            jax.ShapeDtypeStruct((rank, width), F32),
            jax.ShapeDtypeStruct((rank, rows), F32),
            jax.ShapeDtypeStruct((rank, reach), F32),
            jax.ShapeDtypeStruct((rank, kv * HD), F32),
        ],
        compiler_params=pltpu.CompilerParams(vmem_limit_bytes=56 * 2**20),
        cost_estimate=pl.CostEstimate(
            flops=10 * pairs * HD, bytes_accessed=16 * rows * width, transcendentals=pairs
        ),
    )(where, frozen, low_q, low_q_t, up_q, up_v, low_v, grad_out, *given)


class Routes:
    def __init__(self, blocks):
        self.seq = lax.axis_size("seq")
        self.tensor = lax.axis_size("tensor")
        self.half = blocks // 2
        self.y = blocks // 4

    def upper(self, s, t):
        offset = self.half if t >= self.tensor // 2 else 0
        return ((s - offset) // self.half) % 2 == 1

    def send(self, block, target):
        route = []
        for s in range(self.seq):
            for t in range(self.tensor):
                to = target(s, t)
                if to is not None:
                    route.append((s * self.tensor + t, to % self.seq * self.tensor + t))
        return lax.ppermute(block, AXES, route)

    def core(self, block):
        return self.send(block, lambda s, t: s ^ 1)

    def across_y(self, block):
        return self.send(block, lambda s, t: s ^ self.y)

    def own_across_y(self, block):
        return self.send(
            block, lambda s, t: None if self.upper(s, t) and s & self.y else s ^ self.y
        )

    def up(self, block):
        return self.send(block, lambda s, t: None if self.upper(s, t) else s + self.half)

    def within_upper(self, block):
        return self.send(block, lambda s, t: s ^ self.y if self.upper(s, t) else None)

    def down(self, block):
        return self.send(block, lambda s, t: s - self.half if self.upper(s, t) else None)


def gather_blocks(routes, own):
    cut = own.shape[0] // 2
    from_y = routes.own_across_y(own)
    from_z = routes.up(own)
    first = routes.up(from_y[:cut])
    second = routes.within_upper(from_z[cut:])
    found = []
    for block in (own, from_y, from_z):
        found += [block, routes.core(block)]
    return found + [first, second, routes.core(first), routes.core(second)]


def gather_low(routes, own):
    near = jnp.concatenate((own, routes.across_y(own)), axis=1)
    mine = jnp.concatenate((near, routes.up(near)), axis=1)
    other = routes.core(mine)
    rank = own.shape[0]
    both = jnp.stack((mine.reshape(rank, 4, -1), other.reshape(rank, 4, -1)), axis=2)
    return both.reshape(rank, -1)


def sum_over_tensor(part):
    size = lax.axis_size("tensor")
    step = 1
    while step < size:
        part = part + lax.ppermute(part, "tensor", [(i, i ^ step) for i in range(size)])
        step *= 2
    return part


def sum_over_seq(part):
    size = lax.axis_size("seq")
    odd = lax.axis_index("seq") % 2 == 1
    half = part.shape[1] // 2
    low, high = part[:, :half], part[:, half:]
    got = lax.ppermute(jnp.where(odd, low, high), "seq", [(i, i ^ 1) for i in range(size)])
    total = jnp.where(odd, high, low).astype(F32) + got.astype(F32)
    step = 2
    while step < size:
        sent = total.astype(BF16)
        got = lax.ppermute(sent, "seq", [(i, i ^ step) for i in range(size)])
        total = sent.astype(F32) + got.astype(F32)
        step *= 2
    total = total.astype(BF16)
    got = lax.ppermute(total, "seq", [(i, i ^ 1) for i in range(size)])
    return jnp.concatenate((jnp.where(odd, got, total), jnp.where(odd, total, got)), axis=1)


def per_device(
    hidden_in,
    frozen_query,
    key_base,
    frozen_value,
    down_query,
    query_upper_factor,
    down_value,
    value_upper_factor,
    grad_output,
):
    rows = hidden_in.shape[0]
    rank = down_query.shape[1]
    width_here = hidden_in.shape[1]
    kv_width = key_base.shape[1]
    blocks = GROUP // rows
    assert blocks == 8 and rows % 32 == 0
    routes = Routes(blocks)
    seq_at, tensor_at = lax.axis_index("seq"), lax.axis_index("tensor")
    offset = jnp.where(tensor_at >= lax.axis_size("tensor") // 2, routes.half, 0)
    place = (seq_at - offset) % blocks
    where = jnp.stack([place % 2, place // routes.y % 2, place // routes.half]).astype(jnp.int32)

    given = gather_blocks(routes, jnp.concatenate((key_base, frozen_value), axis=1))
    down = jnp.concatenate((down_query, down_value), axis=1)
    part_t = lax.dot_general(down, hidden_in, (((0,), (1,)), ((), ())), preferred_element_type=F32)
    low_t = sum_over_tensor(part_t).astype(BF16)
    low_q_t = low_t[:rank]
    low_v = gather_low(routes, low_t[rank:])

    attention, grad_up_q, back_q, back_v, grad_up_v = attention_call(
        where,
        frozen_query,
        low_q_t.T,
        low_q_t,
        query_upper_factor,
        value_upper_factor,
        low_v,
        grad_output,
        given,
    )

    back_v = back_v.reshape(rank, 4, 2, rows)
    mine = back_v[:, :, 0] + routes.core(back_v[:, :, 1])
    mine = mine[:, 0::2] + routes.across_y(mine[:, 1::2])
    mine = mine[:, 0] + routes.down(mine[:, 1])
    back = sum_over_tensor(jnp.concatenate((back_q, mine), axis=0)).astype(BF16)
    grad_down = dot(back, hidden_in, NN)

    summed = sum_over_seq(
        jnp.concatenate(
            (grad_down[:rank], grad_down[rank:], grad_up_q, grad_up_v), axis=1
        ).astype(BF16)
    ).astype(F32)
    grad_down_query = summed[:, :width_here].T
    grad_down_value = summed[:, width_here : 2 * width_here].T
    grad_up_query = summed[:, 2 * width_here : -kv_width]
    grad_up_value = summed[:, -kv_width:]
    return attention, grad_down_query, grad_up_query, grad_down_value, grad_up_value


def solution(mesh):
    placed = (
        P("seq", "tensor"),
        P("seq", "tensor"),
        P("seq", "tensor"),
        P("seq", "tensor"),
        P("tensor", None),
        P(None, "tensor"),
        P("tensor", None),
        P(None, "tensor"),
        P("seq", "tensor"),
    )
    return jax.shard_map(
        per_device,
        mesh=mesh,
        in_specs=placed,
        out_specs=(
            P("seq", "tensor"),
            P("tensor", None),
            P(None, "tensor"),
            P("tensor", None),
            P(None, "tensor"),
        ),
        check_vma=False,
    )
```

time: 196 us -> 149 us (0.76)
  local copies, waits for them, and re-layouts: 23.1 us -> 7.19 us
  waiting for transfers between devices: 75.2 us -> 60.9 us
  starting transfers between devices: 53.9 us -> 41.2 us
  Pallas kernels: 38.1 us -> 31 us
  other arithmetic: 1.14 us -> 4.29 us
    ppermute x19 -> x15, starting transfers between devices: 42.5 us -> 31 us  [send(): return lax.ppermute(block, AXES, route)]
    ppermute x19 -> x15, waiting for transfers between devices: 48.1 us -> 37.8 us  [send(): return lax.ppermute(block, AXES, route)]
    unnamed x29 -> x12, local copies, waits for them, and re-layouts: 9.94 us -> 2.33 us
    pallas_call x1, Pallas kernels: 38.1 us -> 31 us  [attention_call(): pl.pallas_call(functools.partial(attention_body, rows, per_head, kv, stac...]
    slice x8 -> x1, local copies, waits for them, and re-layouts: 5.32 us -> 0.59 us  [per_device(): low_v = gather_low(routes, low_t[rank:])]
    ppermute x2, waiting for transfers between devices: 3.77 us -> 0.17 us  [sum_over_tensor(): lax.ppermute(part, 'tensor', [(i, i ^ step) for i in range(size)])]
    reshape x8 -> x1, local copies, waits for them, and re-layouts: 2.77 us -> 0.67 us  [gather_low(): return both.reshape(rank, -1)]
  transfers between devices with their start and end apart: 26 -> 22, of which waited for: 12 -> 12; matrix products, arithmetic and copies ran while one was open for 9% -> 4% of each run, Pallas kernels for 0% -> 0%
where the time goes in v2:
time: 149 us; the launch traced here: 148 us
  waiting for transfers between devices  60.9 us (41%)
  starting transfers between devices  41.2 us (28%)
  Pallas kernels  31 us (21%)
  local copies, waits for them, and re-layouts  7.19 us (5%)
  other arithmetic  4.29 us (3%)
  matrix products  2.88 us (2%)
    ppermute x15, waiting for transfers between devices, send(): return lax.ppermute(block, AXES, route)  37.8 us
    pallas_call x1, Pallas kernels, attention_call(): pl.pallas_call(functools.partial(attention_body, rows, per_head, kv, stac...  31 us
    ppermute x15, starting transfers between devices, send(): return lax.ppermute(block, AXES, route)  31 us
    ppermute x3, waiting for transfers between devices, sum_over_seq(): got = lax.ppermute(sent, 'seq', [(i, i ^ step) for i in range(size)])  20.1 us
    ppermute x2, starting transfers between devices, sum_over_tensor(): lax.ppermute(part, 'tensor', [(i, i ^ step) for i in range(size)])  5.29 us
    ppermute x3, starting transfers between devices, sum_over_seq(): got = lax.ppermute(sent, 'seq', [(i, i ^ step) for i in range(size)])  4.75 us
  transfers between devices with their start and end apart: 22, of which 12 were waited for; matrix products, arithmetic and copies ran while one was open for 4% of the time, Pallas kernels for 0%

profile of v2, /device:TPU:0, one launch (start us, length us, event | category | flops | bytes accessed | tf_op | source)
XLA Modules:
  0.0 148.3 jit_solution(11421185514104907242)
XLA Ops:
  0.7 1.6 %copy-done = bf16[256,4096]{1,0:T(8,128)(2,1)S(1)} copy-done((bf16[256,4096]{1,0:T(8,128)(2,1)S(1)}, bf16[256,4096]{1,0:T(8,128)(2,1)}, u32[]{:S(2)}) %copy-start) | copy-done | bytes 2097176
  2.2 1.7 %fusion = f32[32,256]{1,0:T(8,128)S(1)} fusion(bf16[256,4096]{1,0:T(8,128)(2,1)S(1)} %copy-done, bf16[4096,16]{0,1:T(8,128)(2,1)} %param.15, bf16[4096,16]{0,1:T(8,128)(2,1)} %param.13), kind=kOutput, calls=%fused_computation.8 | convolution fusion | flops 67633152 | bytes 2392064 | tf_op jit(solution)/shard_map/dot_general | solution.py:314
  3.9 3.0 %collective-permute-start = (f32[32,256]{1,0:T(8,128)S(1)}, f32[32,256]{1,0:T(8,128)S(1)}, u32[]{:S(2)}, u32[]{:S(2)}) collective-permute-start(f32[32,256]{1,0:T(8,128)S(1)} %fusion), channel_id=1, source_target_pairs={{0,1},{1,0},{2,3},{3,2},{4,5},{5,4},{6,7},{7,6},{8,9},{9,8},{10,11... | collective-permute-start | bytes 98312 | tf_op jit(solution)/shard_map/ppermute | solution.py:266
  8.4 3.5 %collective-permute-start.7 = (bf16[256,1024]{1,0:T(8,128)(2,1)}, bf16[256,1024]{1,0:T(8,128)(2,1)S(1)}, u32[]{:S(2)}, u32[]{:S(2)}) collective-permute-start(bf16[256,1024]{1,0:T(8,128)(2,1)} %constant_dynamic-update-slice_fusion.refs_7_), channel_id=1, source_target_pairs={{0,8},{2,10},{4,12},{6,14},{9,17},{11,19},{13,21},{15,23},{16,24},... | collective-permute-start | bytes 1572872 | tf_op jit(solution)/shard_map/ppermute | solution.py:218
  11.9 3.4 %collective-permute-start.5 = (bf16[256,1024]{1,0:T(8,128)(2,1)}, bf16[256,1024]{1,0:T(8,128)(2,1)S(1)}, u32[]{:S(2)}, u32[]{:S(2)}) collective-permute-start(bf16[256,1024]{1,0:T(8,128)(2,1)} %constant_dynamic-update-slice_fusion.refs_7_), channel_id=1, source_target_pairs={{0,4},{1,5},{2,6},{3,7},{4,0},{6,2},{8,12},{9,13},{10,14},{11,15},... | collective-permute-start | bytes 1572872 | tf_op jit(solution)/shard_map/ppermute | solution.py:218
  16.5 10.8 %collective-permute-done.1 = bf16[16,256]{1,0:T(8,128)(2,1)S(1)} collective-permute-done((bf16[16,256]{1,0:T(8,128)(2,1)S(1)}, bf16[16,256]{1,0:T(8,128)(2,1)S(1)}, u32[]{:S(2)}, u32[]{:S(2)}) %collective-permute-start.1) | collective-permute-done | bytes 8224 | tf_op jit(solution)/shard_map/ppermute | solution.py:218
  27.3 1.3 collective-permute-start.2
  28.6 1.4 collective-permute-done.2
  30.6 1.4 collective-permute-start.10
  32.0 7.2 %collective-permute-start.9 = (bf16[128,1024]{1,0:T(8,128)(2,1)S(1)}, bf16[128,1024]{1,0:T(8,128)(2,1)}, u32[]{:S(2)}, u32[]{:S(2)}) collective-permute-start(bf16[128,1024]{1,0:T(8,128)(2,1)S(1)} %slice.78), channel_id=1, source_target_pairs={{0,8},{2,10},{4,12},{6,14},{9,17},{11,19},{13,21},{15,23},{16,24},... | collective-permute-start | bytes 786440 | tf_op jit(solution)/shard_map/ppermute | solution.py:218
  39.8 4.2 %collective-permute-done.9.refs_13_ = bf16[128,1024]{1,0:T(8,128)(2,1)} collective-permute-done((bf16[128,1024]{1,0:T(8,128)(2,1)S(1)}, bf16[128,1024]{1,0:T(8,128)(2,1)}, u32[]{:S(2)}, u32[]{:S(2)}) %collective-permute-start.9) | collective-permute-done | bytes 262176 | tf_op jit(solution)/shard_map/ppermute | solution.py:218
  46.3 31.0 %shard_map.128 = (bf16[256,4096]{1,0:T(8,128)(2,1)}, f32[16,4096]{1,0:T(8,128)}, f32[16,256]{1,0:T(8,128)}, f32[16,2048]{1,0:T(8,128)}, f32[16,512]{1,0:T(8,128)}) custom-call(s32[3]{0:T(128)} %pad_add_fusion.where, bf16[256,4096]{1,0:T(8,128)(2,1)} %refs_0_.1, bf16[256,16]{1,0:T(8,128)(2,1)} %copy.16.refs_1_, bf16[16,256]{1,0:T(8,128)(2,1)} %get-tuple-element.26.refs_2_, ...), custom_call_target="tpu_custom_call" | custom-call | flops 21474836480 | bytes 16777216 | tf_op jit(solution)/shard_map/pallas_call | solution.py:172
  79.9 10.7 %collective-permute-start.14 = (f32[16,2,256]{2,0,1:T(8,128)S(1)}, f32[16,2,256]{2,0,1:T(8,128)S(1)}, u32[]{:S(2)}, u32[]{:S(2)}) collective-permute-start(f32[16,2,256]{2,0,1:T(8,128)S(1)} %slice.65), channel_id=1, source_target_pairs={{0,4},{1,5},{2,6},{3,7},{4,0},{5,1},{6,2},{7,3},{8,12},{9,13},{10,... | collective-permute-start | bytes 98312 | tf_op jit(solution)/shard_map/ppermute | solution.py:218
  90.6 1.9 %collective-permute-done.14 = f32[16,2,256]{2,0,1:T(8,128)S(1)} collective-permute-done((f32[16,2,256]{2,0,1:T(8,128)S(1)}, f32[16,2,256]{2,0,1:T(8,128)S(1)}, u32[]{:S(2)}, u32[]{:S(2)}) %collective-permute-start.14) | collective-permute-done | bytes 32800 | tf_op jit(solution)/shard_map/ppermute | solution.py:218
  92.6 1.3 collective-permute-start.15
  93.9 18.5 %collective-permute-done.15 = f32[16,256]{1,0:T(8,128)S(1)} collective-permute-done((f32[16,256]{1,0:T(8,128)S(1)}, f32[16,256]{1,0:T(8,128)S(1)}, u32[]{:S(2)}, u32[]{:S(2)}) %collective-permute-start.15) | collective-permute-done | bytes 16416 | tf_op jit(solution)/shard_map/ppermute | solution.py:218
  113.1 2.3 %collective-permute-start.16 = (f32[32,256]{1,0:T(8,128)S(1)}, f32[32,256]{1,0:T(8,128)S(1)}, u32[]{:S(2)}, u32[]{:S(2)}) collective-permute-start(f32[32,256]{1,0:T(8,128)S(1)} %pad_maximum_fusion.5), channel_id=1, source_target_pairs={{0,1},{1,0},{2,3},{3,2},{4,5},{5,4},{6,7},{7,6},{8,9},{9,8},{10,11... | collective-permute-start | bytes 98312 | tf_op jit(solution)/shard_map/ppermute | solution.py:266
  118.7 1.4 collective-permute-done.17
  120.2 1.7 %collective-permute-start.18 = (bf16[16,6400]{1,0:T(8,128)(2,1)S(1)}, bf16[16,6400]{1,0:T(8,128)(2,1)S(1)}, u32[]{:S(2)}, u32[]{:S(2)}) collective-permute-start(bf16[16,6400]{1,0:T(8,128)(2,1)S(1)} %add_convert_fusion.3), channel_id=1, source_target_pairs={{0,4},{2,6},{4,0},{6,2},{8,12},{10,14},{12,8},{14,10},{16,20},{18,... | collective-permute-start | bytes 614408 | tf_op jit(solution)/shard_map/ppermute | solution.py:281
  121.9 5.5 %collective-permute-done.18 = bf16[16,6400]{1,0:T(8,128)(2,1)S(1)} collective-permute-done((bf16[16,6400]{1,0:T(8,128)(2,1)S(1)}, bf16[16,6400]{1,0:T(8,128)(2,1)S(1)}, u32[]{:S(2)}, u32[]{:S(2)}) %collective-permute-start.18) | collective-permute-done | bytes 204832 | tf_op jit(solution)/shard_map/ppermute | solution.py:281
  127.5 6.3 %collective-permute-done.19 = bf16[16,6400]{1,0:T(8,128)(2,1)S(1)} collective-permute-done((bf16[16,6400]{1,0:T(8,128)(2,1)S(1)}, bf16[16,6400]{1,0:T(8,128)(2,1)S(1)}, u32[]{:S(2)}, u32[]{:S(2)}) %collective-permute-start.19) | collective-permute-done | bytes 204832 | tf_op jit(solution)/shard_map/ppermute | solution.py:281
  133.8 3.0 %collective-permute-start.20 = (bf16[16,6400]{1,0:T(8,128)(2,1)S(1)}, bf16[16,6400]{1,0:T(8,128)(2,1)S(1)}, u32[]{:S(2)}, u32[]{:S(2)}) collective-permute-start(bf16[16,6400]{1,0:T(8,128)(2,1)S(1)} %add_convert_fusion.1), channel_id=1, source_target_pairs={{0,16},{2,18},{4,20},{6,22},{8,24},{10,26},{12,28},{14,30},{16,0},... | collective-permute-start | bytes 614408 | tf_op jit(solution)/shard_map/ppermute | solution.py:281
  136.8 8.3 %collective-permute-done.20 = bf16[16,6400]{1,0:T(8,128)(2,1)S(1)} collective-permute-done((bf16[16,6400]{1,0:T(8,128)(2,1)S(1)}, bf16[16,6400]{1,0:T(8,128)(2,1)S(1)}, u32[]{:S(2)}, u32[]{:S(2)}) %collective-permute-start.20) | collective-permute-done | bytes 204832 | tf_op jit(solution)/shard_map/ppermute | solution.py:281
  145.3 1.4 collective-permute-done.21
  (68 shorter events, 14.6 us)
Async XLA Ops:
  3.9 11.4 %collective-permute-start = (f32[32,256]{1,0:T(8,128)S(1)}, f32[32,256]{1,0:T(8,128)S(1)}, u32[]{:S(2)}, u32[]{:S(2)}) collective-permute-start(f32[32,256]{1,0:T(8,128)S(1)} %fusion), channel_id=1, source_target_pairs={{0,1},{1,0},{2,3},{3,2},{4,5},{5,4},{6,7},{7,6},{8,9},{9,8},{10,11... | collective-permute-start | bytes 98312 | tf_op jit(solution)/shard_map/ppermute | solution.py:266
  8.4 22.1 %collective-permute-start.7 = (bf16[256,1024]{1,0:T(8,128)(2,1)}, bf16[256,1024]{1,0:T(8,128)(2,1)S(1)}, u32[]{:S(2)}, u32[]{:S(2)}) collective-permute-start(bf16[256,1024]{1,0:T(8,128)(2,1)} %constant_dynamic-update-slice_fusion.refs_7_), channel_id=1, source_target_pairs={{0,8},{2,10},{4,12},{6,14},{9,17},{11,19},{13,21},{15,23},{16,24},... | collective-permute-start | bytes 1572872 | tf_op jit(solution)/shard_map/ppermute | solution.py:218
  11.9 20.0 %collective-permute-start.5 = (bf16[256,1024]{1,0:T(8,128)(2,1)}, bf16[256,1024]{1,0:T(8,128)(2,1)S(1)}, u32[]{:S(2)}, u32[]{:S(2)}) collective-permute-start(bf16[256,1024]{1,0:T(8,128)(2,1)} %constant_dynamic-update-slice_fusion.refs_7_), channel_id=1, source_target_pairs={{0,4},{1,5},{2,6},{3,7},{4,0},{6,2},{8,12},{9,13},{10,14},{11,15},... | collective-permute-start | bytes 1572872 | tf_op jit(solution)/shard_map/ppermute | solution.py:218
  16.0 11.3 %collective-permute-start.1 = (bf16[16,256]{1,0:T(8,128)(2,1)S(1)}, bf16[16,256]{1,0:T(8,128)(2,1)S(1)}, u32[]{:S(2)}, u32[]{:S(2)}) collective-permute-start(bf16[16,256]{1,0:T(8,128)(2,1)S(1)} %get-tuple-element.24), channel_id=1, source_target_pairs={{0,4},{1,5},{2,6},{3,7},{4,0},{5,1},{6,2},{7,3},{8,12},{9,13},{10,... | collective-permute-start | bytes 24584 | tf_op jit(solution)/shard_map/ppermute | solution.py:218
  27.3 2.7 %collective-permute-start.2 = (bf16[16,512]{1,0:T(8,128)(2,1)S(1)}, bf16[16,512]{1,0:T(8,128)(2,1)S(1)}, u32[]{:S(2)}, u32[]{:S(2)}) collective-permute-start(bf16[16,512]{1,0:T(8,128)(2,1)S(1)} %pad_maximum_fusion.6), channel_id=1, source_target_pairs={{0,8},{2,10},{4,12},{6,14},{9,17},{11,19},{13,21},{15,23},{16,24},... | collective-permute-start | bytes 49160 | tf_op jit(solution)/shard_map/ppermute | solution.py:218
  30.0 9.2 %collective-permute-start.3 = (bf16[16,1024]{1,0:T(8,128)(2,1)S(1)}, bf16[16,1024]{1,0:T(8,128)(2,1)S(1)}, u32[]{:S(2)}, u32[]{:S(2)}) collective-permute-start(bf16[16,1024]{1,0:T(8,128)(2,1)S(1)} %pad_maximum_fusion.4), channel_id=1, source_target_pairs={{0,2},{1,3},{2,0},{3,1},{4,6},{5,7},{6,4},{7,5},{8,10},{9,11},{10,... | collective-permute-start | bytes 98312 | tf_op jit(solution)/shard_map/ppermute | solution.py:218
  30.0 16.2 %collective-permute-start.4 = (bf16[256,1024]{1,0:T(8,128)(2,1)}, bf16[256,1024]{1,0:T(8,128)(2,1)}, u32[]{:S(2)}, u32[]{:S(2)}) collective-permute-start(bf16[256,1024]{1,0:T(8,128)(2,1)} %constant_dynamic-update-slice_fusion.refs_7_), channel_id=1, source_target_pairs={{0,2},{1,3},{2,0},{3,1},{4,6},{5,7},{6,4},{7,5},{8,10},{9,11},{10,... | collective-permute-start | bytes 1572872 | tf_op jit(solution)/shard_map/ppermute | solution.py:218
  30.5 15.7 %copy-start.3 = (bf16[256,1024]{1,0:T(8,128)(2,1)}, bf16[256,1024]{1,0:T(8,128)(2,1)S(1)}, u32[]{:S(2)}) copy-start(bf16[256,1024]{1,0:T(8,128)(2,1)S(1)} %collective-permute-done.7.refs_11_) | copy-start | bytes 1572868
  30.6 9.2 %collective-permute-start.10 = (bf16[128,1024]{1,0:T(8,128)(2,1)S(1)}, bf16[128,1024]{1,0:T(8,128)(2,1)}, u32[]{:S(2)}, u32[]{:S(2)}) collective-permute-start(bf16[128,1024]{1,0:T(8,128)(2,1)S(1)} %slice.79), channel_id=1, source_target_pairs={{1,5},{3,7},{5,1},{7,3},{8,12},{10,14},{12,8},{14,10},{17,21},{19,... | collective-permute-start | bytes 786440 | tf_op jit(solution)/shard_map/ppermute | solution.py:218
  31.9 14.3 %copy-start.4 = (bf16[256,1024]{1,0:T(8,128)(2,1)}, bf16[256,1024]{1,0:T(8,128)(2,1)S(1)}, u32[]{:S(2)}) copy-start(bf16[256,1024]{1,0:T(8,128)(2,1)S(1)} %collective-permute-done.5.refs_9_) | copy-start | bytes 1572868
  32.0 12.0 %collective-permute-start.9 = (bf16[128,1024]{1,0:T(8,128)(2,1)S(1)}, bf16[128,1024]{1,0:T(8,128)(2,1)}, u32[]{:S(2)}, u32[]{:S(2)}) collective-permute-start(bf16[128,1024]{1,0:T(8,128)(2,1)S(1)} %slice.78), channel_id=1, source_target_pairs={{0,8},{2,10},{4,12},{6,14},{9,17},{11,19},{13,21},{15,23},{16,24},... | collective-permute-start | bytes 786440 | tf_op jit(solution)/shard_map/ppermute | solution.py:218
  39.2 7.0 %collective-permute-start.8 = (bf16[256,1024]{1,0:T(8,128)(2,1)S(1)}, bf16[256,1024]{1,0:T(8,128)(2,1)}, u32[]{:S(2)}, u32[]{:S(2)}) collective-permute-start(bf16[256,1024]{1,0:T(8,128)(2,1)S(1)} %collective-permute-done.7.refs_11_), channel_id=1, source_target_pairs={{0,2},{1,3},{2,0},{3,1},{4,6},{5,7},{6,4},{7,5},{8,10},{9,11},{10,... | collective-permute-start | bytes 1572872 | tf_op jit(solution)/shard_map/ppermute | solution.py:218
  39.2 7.1 %collective-permute-start.6 = (bf16[256,1024]{1,0:T(8,128)(2,1)S(1)}, bf16[256,1024]{1,0:T(8,128)(2,1)}, u32[]{:S(2)}, u32[]{:S(2)}) collective-permute-start(bf16[256,1024]{1,0:T(8,128)(2,1)S(1)} %collective-permute-done.5.refs_9_), channel_id=1, source_target_pairs={{0,2},{1,3},{2,0},{3,1},{4,6},{5,7},{6,4},{7,5},{8,10},{9,11},{10,... | collective-permute-start | bytes 1572872 | tf_op jit(solution)/shard_map/ppermute | solution.py:218
  39.7 6.5 %collective-permute-start.12 = (bf16[128,1024]{1,0:T(8,128)(2,1)}, bf16[128,1024]{1,0:T(8,128)(2,1)}, u32[]{:S(2)}, u32[]{:S(2)}) collective-permute-start(bf16[128,1024]{1,0:T(8,128)(2,1)} %collective-permute-done.10.refs_14_), channel_id=1, source_target_pairs={{0,2},{1,3},{2,0},{3,1},{4,6},{5,7},{6,4},{7,5},{8,10},{9,11},{10,... | collective-permute-start | bytes 786440 | tf_op jit(solution)/shard_map/ppermute | solution.py:218
  43.9 2.3 %collective-permute-start.11 = (bf16[128,1024]{1,0:T(8,128)(2,1)}, bf16[128,1024]{1,0:T(8,128)(2,1)}, u32[]{:S(2)}, u32[]{:S(2)}) collective-permute-start(bf16[128,1024]{1,0:T(8,128)(2,1)} %collective-permute-done.9.refs_13_), channel_id=1, source_target_pairs={{0,2},{1,3},{2,0},{3,1},{4,6},{5,7},{6,4},{7,5},{8,10},{9,11},{10,... | collective-permute-start | bytes 786440 | tf_op jit(solution)/shard_map/ppermute | solution.py:218
  78.4 1.5 collective-permute-start.13
  79.9 12.6 %collective-permute-start.14 = (f32[16,2,256]{2,0,1:T(8,128)S(1)}, f32[16,2,256]{2,0,1:T(8,128)S(1)}, u32[]{:S(2)}, u32[]{:S(2)}) collective-permute-start(f32[16,2,256]{2,0,1:T(8,128)S(1)} %slice.65), channel_id=1, source_target_pairs={{0,4},{1,5},{2,6},{3,7},{4,0},{5,1},{6,2},{7,3},{8,12},{9,13},{10,... | collective-permute-start | bytes 98312 | tf_op jit(solution)/shard_map/ppermute | solution.py:218
  92.6 19.8 %collective-permute-start.15 = (f32[16,256]{1,0:T(8,128)S(1)}, f32[16,256]{1,0:T(8,128)S(1)}, u32[]{:S(2)}, u32[]{:S(2)}) collective-permute-start(f32[16,256]{1,0:T(8,128)S(1)} %slice_bitcast_fusion.2), channel_id=1, source_target_pairs={{1,25},{3,27},{5,29},{7,31},{8,0},{10,2},{12,4},{14,6},{17,9},{19,... | collective-permute-start | bytes 49160 | tf_op jit(solution)/shard_map/ppermute | solution.py:218
  113.1 4.2 %collective-permute-start.16 = (f32[32,256]{1,0:T(8,128)S(1)}, f32[32,256]{1,0:T(8,128)S(1)}, u32[]{:S(2)}, u32[]{:S(2)}) collective-permute-start(f32[32,256]{1,0:T(8,128)S(1)} %pad_maximum_fusion.5), channel_id=1, source_target_pairs={{0,1},{1,0},{2,3},{3,2},{4,5},{5,4},{6,7},{7,6},{8,9},{9,8},{10,11... | collective-permute-start | bytes 98312 | tf_op jit(solution)/shard_map/ppermute | solution.py:266
  118.6 1.5 %collective-permute-start.17 = (bf16[16,6400]{1,0:T(8,128)(2,1)S(1)}, bf16[16,6400]{1,0:T(8,128)(2,1)S(1)}, u32[]{:S(2)}, u32[]{:S(2)}) collective-permute-start(bf16[16,6400]{1,0:T(8,128)(2,1)S(1)} %broadcast_select_fusion.2), channel_id=1, source_target_pairs={{0,2},{2,0},{4,6},{6,4},{8,10},{10,8},{12,14},{14,12},{16,18},{18,... | collective-permute-start | bytes 614408 | tf_op jit(solution)/shard_map/ppermute | solution.py:276
  120.2 7.2 %collective-permute-start.18 = (bf16[16,6400]{1,0:T(8,128)(2,1)S(1)}, bf16[16,6400]{1,0:T(8,128)(2,1)S(1)}, u32[]{:S(2)}, u32[]{:S(2)}) collective-permute-start(bf16[16,6400]{1,0:T(8,128)(2,1)S(1)} %add_convert_fusion.3), channel_id=1, source_target_pairs={{0,4},{2,6},{4,0},{6,2},{8,12},{10,14},{12,8},{14,10},{16,20},{18,... | collective-permute-start | bytes 614408 | tf_op jit(solution)/shard_map/ppermute | solution.py:281
  127.4 6.4 %collective-permute-start.19 = (bf16[16,6400]{1,0:T(8,128)(2,1)S(1)}, bf16[16,6400]{1,0:T(8,128)(2,1)S(1)}, u32[]{:S(2)}, u32[]{:S(2)}) collective-permute-start(bf16[16,6400]{1,0:T(8,128)(2,1)S(1)} %add_convert_fusion.2), channel_id=1, source_target_pairs={{0,8},{2,10},{4,12},{6,14},{8,0},{10,2},{12,4},{14,6},{16,24},{18,... | collective-permute-start | bytes 614408 | tf_op jit(solution)/shard_map/ppermute | solution.py:281
  133.8 11.3 %collective-permute-start.20 = (bf16[16,6400]{1,0:T(8,128)(2,1)S(1)}, bf16[16,6400]{1,0:T(8,128)(2,1)S(1)}, u32[]{:S(2)}, u32[]{:S(2)}) collective-permute-start(bf16[16,6400]{1,0:T(8,128)(2,1)S(1)} %add_convert_fusion.1), channel_id=1, source_target_pairs={{0,16},{2,18},{4,20},{6,22},{8,24},{10,26},{12,28},{14,30},{16,0},... | collective-permute-start | bytes 614408 | tf_op jit(solution)/shard_map/ppermute | solution.py:281
  145.2 1.5 %collective-permute-start.21 = (bf16[16,6400]{1,0:T(8,128)(2,1)S(1)}, bf16[16,6400]{1,0:T(8,128)(2,1)S(1)}, u32[]{:S(2)}, u32[]{:S(2)}) collective-permute-start(bf16[16,6400]{1,0:T(8,128)(2,1)S(1)} %add_convert_fusion), channel_id=1, source_target_pairs={{0,2},{2,0},{4,6},{6,4},{8,10},{10,8},{12,14},{14,12},{16,18},{18,... | collective-permute-start | bytes 614408 | tf_op jit(solution)/shard_map/ppermute | solution.py:285
  (3 other events, 14.9 us)

commit v3 on v2

--- a/solution.py
+++ b/solution.py
@@ -25,17 +25,24 @@
     return lax.dot_general(a, b, dims, preferred_element_type=F32)
 
 
+def place_in_group(blocks):
+    shifted = lax.axis_index("tensor") >= lax.axis_size("tensor") // 2
+    return (lax.axis_index("seq") + jnp.where(shifted, blocks // 2, 0)) % blocks
+
+
 ONES = 16
 
 
-def attention_body(rows, per_head, kv, stacked, where, *refs):
-    frozen, low_q, low_q_t, up_q, up_v, low_v, grad_out = refs[:7]
-    given = refs[7:17]
-    out, grad_up_q, back_q, back_v, grad_up_v = refs[17:22]
-    scores, probs, grad_s, keys, keys_t, values, values_t, grad_v = refs[22:]
+def attention_body(rows, per_head, kv, stacked, blocks_in_group, *refs):
+    frozen, low_q_t, up_q, up_v, grad_out = refs[:5]
+    low_v = refs[5:9]
+    given = refs[9:19]
+    out, grad_up_q, back_q, back_v, back_v_sibling, grad_up_v = refs[19:25]
+    low_q, scores, probs, grad_s, keys, keys_t, values, values_t, grad_v = refs[25:]
     scale = float(HD) ** -0.5
     to_log2 = scale * LOG2E
-    core, y_bit, z_bit = where[0], where[1], where[2]
+    place = place_in_group(blocks_in_group)
+    core, y_bit, z_bit = place % 2, place // (blocks_in_group // 4) % 2, place // (blocks_in_group // 2)
     half = rows // 2
     parts = [(given[j], 0, rows) for j in range(6)]
     parts = [[p] for p in parts]
@@ -46,6 +53,8 @@
     steps_per_kv = per_head // stacked
     back_q[...] = jnp.zeros_like(back_q)
     back_v[...] = jnp.zeros_like(back_v)
+    back_v_sibling[...] = jnp.zeros_like(back_v)
+    low_q[...] = low_q_t[...].T
     key_at = lax.broadcasted_iota(jnp.int32, (rows, columns), 0)
     query_at = lax.broadcasted_iota(jnp.int32, (rows, columns), 1) % rows
 
@@ -53,12 +62,12 @@
         for slot, j in enumerate(blocks):
             for ref, first, count in parts[j]:
                 at = slice(slot * rows + first, slot * rows + first + count)
-                low_at = slice(j * rows + first, j * rows + first + count)
+                low_at = slice(j % 2 * rows + first, j % 2 * rows + first + count)
                 block = ref[:, :width_kv]
                 keys[at, :] = block
                 keys_t[:, at] = block.T
                 added = lax.dot_general(
-                    low_v[:, low_at], up_v[...], (((0,), (0,)), ((), ())), preferred_element_type=F32
+                    low_v[j // 2][:, low_at], up_v[...], (((0,), (0,)), ((), ())), preferred_element_type=F32
                 )
                 block = (ref[:, width_kv:].astype(F32) + ADAPTER_SCALE * added).astype(BF16)
                 values[at, :] = block
@@ -74,11 +83,12 @@
             total = None
             for slot, j in enumerate(blocks):
                 rounded = grad_v[slot * rows : (slot + 1) * rows, cols].astype(BF16)
-                at = slice(j * rows, (j + 1) * rows)
-                back_v[:, at] += ADAPTER_SCALE * dot(up_v[:, cols], rounded, NT)
-                term = dot(low_v[:, at], rounded, NN)
+                at = slice(j // 2 * rows, (j // 2 + 1) * rows)
+                target = back_v_sibling if j % 2 else back_v
+                target[:, at] += ADAPTER_SCALE * dot(up_v[:, cols], rounded, NT)
+                term = dot(low_v[j // 2][:, j % 2 * rows : (j % 2 + 1) * rows], rounded, NN)
                 total = term if total is None else total + term
-            grad_up_v[:, cols] = ADAPTER_SCALE * total
+            grad_up_v[:, cols] = (ADAPTER_SCALE * total).astype(BF16)
 
     def attend(length, pipelined):
         def wide(i):
@@ -125,7 +135,7 @@
             back = None
             for a in range(stacked):
                 one = grad_query[:, a * rows : (a + 1) * rows]
-                grad_up_q[:, narrow(i, a)] = ADAPTER_SCALE * dot(low_q_t[...], one, NT)
+                grad_up_q[:, narrow(i, a)] = (ADAPTER_SCALE * dot(low_q_t[...], one, NT)).astype(BF16)
                 term = dot(up_q[:, narrow(i, a)], one, NN)
                 back = term if back is None else back + term
             back_q[...] += ADAPTER_SCALE * back
@@ -160,20 +170,21 @@
                 finish(blocks)
 
 
-def attention_call(where, frozen, low_q, low_q_t, up_q, up_v, low_v, grad_out, given):
+def attention_call(frozen, low_q_t, up_q, up_v, grad_out, low_v, given):
     rows, width = frozen.shape
     kv = up_v.shape[1] // HD
     rank = up_q.shape[0]
     per_head = width // HD // kv
-    reach = low_v.shape[1]
+    reach = GROUP
     stacked = 2
     vmem = pl.BlockSpec(memory_space=pltpu.VMEM)
     pairs = rows * reach * per_head * kv
     return pl.pallas_call(
-        functools.partial(attention_body, rows, per_head, kv, stacked),
-        in_specs=[pl.BlockSpec(memory_space=pltpu.SMEM)] + [vmem] * (7 + len(given)),
-        out_specs=[vmem] * 5,
+        functools.partial(attention_body, rows, per_head, kv, stacked, GROUP // rows),
+        in_specs=[vmem] * (5 + len(low_v) + len(given)),
+        out_specs=[vmem] * 6,
         scratch_shapes=[
+            pltpu.VMEM((rows, rank), BF16),
             pltpu.VMEM((2, reach, stacked * rows), F32),
             pltpu.VMEM((reach, stacked * rows), BF16),
             pltpu.VMEM((reach, stacked * rows), BF16),
@@ -185,16 +196,17 @@
         ],
         out_shape=[
             jax.ShapeDtypeStruct((rows, width), BF16),
-            jax.ShapeDtypeStruct((rank, width), F32),
+            jax.ShapeDtypeStruct((rank, width), BF16),
             jax.ShapeDtypeStruct((rank, rows), F32),
-            jax.ShapeDtypeStruct((rank, reach), F32),
-            jax.ShapeDtypeStruct((rank, kv * HD), F32),
+            jax.ShapeDtypeStruct((rank, reach // 2), F32),
+            jax.ShapeDtypeStruct((rank, reach // 2), F32),
+            jax.ShapeDtypeStruct((rank, kv * HD), BF16),
         ],
         compiler_params=pltpu.CompilerParams(vmem_limit_bytes=56 * 2**20),
         cost_estimate=pl.CostEstimate(
             flops=10 * pairs * HD, bytes_accessed=16 * rows * width, transcendentals=pairs
         ),
-    )(where, frozen, low_q, low_q_t, up_q, up_v, low_v, grad_out, *given)
+    )(frozen, low_q_t, up_q, up_v, grad_out, *low_v, *given)
 
 
 class Routes:
@@ -230,6 +242,11 @@
 
     def up(self, block):
         return self.send(block, lambda s, t: None if self.upper(s, t) else s + self.half)
+
+    def up_across_y(self, block):
+        return self.send(
+            block, lambda s, t: None if self.upper(s, t) else (s + self.half) ^ self.y
+        )
 
     def within_upper(self, block):
         return self.send(block, lambda s, t: s ^ self.y if self.upper(s, t) else None)
@@ -251,12 +268,8 @@
 
 
 def gather_low(routes, own):
-    near = jnp.concatenate((own, routes.across_y(own)), axis=1)
-    mine = jnp.concatenate((near, routes.up(near)), axis=1)
-    other = routes.core(mine)
-    rank = own.shape[0]
-    both = jnp.stack((mine.reshape(rank, 4, -1), other.reshape(rank, 4, -1)), axis=2)
-    return both.reshape(rank, -1)
+    both = jnp.concatenate((own, routes.core(own)), axis=1)
+    return [both, routes.across_y(both), routes.up(both), routes.up_across_y(both)]
 
 
 def sum_over_tensor(part):
@@ -268,22 +281,35 @@
     return part
 
 
-def sum_over_seq(part):
-    size = lax.axis_size("seq")
+def swap(block, step):
+    return lax.ppermute(block, "seq", [(i, i ^ step) for i in range(lax.axis_size("seq"))])
+
+
+def split_for_core(part):
     odd = lax.axis_index("seq") % 2 == 1
     half = part.shape[1] // 2
     low, high = part[:, :half], part[:, half:]
-    got = lax.ppermute(jnp.where(odd, low, high), "seq", [(i, i ^ 1) for i in range(size)])
-    total = jnp.where(odd, high, low).astype(F32) + got.astype(F32)
+    return jnp.where(odd, high, low), jnp.where(odd, low, high)
+
+
+def join_cores(total):
+    odd = lax.axis_index("seq") % 2 == 1
+    got = swap(total, 1)
+    return jnp.concatenate((jnp.where(odd, got, total), jnp.where(odd, total, got)), axis=1)
+
+
+def add_up(mine, got):
+    return (mine.astype(F32) + got.astype(F32)).astype(BF16)
+
+
+def sum_over_seq(part):
+    kept, sent = split_for_core(part)
+    total = add_up(kept, swap(sent, 1))
     step = 2
-    while step < size:
-        sent = total.astype(BF16)
-        got = lax.ppermute(sent, "seq", [(i, i ^ step) for i in range(size)])
-        total = sent.astype(F32) + got.astype(F32)
+    while step < lax.axis_size("seq"):
+        total = add_up(total, swap(total, step))
         step *= 2
-    total = total.astype(BF16)
-    got = lax.ppermute(total, "seq", [(i, i ^ 1) for i in range(size)])
-    return jnp.concatenate((jnp.where(odd, got, total), jnp.where(odd, total, got)), axis=1)
+    return join_cores(total)
 
 
 def per_device(
@@ -304,11 +330,6 @@
     blocks = GROUP // rows
     assert blocks == 8 and rows % 32 == 0
     routes = Routes(blocks)
-    seq_at, tensor_at = lax.axis_index("seq"), lax.axis_index("tensor")
-    offset = jnp.where(tensor_at >= lax.axis_size("tensor") // 2, routes.half, 0)
-    place = (seq_at - offset) % blocks
-    where = jnp.stack([place % 2, place // routes.y % 2, place // routes.half]).astype(jnp.int32)
-
     given = gather_blocks(routes, jnp.concatenate((key_base, frozen_value), axis=1))
     down = jnp.concatenate((down_query, down_value), axis=1)
     part_t = lax.dot_general(down, hidden_in, (((0,), (1,)), ((), ())), preferred_element_type=F32)
@@ -316,35 +337,31 @@
     low_q_t = low_t[:rank]
     low_v = gather_low(routes, low_t[rank:])
 
-    attention, grad_up_q, back_q, back_v, grad_up_v = attention_call(
-        where,
+    attention, grad_up_q, back_q, back_v, back_v_sibling, grad_up_v = attention_call(
         frozen_query,
-        low_q_t.T,
         low_q_t,
         query_upper_factor,
         value_upper_factor,
+        grad_output,
         low_v,
-        grad_output,
         given,
     )
 
-    back_v = back_v.reshape(rank, 4, 2, rows)
-    mine = back_v[:, :, 0] + routes.core(back_v[:, :, 1])
-    mine = mine[:, 0::2] + routes.across_y(mine[:, 1::2])
-    mine = mine[:, 0] + routes.down(mine[:, 1])
-    back = sum_over_tensor(jnp.concatenate((back_q, mine), axis=0)).astype(BF16)
-    grad_down = dot(back, hidden_in, NN)
-
-    summed = sum_over_seq(
-        jnp.concatenate(
-            (grad_down[:rank], grad_down[rank:], grad_up_q, grad_up_v), axis=1
-        ).astype(BF16)
-    ).astype(F32)
-    grad_down_query = summed[:, :width_here].T
-    grad_down_value = summed[:, width_here : 2 * width_here].T
-    grad_up_query = summed[:, 2 * width_here : -kv_width]
-    grad_up_value = summed[:, -kv_width:]
-    return attention, grad_down_query, grad_up_query, grad_down_value, grad_up_value
+    grad_up = sum_over_seq(jnp.concatenate((grad_up_q, grad_up_v), axis=1)).astype(F32)
+    back_v = (back_v + routes.core(back_v_sibling)).reshape(rank, 4, rows)
+    back_v = back_v[:, 0::2] + routes.across_y(back_v[:, 1::2])
+    back_v = back_v[:, 0] + routes.down(back_v[:, 1])
+    back = sum_over_tensor(jnp.concatenate((back_q, back_v), axis=0)).astype(BF16)
+    grad_down = dot(back, hidden_in, NN).astype(BF16)
+    grad_down = sum_over_seq(jnp.concatenate((grad_down[:rank], grad_down[rank:]), axis=1))
+    grad_down = grad_down.astype(F32)
+    return (
+        attention,
+        grad_down[:, :width_here].T,
+        grad_up[:, :-kv_width],
+        grad_down[:, width_here:].T,
+        grad_up[:, -kv_width:],
+    )
 
 
 def solution(mesh):

time: 149 us -> 133 us (0.89)
  waiting for transfers between devices: 60.9 us -> 42.3 us
  starting transfers between devices: 41.2 us -> 46.2 us
  local copies, waits for them, and re-layouts: 7.19 us -> 5.01 us
    ppermute x5 -> x10, waiting for transfers between devices: 23 us -> 10.8 us  [swap(): lax.ppermute(block, 'seq', [(i, i ^ step) for i in range(lax.axis_size('s...]
    ppermute x5 -> x10, starting transfers between devices: 4.89 us -> 12.2 us  [swap(): lax.ppermute(block, 'seq', [(i, i ^ step) for i in range(lax.axis_size('s...]
    ppermute x15 -> x16, waiting for transfers between devices: 37.8 us -> 31.4 us  [send(): return lax.ppermute(block, AXES, route)]
    another operation x4 -> x0, other arithmetic: 2.53 us -> none
    reshape x2 -> x1, local copies, waits for them, and re-layouts: 1.68 us -> 0.03 us  [per_device(): back_v = (back_v + routes.core(back_v_sibling)).reshape(rank, 4, rows)]
    ppermute x15 -> x16, starting transfers between devices: 31 us -> 29.7 us  [send(): return lax.ppermute(block, AXES, route)]
  transfers between devices with their start and end apart: 22 -> 28, of which waited for: 12 -> 15; matrix products, arithmetic and copies ran while one was open for 4% -> 5% of each run, Pallas kernels for 0% -> 0%
where the time goes in v3:
time: 133 us
  starting transfers between devices  46.2 us (35%)
  waiting for transfers between devices  42.3 us (32%)
  Pallas kernels  30.9 us (23%)
  local copies, waits for them, and re-layouts  5.01 us (4%)
  other arithmetic  4.4 us (3%)
  matrix products  2.88 us (2%)
    ppermute x16, waiting for transfers between devices, send(): return lax.ppermute(block, AXES, route)  31.4 us
    pallas_call x1, Pallas kernels, attention_call(): pl.pallas_call(functools.partial(attention_body, rows, per_head, kv, stac...  30.9 us
    ppermute x16, starting transfers between devices, send(): return lax.ppermute(block, AXES, route)  29.7 us
    ppermute x10, starting transfers between devices, swap(): lax.ppermute(block, 'seq', [(i, i ^ step) for i in range(lax.axis_size('s...  12.2 us
    ppermute x10, waiting for transfers between devices, swap(): lax.ppermute(block, 'seq', [(i, i ^ step) for i in range(lax.axis_size('s...  10.8 us
    ppermute x2, starting transfers between devices, sum_over_tensor(): lax.ppermute(part, 'tensor', [(i, i ^ step) for i in range(size)])  4.3 us
  transfers between devices with their start and end apart: 28, of which 15 were waited for; matrix products, arithmetic and copies ran while one was open for 5% of the time, Pallas kernels for 0%

profile of v3, /device:TPU:0, one launch (start us, length us, event | category | flops | bytes accessed | tf_op | source)
XLA Modules:
  0.0 132.8 jit_solution(3014331732349902832)
XLA Ops:
  0.7 1.6 %copy-done = bf16[256,4096]{1,0:T(8,128)(2,1)S(1)} copy-done((bf16[256,4096]{1,0:T(8,128)(2,1)S(1)}, bf16[256,4096]{1,0:T(8,128)(2,1)}, u32[]{:S(2)}) %copy-start) | copy-done | bytes 2097176
  2.2 1.7 %fusion = f32[32,256]{1,0:T(8,128)S(1)} fusion(bf16[256,4096]{1,0:T(8,128)(2,1)S(1)} %copy-done, bf16[4096,16]{0,1:T(8,128)(2,1)} %param.15, bf16[4096,16]{0,1:T(8,128)(2,1)} %param.13), kind=kOutput, calls=%fused_computation.3 | convolution fusion | flops 67633152 | bytes 2392064 | tf_op jit(solution)/shard_map/dot_general | solution.py:335
  3.9 3.0 %collective-permute-start = (f32[32,256]{1,0:T(8,128)S(1)}, f32[32,256]{1,0:T(8,128)S(1)}, u32[]{:S(2)}, u32[]{:S(2)}) collective-permute-start(f32[32,256]{1,0:T(8,128)S(1)} %fusion), channel_id=1, source_target_pairs={{0,1},{1,0},{2,3},{3,2},{4,5},{5,4},{6,7},{7,6},{8,9},{9,8},{10,11... | collective-permute-start | bytes 98312 | tf_op jit(solution)/shard_map/ppermute | solution.py:279
  7.0 3.4 %collective-permute-start.6 = (bf16[256,1024]{1,0:T(8,128)(2,1)S(1)}, bf16[256,1024]{1,0:T(8,128)(2,1)S(1)}, u32[]{:S(2)}, u32[]{:S(2)}) collective-permute-start(bf16[256,1024]{1,0:T(8,128)(2,1)S(1)} %constant_dynamic-update-slice_fusion.refs_9_), channel_id=1, source_target_pairs={{0,4},{1,5},{2,6},{3,7},{4,0},{6,2},{8,12},{9,13},{10,14},{11,15},... | collective-permute-start | bytes 1572872 | tf_op jit(solution)/shard_map/ppermute | solution.py:230
  10.5 3.5 %collective-permute-start.8 = (bf16[256,1024]{1,0:T(8,128)(2,1)S(1)}, bf16[256,1024]{1,0:T(8,128)(2,1)S(1)}, u32[]{:S(2)}, u32[]{:S(2)}) collective-permute-start(bf16[256,1024]{1,0:T(8,128)(2,1)S(1)} %constant_dynamic-update-slice_fusion.refs_9_), channel_id=1, source_target_pairs={{0,8},{2,10},{4,12},{6,14},{9,17},{11,19},{13,21},{15,23},{16,24},... | collective-permute-start | bytes 1572872 | tf_op jit(solution)/shard_map/ppermute | solution.py:230
  17.1 2.7 %collective-permute-start.4 = (bf16[16,512]{1,0:T(8,128)(2,1)S(1)}, bf16[16,512]{1,0:T(8,128)(2,1)S(1)}, u32[]{:S(2)}, u32[]{:S(2)}) collective-permute-start(bf16[16,512]{1,0:T(8,128)(2,1)S(1)} %pad_maximum_fusion.2.refs_5_), channel_id=1, source_target_pairs={{0,12},{2,14},{4,8},{6,10},{9,21},{11,23},{13,17},{15,19},{16,28},... | collective-permute-start | bytes 49160 | tf_op jit(solution)/shard_map/ppermute | solution.py:230
  19.8 2.6 %collective-permute-done.6.refs_11_ = bf16[256,1024]{1,0:T(8,128)(2,1)S(1)} collective-permute-done((bf16[256,1024]{1,0:T(8,128)(2,1)S(1)}, bf16[256,1024]{1,0:T(8,128)(2,1)S(1)}, u32[]{:S(2)}, u32[]{:S(2)}) %collective-permute-start.6) | collective-permute-done | bytes 524320 | tf_op jit(solution)/shard_map/ppermute | solution.py:230
  22.5 2.4 %collective-permute-done.8.refs_13_ = bf16[256,1024]{1,0:T(8,128)(2,1)S(1)} collective-permute-done((bf16[256,1024]{1,0:T(8,128)(2,1)S(1)}, bf16[256,1024]{1,0:T(8,128)(2,1)S(1)}, u32[]{:S(2)}, u32[]{:S(2)}) %collective-permute-start.8) | collective-permute-done | bytes 524320 | tf_op jit(solution)/shard_map/ppermute | solution.py:230
  24.9 4.4 %collective-permute-start.10 = (bf16[128,1024]{1,0:T(8,128)(2,1)S(1)}, bf16[128,1024]{1,0:T(8,128)(2,1)S(1)}, u32[]{:S(2)}, u32[]{:S(2)}) collective-permute-start(bf16[128,1024]{1,0:T(8,128)(2,1)S(1)} %slice.66), channel_id=1, source_target_pairs={{0,8},{2,10},{4,12},{6,14},{9,17},{11,19},{13,21},{15,23},{16,24},... | collective-permute-start | bytes 786440 | tf_op jit(solution)/shard_map/ppermute | solution.py:230
  30.7 2.5 %collective-permute-done.10.refs_15_ = bf16[128,1024]{1,0:T(8,128)(2,1)S(1)} collective-permute-done((bf16[128,1024]{1,0:T(8,128)(2,1)S(1)}, bf16[128,1024]{1,0:T(8,128)(2,1)S(1)}, u32[]{:S(2)}, u32[]{:S(2)}) %collective-permute-start.10) | collective-permute-done | bytes 262176 | tf_op jit(solution)/shard_map/ppermute | solution.py:230
  36.2 30.9 %shard_map.128 = (bf16[256,4096]{1,0:T(8,128)(2,1)}, bf16[16,4096]{1,0:T(8,128)(2,1)}, f32[16,256]{1,0:T(8,128)}, f32[16,1024]{1,0:T(8,128)}, f32[16,1024]{1,0:T(8,128)}, /*index=5*/bf16[16,512]{1,0:T(8,128)(2,1)}) custom-call(bf16[256,4096]{1,0:T(8,128)(2,1)} %refs_0_.1, bf16[16,256]{1,0:T(8,128)(2,1)} %get-tuple-element.24.refs_1_, ...), custom_call_target="tpu_custom_call" | custom-call | flops 21474836480 | bytes 16777216 | tf_op jit(solution)/shard_map/pallas_call | solution.py:182
  67.3 1.3 collective-permute-done.14
  69.6 11.1 %collective-permute-start.15 = (f32[16,2,256]{2,0,1:T(8,128)S(1)}, f32[16,2,256]{2,0,1:T(8,128)S(1)}, u32[]{:S(2)}, u32[]{:S(2)}) collective-permute-start(f32[16,2,256]{2,0,1:T(8,128)S(1)} %copy.17), channel_id=1, source_target_pairs={{0,4},{1,5},{2,6},{3,7},{4,0},{5,1},{6,2},{7,3},{8,12},{9,13},{10,... | collective-permute-start | bytes 98312 | tf_op jit(solution)/shard_map/ppermute | solution.py:230
  80.8 1.8 %collective-permute-done.15 = f32[16,2,256]{2,0,1:T(8,128)S(1)} collective-permute-done((f32[16,2,256]{2,0,1:T(8,128)S(1)}, f32[16,2,256]{2,0,1:T(8,128)S(1)}, u32[]{:S(2)}, u32[]{:S(2)}) %collective-permute-start.15) | collective-permute-done | bytes 32800 | tf_op jit(solution)/shard_map/ppermute | solution.py:230
  84.9 18.1 %collective-permute-done.16 = f32[16,256]{1,0:T(8,128)S(1)} collective-permute-done((f32[16,256]{1,0:T(8,128)S(1)}, f32[16,256]{1,0:T(8,128)S(1)}, u32[]{:S(2)}, u32[]{:S(2)}) %collective-permute-start.16) | collective-permute-done | bytes 16416 | tf_op jit(solution)/shard_map/ppermute | solution.py:230
  106.0 1.5 %collective-permute-start.24 = (bf16[16,2304]{1,0:T(8,128)(2,1)S(1)}, bf16[16,2304]{1,0:T(8,128)(2,1)S(1)}, u32[]{:S(2)}, u32[]{:S(2)}) collective-permute-start(bf16[16,2304]{1,0:T(8,128)(2,1)S(1)} %add_convert_fusion.7), channel_id=1, source_target_pairs={{0,4},{2,6},{4,0},{6,2},{8,12},{10,14},{12,8},{14,10},{16,20},{18,... | collective-permute-start | bytes 221192 | tf_op jit(solution)/shard_map/ppermute | solution.py:285
  108.9 1.5 %collective-permute-done.24 = bf16[16,2304]{1,0:T(8,128)(2,1)S(1)} collective-permute-done((bf16[16,2304]{1,0:T(8,128)(2,1)S(1)}, bf16[16,2304]{1,0:T(8,128)(2,1)S(1)}, u32[]{:S(2)}, u32[]{:S(2)}) %collective-permute-start.24) | collective-permute-done | bytes 73760 | tf_op jit(solution)/shard_map/ppermute | solution.py:285
  111.3 2.0 %collective-permute-start.19 = (bf16[16,4096]{1,0:T(8,128)(2,1)S(1)}, bf16[16,4096]{1,0:T(8,128)(2,1)S(1)}, u32[]{:S(2)}, u32[]{:S(2)}) collective-permute-start(bf16[16,4096]{1,0:T(8,128)(2,1)S(1)} %add_convert_fusion.3), channel_id=1, source_target_pairs={{0,4},{2,6},{4,0},{6,2},{8,12},{10,14},{12,8},{14,10},{16,20},{18,... | collective-permute-start | bytes 393224 | tf_op jit(solution)/shard_map/ppermute | solution.py:285
  113.4 1.4 %collective-permute-done.25 = bf16[16,2304]{1,0:T(8,128)(2,1)S(1)} collective-permute-done((bf16[16,2304]{1,0:T(8,128)(2,1)S(1)}, bf16[16,2304]{1,0:T(8,128)(2,1)S(1)}, u32[]{:S(2)}, u32[]{:S(2)}) %collective-permute-start.25) | collective-permute-done | bytes 73760 | tf_op jit(solution)/shard_map/ppermute | solution.py:285
  114.8 2.7 %collective-permute-start.26 = (bf16[16,2304]{1,0:T(8,128)(2,1)S(1)}, bf16[16,2304]{1,0:T(8,128)(2,1)S(1)}, u32[]{:S(2)}, u32[]{:S(2)}) collective-permute-start(bf16[16,2304]{1,0:T(8,128)(2,1)S(1)} %add_convert_fusion.5), channel_id=1, source_target_pairs={{0,16},{2,18},{4,20},{6,22},{8,24},{10,26},{12,28},{14,30},{16,0},... | collective-permute-start | bytes 221192 | tf_op jit(solution)/shard_map/ppermute | solution.py:285
  117.6 2.1 %collective-permute-start.20 = (bf16[16,4096]{1,0:T(8,128)(2,1)S(1)}, bf16[16,4096]{1,0:T(8,128)(2,1)S(1)}, u32[]{:S(2)}, u32[]{:S(2)}) collective-permute-start(bf16[16,4096]{1,0:T(8,128)(2,1)S(1)} %add_convert_fusion.2), channel_id=1, source_target_pairs={{0,8},{2,10},{4,12},{6,14},{8,0},{10,2},{12,4},{14,6},{16,24},{18,... | collective-permute-start | bytes 393224 | tf_op jit(solution)/shard_map/ppermute | solution.py:285
  120.3 2.3 %collective-permute-done.20 = bf16[16,4096]{1,0:T(8,128)(2,1)S(1)} collective-permute-done((bf16[16,4096]{1,0:T(8,128)(2,1)S(1)}, bf16[16,4096]{1,0:T(8,128)(2,1)S(1)}, u32[]{:S(2)}, u32[]{:S(2)}) %collective-permute-start.20) | collective-permute-done | bytes 131104 | tf_op jit(solution)/shard_map/ppermute | solution.py:285
  122.7 2.7 %collective-permute-start.21 = (bf16[16,4096]{1,0:T(8,128)(2,1)S(1)}, bf16[16,4096]{1,0:T(8,128)(2,1)S(1)}, u32[]{:S(2)}, u32[]{:S(2)}) collective-permute-start(bf16[16,4096]{1,0:T(8,128)(2,1)S(1)} %add_convert_fusion.1), channel_id=1, source_target_pairs={{0,16},{2,18},{4,20},{6,22},{8,24},{10,26},{12,28},{14,30},{16,0},... | collective-permute-start | bytes 393224 | tf_op jit(solution)/shard_map/ppermute | solution.py:285
  125.4 5.0 %collective-permute-done.21 = bf16[16,4096]{1,0:T(8,128)(2,1)S(1)} collective-permute-done((bf16[16,4096]{1,0:T(8,128)(2,1)S(1)}, bf16[16,4096]{1,0:T(8,128)(2,1)S(1)}, u32[]{:S(2)}, u32[]{:S(2)}) %collective-permute-start.21) | collective-permute-done | bytes 131104 | tf_op jit(solution)/shard_map/ppermute | solution.py:285
  (102 shorter events, 19.3 us)
Async XLA Ops:
  3.9 10.1 %collective-permute-start = (f32[32,256]{1,0:T(8,128)S(1)}, f32[32,256]{1,0:T(8,128)S(1)}, u32[]{:S(2)}, u32[]{:S(2)}) collective-permute-start(f32[32,256]{1,0:T(8,128)S(1)} %fusion), channel_id=1, source_target_pairs={{0,1},{1,0},{2,3},{3,2},{4,5},{5,4},{6,7},{7,6},{8,9},{9,8},{10,11... | collective-permute-start | bytes 98312 | tf_op jit(solution)/shard_map/ppermute | solution.py:279
  7.0 15.5 %collective-permute-start.6 = (bf16[256,1024]{1,0:T(8,128)(2,1)S(1)}, bf16[256,1024]{1,0:T(8,128)(2,1)S(1)}, u32[]{:S(2)}, u32[]{:S(2)}) collective-permute-start(bf16[256,1024]{1,0:T(8,128)(2,1)S(1)} %constant_dynamic-update-slice_fusion.refs_9_), channel_id=1, source_target_pairs={{0,4},{1,5},{2,6},{3,7},{4,0},{6,2},{8,12},{9,13},{10,14},{11,15},... | collective-permute-start | bytes 1572872 | tf_op jit(solution)/shard_map/ppermute | solution.py:230
  10.5 14.5 %collective-permute-start.8 = (bf16[256,1024]{1,0:T(8,128)(2,1)S(1)}, bf16[256,1024]{1,0:T(8,128)(2,1)S(1)}, u32[]{:S(2)}, u32[]{:S(2)}) collective-permute-start(bf16[256,1024]{1,0:T(8,128)(2,1)S(1)} %constant_dynamic-update-slice_fusion.refs_9_), channel_id=1, source_target_pairs={{0,8},{2,10},{4,12},{6,14},{9,17},{11,19},{13,21},{15,23},{16,24},... | collective-permute-start | bytes 1572872 | tf_op jit(solution)/shard_map/ppermute | solution.py:230
  15.8 13.6 %collective-permute-start.2 = (bf16[16,512]{1,0:T(8,128)(2,1)S(1)}, bf16[16,512]{1,0:T(8,128)(2,1)S(1)}, u32[]{:S(2)}, u32[]{:S(2)}) collective-permute-start(bf16[16,512]{1,0:T(8,128)(2,1)S(1)} %pad_maximum_fusion.2.refs_5_), channel_id=1, source_target_pairs={{0,4},{1,5},{2,6},{3,7},{4,0},{5,1},{6,2},{7,3},{8,12},{9,13},{10,... | collective-permute-start | bytes 49160 | tf_op jit(solution)/shard_map/ppermute | solution.py:230
  15.8 14.3 %collective-permute-start.3 = (bf16[16,512]{1,0:T(8,128)(2,1)S(1)}, bf16[16,512]{1,0:T(8,128)(2,1)S(1)}, u32[]{:S(2)}, u32[]{:S(2)}) collective-permute-start(bf16[16,512]{1,0:T(8,128)(2,1)S(1)} %pad_maximum_fusion.2.refs_5_), channel_id=1, source_target_pairs={{0,8},{2,10},{4,12},{6,14},{9,17},{11,19},{13,21},{15,23},{16,24},... | collective-permute-start | bytes 49160 | tf_op jit(solution)/shard_map/ppermute | solution.py:230
  17.1 13.1 %collective-permute-start.4 = (bf16[16,512]{1,0:T(8,128)(2,1)S(1)}, bf16[16,512]{1,0:T(8,128)(2,1)S(1)}, u32[]{:S(2)}, u32[]{:S(2)}) collective-permute-start(bf16[16,512]{1,0:T(8,128)(2,1)S(1)} %pad_maximum_fusion.2.refs_5_), channel_id=1, source_target_pairs={{0,12},{2,14},{4,8},{6,10},{9,21},{11,23},{13,17},{15,19},{16,28},... | collective-permute-start | bytes 49160 | tf_op jit(solution)/shard_map/ppermute | solution.py:230
  22.5 11.2 %collective-permute-start.5 = (bf16[256,1024]{1,0:T(8,128)(2,1)S(1)}, bf16[256,1024]{1,0:T(8,128)(2,1)S(1)}, u32[]{:S(2)}, u32[]{:S(2)}) collective-permute-start(bf16[256,1024]{1,0:T(8,128)(2,1)S(1)} %constant_dynamic-update-slice_fusion.refs_9_), channel_id=1, source_target_pairs={{0,2},{1,3},{2,0},{3,1},{4,6},{5,7},{6,4},{7,5},{8,10},{9,11},{10,... | collective-permute-start | bytes 1572872 | tf_op jit(solution)/shard_map/ppermute | solution.py:230
  24.9 8.3 %collective-permute-start.10 = (bf16[128,1024]{1,0:T(8,128)(2,1)S(1)}, bf16[128,1024]{1,0:T(8,128)(2,1)S(1)}, u32[]{:S(2)}, u32[]{:S(2)}) collective-permute-start(bf16[128,1024]{1,0:T(8,128)(2,1)S(1)} %slice.66), channel_id=1, source_target_pairs={{0,8},{2,10},{4,12},{6,14},{9,17},{11,19},{13,21},{15,23},{16,24},... | collective-permute-start | bytes 786440 | tf_op jit(solution)/shard_map/ppermute | solution.py:230
  29.4 3.8 %collective-permute-start.11 = (bf16[128,1024]{1,0:T(8,128)(2,1)S(1)}, bf16[128,1024]{1,0:T(8,128)(2,1)S(1)}, u32[]{:S(2)}, u32[]{:S(2)}) collective-permute-start(bf16[128,1024]{1,0:T(8,128)(2,1)S(1)} %slice.67), channel_id=1, source_target_pairs={{1,5},{3,7},{5,1},{7,3},{8,12},{10,14},{12,8},{14,10},{17,21},{19,... | collective-permute-start | bytes 786440 | tf_op jit(solution)/shard_map/ppermute | solution.py:230
  30.1 5.0 %collective-permute-start.7 = (bf16[256,1024]{1,0:T(8,128)(2,1)S(1)}, bf16[256,1024]{1,0:T(8,128)(2,1)S(1)}, u32[]{:S(2)}, u32[]{:S(2)}) collective-permute-start(bf16[256,1024]{1,0:T(8,128)(2,1)S(1)} %collective-permute-done.6.refs_11_), channel_id=1, source_target_pairs={{0,2},{1,3},{2,0},{3,1},{4,6},{5,7},{6,4},{7,5},{8,10},{9,11},{10,... | collective-permute-start | bytes 1572872 | tf_op jit(solution)/shard_map/ppermute | solution.py:230
  30.2 4.9 %collective-permute-start.9 = (bf16[256,1024]{1,0:T(8,128)(2,1)S(1)}, bf16[256,1024]{1,0:T(8,128)(2,1)S(1)}, u32[]{:S(2)}, u32[]{:S(2)}) collective-permute-start(bf16[256,1024]{1,0:T(8,128)(2,1)S(1)} %collective-permute-done.8.refs_13_), channel_id=1, source_target_pairs={{0,2},{1,3},{2,0},{3,1},{4,6},{5,7},{6,4},{7,5},{8,10},{9,11},{10,... | collective-permute-start | bytes 1572872 | tf_op jit(solution)/shard_map/ppermute | solution.py:230
  33.2 1.9 %collective-permute-start.13 = (bf16[128,1024]{1,0:T(8,128)(2,1)S(1)}, bf16[128,1024]{1,0:T(8,128)(2,1)S(1)}, u32[]{:S(2)}, u32[]{:S(2)}) collective-permute-start(bf16[128,1024]{1,0:T(8,128)(2,1)S(1)} %collective-permute-done.11.refs_16_), channel_id=1, source_target_pairs={{0,2},{1,3},{2,0},{3,1},{4,6},{5,7},{6,4},{7,5},{8,10},{9,11},{10,... | collective-permute-start | bytes 786440 | tf_op jit(solution)/shard_map/ppermute | solution.py:230
  69.6 13.0 %collective-permute-start.15 = (f32[16,2,256]{2,0,1:T(8,128)S(1)}, f32[16,2,256]{2,0,1:T(8,128)S(1)}, u32[]{:S(2)}, u32[]{:S(2)}) collective-permute-start(f32[16,2,256]{2,0,1:T(8,128)S(1)} %copy.17), channel_id=1, source_target_pairs={{0,4},{1,5},{2,6},{3,7},{4,0},{5,1},{6,2},{7,3},{8,12},{9,13},{10,... | collective-permute-start | bytes 98312 | tf_op jit(solution)/shard_map/ppermute | solution.py:230
  82.6 20.4 %collective-permute-start.16 = (f32[16,256]{1,0:T(8,128)S(1)}, f32[16,256]{1,0:T(8,128)S(1)}, u32[]{:S(2)}, u32[]{:S(2)}) collective-permute-start(f32[16,256]{1,0:T(8,128)S(1)} %slice_bitcast_fusion.2), channel_id=1, source_target_pairs={{1,25},{3,27},{5,29},{7,31},{8,0},{10,2},{12,4},{14,6},{17,9},{19,... | collective-permute-start | bytes 49160 | tf_op jit(solution)/shard_map/ppermute | solution.py:230
  84.8 20.2 %collective-permute-start.23 = (bf16[16,2304]{1,0:T(8,128)(2,1)S(1)}, bf16[16,2304]{1,0:T(8,128)(2,1)S(1)}, u32[]{:S(2)}, u32[]{:S(2)}) collective-permute-start(bf16[16,2304]{1,0:T(8,128)(2,1)S(1)} %broadcast_select_fusion.5), channel_id=1, source_target_pairs={{0,2},{2,0},{4,6},{6,4},{8,10},{10,8},{12,14},{14,12},{16,18},{18,... | collective-permute-start | bytes 221192 | tf_op jit(solution)/shard_map/ppermute | solution.py:285
  103.7 3.9 %collective-permute-start.17 = (f32[32,256]{1,0:T(8,128)S(1)}, f32[32,256]{1,0:T(8,128)S(1)}, u32[]{:S(2)}, u32[]{:S(2)}) collective-permute-start(f32[32,256]{1,0:T(8,128)S(1)} %pad_maximum_fusion.1), channel_id=1, source_target_pairs={{0,1},{1,0},{2,3},{3,2},{4,5},{5,4},{6,7},{7,6},{8,9},{9,8},{10,11... | collective-permute-start | bytes 98312 | tf_op jit(solution)/shard_map/ppermute | solution.py:279
  106.0 4.4 %collective-permute-start.24 = (bf16[16,2304]{1,0:T(8,128)(2,1)S(1)}, bf16[16,2304]{1,0:T(8,128)(2,1)S(1)}, u32[]{:S(2)}, u32[]{:S(2)}) collective-permute-start(bf16[16,2304]{1,0:T(8,128)(2,1)S(1)} %add_convert_fusion.7), channel_id=1, source_target_pairs={{0,4},{2,6},{4,0},{6,2},{8,12},{10,14},{12,8},{14,10},{16,20},{18,... | collective-permute-start | bytes 221192 | tf_op jit(solution)/shard_map/ppermute | solution.py:285
  108.8 2.5 %collective-permute-start.18 = (bf16[16,4096]{1,0:T(8,128)(2,1)S(1)}, bf16[16,4096]{1,0:T(8,128)(2,1)S(1)}, u32[]{:S(2)}, u32[]{:S(2)}) collective-permute-start(bf16[16,4096]{1,0:T(8,128)(2,1)S(1)} %broadcast_select_fusion.2), channel_id=1, source_target_pairs={{0,2},{2,0},{4,6},{6,4},{8,10},{10,8},{12,14},{14,12},{16,18},{18,... | collective-permute-start | bytes 393224 | tf_op jit(solution)/shard_map/ppermute | solution.py:285
  110.4 4.4 %collective-permute-start.25 = (bf16[16,2304]{1,0:T(8,128)(2,1)S(1)}, bf16[16,2304]{1,0:T(8,128)(2,1)S(1)}, u32[]{:S(2)}, u32[]{:S(2)}) collective-permute-start(bf16[16,2304]{1,0:T(8,128)(2,1)S(1)} %add_convert_fusion.6), channel_id=1, source_target_pairs={{0,8},{2,10},{4,12},{6,14},{8,0},{10,2},{12,4},{14,6},{16,24},{18,... | collective-permute-start | bytes 221192 | tf_op jit(solution)/shard_map/ppermute | solution.py:285
  111.3 6.2 %collective-permute-start.19 = (bf16[16,4096]{1,0:T(8,128)(2,1)S(1)}, bf16[16,4096]{1,0:T(8,128)(2,1)S(1)}, u32[]{:S(2)}, u32[]{:S(2)}) collective-permute-start(bf16[16,4096]{1,0:T(8,128)(2,1)S(1)} %add_convert_fusion.3), channel_id=1, source_target_pairs={{0,4},{2,6},{4,0},{6,2},{8,12},{10,14},{12,8},{14,10},{16,20},{18,... | collective-permute-start | bytes 393224 | tf_op jit(solution)/shard_map/ppermute | solution.py:285
  114.8 5.3 %collective-permute-start.26 = (bf16[16,2304]{1,0:T(8,128)(2,1)S(1)}, bf16[16,2304]{1,0:T(8,128)(2,1)S(1)}, u32[]{:S(2)}, u32[]{:S(2)}) collective-permute-start(bf16[16,2304]{1,0:T(8,128)(2,1)S(1)} %add_convert_fusion.5), channel_id=1, source_target_pairs={{0,16},{2,18},{4,20},{6,22},{8,24},{10,26},{12,28},{14,30},{16,0},... | collective-permute-start | bytes 221192 | tf_op jit(solution)/shard_map/ppermute | solution.py:285
  117.6 5.0 %collective-permute-start.20 = (bf16[16,4096]{1,0:T(8,128)(2,1)S(1)}, bf16[16,4096]{1,0:T(8,128)(2,1)S(1)}, u32[]{:S(2)}, u32[]{:S(2)}) collective-permute-start(bf16[16,4096]{1,0:T(8,128)(2,1)S(1)} %add_convert_fusion.2), channel_id=1, source_target_pairs={{0,8},{2,10},{4,12},{6,14},{8,0},{10,2},{12,4},{14,6},{16,24},{18,... | collective-permute-start | bytes 393224 | tf_op jit(solution)/shard_map/ppermute | solution.py:285
  120.2 5.2 %collective-permute-start.27 = (bf16[16,2304]{1,0:T(8,128)(2,1)S(1)}, bf16[16,2304]{1,0:T(8,128)(2,1)S(1)}, u32[]{:S(2)}, u32[]{:S(2)}) collective-permute-start(bf16[16,2304]{1,0:T(8,128)(2,1)S(1)} %add_convert_fusion.4), channel_id=1, source_target_pairs={{0,2},{2,0},{4,6},{6,4},{8,10},{10,8},{12,14},{14,12},{16,18},{18,... | collective-permute-start | bytes 221192 | tf_op jit(solution)/shard_map/ppermute | solution.py:285
  122.7 7.8 %collective-permute-start.21 = (bf16[16,4096]{1,0:T(8,128)(2,1)S(1)}, bf16[16,4096]{1,0:T(8,128)(2,1)S(1)}, u32[]{:S(2)}, u32[]{:S(2)}) collective-permute-start(bf16[16,4096]{1,0:T(8,128)(2,1)S(1)} %add_convert_fusion.1), channel_id=1, source_target_pairs={{0,16},{2,18},{4,20},{6,22},{8,24},{10,26},{12,28},{14,30},{16,0},... | collective-permute-start | bytes 393224 | tf_op jit(solution)/shard_map/ppermute | solution.py:285
  (21 other events, 115.0 us)

commit v4 on v3

--- a/solution.py
+++ b/solution.py
@@ -12,6 +12,7 @@
 ADAPTER_SCALE = 0.5
 LOG2E = 1.4426950408889634
 MASKED = -1e30
+VMEM_LIMIT = 40
 
 F32 = jnp.float32
 BF16 = jnp.bfloat16
@@ -90,7 +91,7 @@
                 total = term if total is None else total + term
             grad_up_v[:, cols] = (ADAPTER_SCALE * total).astype(BF16)
 
-    def attend(length, pipelined):
+    def attend(length):
         def wide(i):
             return pl.ds(pl.multiple_of(i * (stacked * HD), stacked * HD), stacked * HD)
 
@@ -100,24 +101,25 @@
         def kv_cols(i):
             return pl.ds(pl.multiple_of((i // steps_per_kv) * HD, HD), HD)
 
-        def score(i, slot):
+        def score(i):
             query = frozen[:, wide(i)].astype(F32) + ADAPTER_SCALE * dot(low_q[...], up_q[:, wide(i)], NN)
             query = query.astype(BF16)
             query = jnp.concatenate([query[:, a * HD : (a + 1) * HD] for a in range(stacked)], axis=0)
             s = dot(keys[:length, kv_cols(i)], query, NT)
             own = jnp.where(key_at <= query_at, s[:rows], MASKED)
             sibling = jnp.where(core > 0, s[rows : 2 * rows], MASKED)
-            scores[slot, :rows, :] = own
-            scores[slot, rows : 2 * rows, :] = sibling
+            scores[:rows, :] = own
+            scores[rows : 2 * rows, :] = sibling
             top = jnp.max(jnp.maximum(own, sibling), axis=0, keepdims=True)
             if length > 2 * rows:
                 rest = s[2 * rows :]
-                scores[slot, 2 * rows : length, :] = rest
+                scores[2 * rows : length, :] = rest
                 top = jnp.maximum(top, jnp.max(rest, axis=0, keepdims=True))
             return top * to_log2
 
-        def follow(i, slot, top):
-            probs[:length, :] = jnp.exp2(scores[slot, :length, :] * to_log2 - top).astype(BF16)
+        def one_step(i, top):
+            probs[:length, :] = jnp.exp2(scores[:length, :] * to_log2 - top).astype(BF16)
+            later = score(jnp.minimum(i + 1, steps - 1))
             attended = dot(values_t[i // steps_per_kv, :, :length], probs[:length, :], NN)
             inverse = 1.0 / attended[HD : HD + 1, :]
             attended = (attended[:HD] * inverse).astype(BF16)
@@ -140,24 +142,9 @@
                 back = term if back is None else back + term
             back_q[...] += ADAPTER_SCALE * back
 
-        if pipelined:
-
-            def two_steps(t, top):
-                for u in range(2):
-                    i = 2 * t + u
-                    later = score(jnp.minimum(i + 1, steps - 1), 1 - u)
-                    follow(i, u, top)
-                    top = later
-                return top
-
-            lax.fori_loop(0, steps // 2, two_steps, score(0, 0))
-        else:
-
-            def one_step(i, carry):
-                follow(i, 0, score(i, 0))
-                return carry
-
-            lax.fori_loop(0, steps, one_step, 0)
+            return later
+
+        lax.fori_loop(0, steps, one_step, score(0))
 
     for y in (0, 1):
         for z in (0, 1):
@@ -166,7 +153,7 @@
             def _():
                 blocks = [0, 1] + [2, 3] * y + [4, 5, 6, 7] * z
                 prepare(blocks)
-                attend(len(blocks) * rows, len(blocks) == 8 and steps % 2 == 0)
+                attend(len(blocks) * rows)
                 finish(blocks)
 
 
@@ -185,7 +172,7 @@
         out_specs=[vmem] * 6,
         scratch_shapes=[
             pltpu.VMEM((rows, rank), BF16),
-            pltpu.VMEM((2, reach, stacked * rows), F32),
+            pltpu.VMEM((reach, stacked * rows), F32),
             pltpu.VMEM((reach, stacked * rows), BF16),
             pltpu.VMEM((reach, stacked * rows), BF16),
             pltpu.VMEM((reach, kv * HD), BF16),
@@ -202,7 +189,7 @@
             jax.ShapeDtypeStruct((rank, reach // 2), F32),
             jax.ShapeDtypeStruct((rank, kv * HD), BF16),
         ],
-        compiler_params=pltpu.CompilerParams(vmem_limit_bytes=56 * 2**20),
+        compiler_params=pltpu.CompilerParams(vmem_limit_bytes=VMEM_LIMIT * 2**20),
         cost_estimate=pl.CostEstimate(
             flops=10 * pairs * HD, bytes_accessed=16 * rows * width, transcendentals=pairs
         ),

time: 133 us -> 126 us (0.947)
  Pallas kernels: 30.9 us -> 22.3 us
  waiting for transfers between devices: 42.3 us -> 48.6 us
  other arithmetic: 4.4 us -> 1.04 us
    pallas_call x1, Pallas kernels: 30.9 us -> 22.3 us  [attention_call(): pl.pallas_call(functools.partial(attention_body, rows, per_head, kv, stac...]
    ppermute x16, waiting for transfers between devices: 31.4 us -> 38 us  [send(): return lax.ppermute(block, AXES, route)]
  transfers between devices with their start and end apart: 28 -> 28, of which waited for: 15 -> 15; matrix products, arithmetic and copies ran while one was open for 5% -> 3% of each run, Pallas kernels for 0% -> 0%
where the time goes in v4:
time: 126 us; the launch traced here: 125 us
  waiting for transfers between devices  48.6 us (39%)
  starting transfers between devices  45.7 us (36%)
  Pallas kernels  22.3 us (18%)
  local copies, waits for them, and re-layouts  4.4 us (3%)
  matrix products  2.32 us (2%)
    ppermute x16, waiting for transfers between devices, send(): return lax.ppermute(block, AXES, route)  38 us
    ppermute x16, starting transfers between devices, send(): return lax.ppermute(block, AXES, route)  28.5 us
    pallas_call x1, Pallas kernels, attention_call(): pl.pallas_call(functools.partial(attention_body, rows, per_head, kv, stac...  22.3 us
    ppermute x10, starting transfers between devices, swap(): lax.ppermute(block, 'seq', [(i, i ^ step) for i in range(lax.axis_size('s...  13.3 us
    ppermute x10, waiting for transfers between devices, swap(): lax.ppermute(block, 'seq', [(i, i ^ step) for i in range(lax.axis_size('s...  9.62 us
    ppermute x2, starting transfers between devices, sum_over_tensor(): lax.ppermute(part, 'tensor', [(i, i ^ step) for i in range(size)])  3.89 us
  transfers between devices with their start and end apart: 28, of which 15 were waited for; matrix products, arithmetic and copies ran while one was open for 3% of the time, Pallas kernels for 0%

profile of v4, /device:TPU:0, one launch (start us, length us, event | category | flops | bytes accessed | tf_op | source)
XLA Modules:
  0.0 125.4 jit_solution(17151804923284721928)
XLA Ops:
  0.7 1.5 %copy-done = bf16[256,4096]{1,0:T(8,128)(2,1)S(1)} copy-done((bf16[256,4096]{1,0:T(8,128)(2,1)S(1)}, bf16[256,4096]{1,0:T(8,128)(2,1)}, u32[]{:S(2)}) %copy-start) | copy-done | bytes 2097176
  2.2 1.8 %fusion = f32[32,256]{1,0:T(8,128)S(1)} fusion(bf16[256,4096]{1,0:T(8,128)(2,1)S(1)} %copy-done, bf16[4096,16]{0,1:T(8,128)(2,1)} %param.15, bf16[4096,16]{0,1:T(8,128)(2,1)} %param.13), kind=kOutput, calls=%fused_computation.3 | convolution fusion | flops 67633152 | bytes 2392064 | tf_op jit(solution)/shard_map/dot_general | solution.py:322
  4.1 3.0 %collective-permute-start = (f32[32,256]{1,0:T(8,128)S(1)}, f32[32,256]{1,0:T(8,128)S(1)}, u32[]{:S(2)}, u32[]{:S(2)}) collective-permute-start(f32[32,256]{1,0:T(8,128)S(1)} %fusion), channel_id=1, source_target_pairs={{0,1},{1,0},{2,3},{3,2},{4,5},{5,4},{6,7},{7,6},{8,9},{9,8},{10,11... | collective-permute-start | bytes 98312 | tf_op jit(solution)/shard_map/ppermute | solution.py:266
  8.1 3.4 %collective-permute-start.6 = (bf16[256,1024]{1,0:T(8,128)(2,1)S(1)}, bf16[256,1024]{1,0:T(8,128)(2,1)S(1)}, u32[]{:S(2)}, u32[]{:S(2)}) collective-permute-start(bf16[256,1024]{1,0:T(8,128)(2,1)S(1)} %constant_dynamic-update-slice_fusion.refs_9_), channel_id=1, source_target_pairs={{0,4},{1,5},{2,6},{3,7},{4,0},{6,2},{8,12},{9,13},{10,14},{11,15},... | collective-permute-start | bytes 1572872 | tf_op jit(solution)/shard_map/ppermute | solution.py:217
  11.5 3.5 %collective-permute-start.8 = (bf16[256,1024]{1,0:T(8,128)(2,1)S(1)}, bf16[256,1024]{1,0:T(8,128)(2,1)S(1)}, u32[]{:S(2)}, u32[]{:S(2)}) collective-permute-start(bf16[256,1024]{1,0:T(8,128)(2,1)S(1)} %constant_dynamic-update-slice_fusion.refs_9_), channel_id=1, source_target_pairs={{0,8},{2,10},{4,12},{6,14},{9,17},{11,19},{13,21},{15,23},{16,24},... | collective-permute-start | bytes 1572872 | tf_op jit(solution)/shard_map/ppermute | solution.py:217
  16.4 1.3 %collective-permute-start.3 = (bf16[16,512]{1,0:T(8,128)(2,1)S(1)}, bf16[16,512]{1,0:T(8,128)(2,1)S(1)}, u32[]{:S(2)}, u32[]{:S(2)}) collective-permute-start(bf16[16,512]{1,0:T(8,128)(2,1)S(1)} %pad_maximum_fusion.2.refs_5_), channel_id=1, source_target_pairs={{0,8},{2,10},{4,12},{6,14},{9,17},{11,19},{13,21},{15,23},{16,24},... | collective-permute-start | bytes 49160 | tf_op jit(solution)/shard_map/ppermute | solution.py:217
  17.7 2.7 %collective-permute-start.4 = (bf16[16,512]{1,0:T(8,128)(2,1)S(1)}, bf16[16,512]{1,0:T(8,128)(2,1)S(1)}, u32[]{:S(2)}, u32[]{:S(2)}) collective-permute-start(bf16[16,512]{1,0:T(8,128)(2,1)S(1)} %pad_maximum_fusion.2.refs_5_), channel_id=1, source_target_pairs={{0,12},{2,14},{4,8},{6,10},{9,21},{11,23},{13,17},{15,19},{16,28},... | collective-permute-start | bytes 49160 | tf_op jit(solution)/shard_map/ppermute | solution.py:217
  20.4 3.2 %collective-permute-done.6.refs_11_ = bf16[256,1024]{1,0:T(8,128)(2,1)S(1)} collective-permute-done((bf16[256,1024]{1,0:T(8,128)(2,1)S(1)}, bf16[256,1024]{1,0:T(8,128)(2,1)S(1)}, u32[]{:S(2)}, u32[]{:S(2)}) %collective-permute-start.6) | collective-permute-done | bytes 524320 | tf_op jit(solution)/shard_map/ppermute | solution.py:217
  23.6 2.4 %collective-permute-done.8.refs_13_ = bf16[256,1024]{1,0:T(8,128)(2,1)S(1)} collective-permute-done((bf16[256,1024]{1,0:T(8,128)(2,1)S(1)}, bf16[256,1024]{1,0:T(8,128)(2,1)S(1)}, u32[]{:S(2)}, u32[]{:S(2)}) %collective-permute-start.8) | collective-permute-done | bytes 524320 | tf_op jit(solution)/shard_map/ppermute | solution.py:217
  26.0 4.4 %collective-permute-start.10 = (bf16[128,1024]{1,0:T(8,128)(2,1)S(1)}, bf16[128,1024]{1,0:T(8,128)(2,1)S(1)}, u32[]{:S(2)}, u32[]{:S(2)}) collective-permute-start(bf16[128,1024]{1,0:T(8,128)(2,1)S(1)} %slice.66), channel_id=1, source_target_pairs={{0,8},{2,10},{4,12},{6,14},{9,17},{11,19},{13,21},{15,23},{16,24},... | collective-permute-start | bytes 786440 | tf_op jit(solution)/shard_map/ppermute | solution.py:217
  31.7 2.5 %collective-permute-done.10.refs_15_ = bf16[128,1024]{1,0:T(8,128)(2,1)S(1)} collective-permute-done((bf16[128,1024]{1,0:T(8,128)(2,1)S(1)}, bf16[128,1024]{1,0:T(8,128)(2,1)S(1)}, u32[]{:S(2)}, u32[]{:S(2)}) %collective-permute-start.10) | collective-permute-done | bytes 262176 | tf_op jit(solution)/shard_map/ppermute | solution.py:217
  36.2 22.3 %shard_map.128 = (bf16[256,4096]{1,0:T(8,128)(2,1)}, bf16[16,4096]{1,0:T(8,128)(2,1)S(1)}, f32[16,256]{1,0:T(8,128)S(1)}, f32[16,1024]{1,0:T(8,128)S(1)}, f32[16...) custom-call(bf16[256,4096]{1,0:T(8,128)(2,1)S(1)} %copy-done.1, bf16[16,256]{1,0:T(8,128)(2,1)S(1)} %get-tuple-element.24.refs_1_, ...), custom_call_target="tpu_custom_call" | custom-call | flops 21474836480 | bytes 16777216 | tf_op jit(solution)/shard_map/pallas_call | solution.py:169
  60.0 9.9 %collective-permute-start.15 = (f32[16,2,256]{2,0,1:T(8,128)S(1)}, f32[16,2,256]{2,0,1:T(8,128)S(1)}, u32[]{:S(2)}, u32[]{:S(2)}) collective-permute-start(f32[16,2,256]{2,0,1:T(8,128)S(1)} %copy.17), channel_id=1, source_target_pairs={{0,4},{1,5},{2,6},{3,7},{4,0},{5,1},{6,2},{7,3},{8,12},{9,13},{10,... | collective-permute-start | bytes 98312 | tf_op jit(solution)/shard_map/ppermute | solution.py:217
  70.0 1.8 %collective-permute-done.15 = f32[16,2,256]{2,0,1:T(8,128)S(1)} collective-permute-done((f32[16,2,256]{2,0,1:T(8,128)S(1)}, f32[16,2,256]{2,0,1:T(8,128)S(1)}, u32[]{:S(2)}, u32[]{:S(2)}) %collective-permute-start.15) | collective-permute-done | bytes 32800 | tf_op jit(solution)/shard_map/ppermute | solution.py:217
  71.8 1.3 %collective-permute-start.16 = (f32[16,256]{1,0:T(8,128)S(1)}, f32[16,256]{1,0:T(8,128)S(1)}, u32[]{:S(2)}, u32[]{:S(2)}) collective-permute-start(f32[16,256]{1,0:T(8,128)S(1)} %slice_bitcast_fusion.2), channel_id=1, source_target_pairs={{1,25},{3,27},{5,29},{7,31},{8,0},{10,2},{12,4},{14,6},{17,9},{19,... | collective-permute-start | bytes 49160 | tf_op jit(solution)/shard_map/ppermute | solution.py:217
  73.2 24.3 %collective-permute-done.16 = f32[16,256]{1,0:T(8,128)S(1)} collective-permute-done((f32[16,256]{1,0:T(8,128)S(1)}, f32[16,256]{1,0:T(8,128)S(1)}, u32[]{:S(2)}, u32[]{:S(2)}) %collective-permute-start.16) | collective-permute-done | bytes 16416 | tf_op jit(solution)/shard_map/ppermute | solution.py:217
  98.5 2.1 %collective-permute-start.24 = (bf16[16,2304]{1,0:T(8,128)(2,1)S(1)}, bf16[16,2304]{1,0:T(8,128)(2,1)S(1)}, u32[]{:S(2)}, u32[]{:S(2)}) collective-permute-start(bf16[16,2304]{1,0:T(8,128)(2,1)S(1)} %add_convert_fusion.7), channel_id=1, source_target_pairs={{0,4},{2,6},{4,0},{6,2},{8,12},{10,14},{12,8},{14,10},{16,20},{18,... | collective-permute-start | bytes 221192 | tf_op jit(solution)/shard_map/ppermute | solution.py:272
  102.9 1.4 %collective-permute-start.25 = (bf16[16,2304]{1,0:T(8,128)(2,1)S(1)}, bf16[16,2304]{1,0:T(8,128)(2,1)S(1)}, u32[]{:S(2)}, u32[]{:S(2)}) collective-permute-start(bf16[16,2304]{1,0:T(8,128)(2,1)S(1)} %add_convert_fusion.6), channel_id=1, source_target_pairs={{0,8},{2,10},{4,12},{6,14},{8,0},{10,2},{12,4},{14,6},{16,24},{18,... | collective-permute-start | bytes 221192 | tf_op jit(solution)/shard_map/ppermute | solution.py:272
  104.4 2.1 %collective-permute-start.19 = (bf16[16,4096]{1,0:T(8,128)(2,1)S(1)}, bf16[16,4096]{1,0:T(8,128)(2,1)S(1)}, u32[]{:S(2)}, u32[]{:S(2)}) collective-permute-start(bf16[16,4096]{1,0:T(8,128)(2,1)S(1)} %add_convert_fusion.3), channel_id=1, source_target_pairs={{0,4},{2,6},{4,0},{6,2},{8,12},{10,14},{12,8},{14,10},{16,20},{18,... | collective-permute-start | bytes 393224 | tf_op jit(solution)/shard_map/ppermute | solution.py:272
  107.4 2.7 %collective-permute-start.26 = (bf16[16,2304]{1,0:T(8,128)(2,1)S(1)}, bf16[16,2304]{1,0:T(8,128)(2,1)S(1)}, u32[]{:S(2)}, u32[]{:S(2)}) collective-permute-start(bf16[16,2304]{1,0:T(8,128)(2,1)S(1)} %add_convert_fusion.5), channel_id=1, source_target_pairs={{0,16},{2,18},{4,20},{6,22},{8,24},{10,26},{12,28},{14,30},{16,0},... | collective-permute-start | bytes 221192 | tf_op jit(solution)/shard_map/ppermute | solution.py:272
  110.1 2.1 %collective-permute-start.20 = (bf16[16,4096]{1,0:T(8,128)(2,1)S(1)}, bf16[16,4096]{1,0:T(8,128)(2,1)S(1)}, u32[]{:S(2)}, u32[]{:S(2)}) collective-permute-start(bf16[16,4096]{1,0:T(8,128)(2,1)S(1)} %add_convert_fusion.2), channel_id=1, source_target_pairs={{0,8},{2,10},{4,12},{6,14},{8,0},{10,2},{12,4},{14,6},{16,24},{18,... | collective-permute-start | bytes 393224 | tf_op jit(solution)/shard_map/ppermute | solution.py:272
  112.9 2.3 %collective-permute-done.20 = bf16[16,4096]{1,0:T(8,128)(2,1)S(1)} collective-permute-done((bf16[16,4096]{1,0:T(8,128)(2,1)S(1)}, bf16[16,4096]{1,0:T(8,128)(2,1)S(1)}, u32[]{:S(2)}, u32[]{:S(2)}) %collective-permute-start.20) | collective-permute-done | bytes 131104 | tf_op jit(solution)/shard_map/ppermute | solution.py:272
  115.2 2.7 %collective-permute-start.21 = (bf16[16,4096]{1,0:T(8,128)(2,1)S(1)}, bf16[16,4096]{1,0:T(8,128)(2,1)S(1)}, u32[]{:S(2)}, u32[]{:S(2)}) collective-permute-start(bf16[16,4096]{1,0:T(8,128)(2,1)S(1)} %add_convert_fusion.1), channel_id=1, source_target_pairs={{0,16},{2,18},{4,20},{6,22},{8,24},{10,26},{12,28},{14,30},{16,0},... | collective-permute-start | bytes 393224 | tf_op jit(solution)/shard_map/ppermute | solution.py:272
  118.0 5.1 %collective-permute-done.21 = bf16[16,4096]{1,0:T(8,128)(2,1)S(1)} collective-permute-done((bf16[16,4096]{1,0:T(8,128)(2,1)S(1)}, bf16[16,4096]{1,0:T(8,128)(2,1)S(1)}, u32[]{:S(2)}, u32[]{:S(2)}) %collective-permute-start.21) | collective-permute-done | bytes 131104 | tf_op jit(solution)/shard_map/ppermute | solution.py:272
  (80 shorter events, 14.5 us)
Async XLA Ops:
  4.1 11.0 %collective-permute-start = (f32[32,256]{1,0:T(8,128)S(1)}, f32[32,256]{1,0:T(8,128)S(1)}, u32[]{:S(2)}, u32[]{:S(2)}) collective-permute-start(f32[32,256]{1,0:T(8,128)S(1)} %fusion), channel_id=1, source_target_pairs={{0,1},{1,0},{2,3},{3,2},{4,5},{5,4},{6,7},{7,6},{8,9},{9,8},{10,11... | collective-permute-start | bytes 98312 | tf_op jit(solution)/shard_map/ppermute | solution.py:266
  8.1 15.5 %collective-permute-start.6 = (bf16[256,1024]{1,0:T(8,128)(2,1)S(1)}, bf16[256,1024]{1,0:T(8,128)(2,1)S(1)}, u32[]{:S(2)}, u32[]{:S(2)}) collective-permute-start(bf16[256,1024]{1,0:T(8,128)(2,1)S(1)} %constant_dynamic-update-slice_fusion.refs_9_), channel_id=1, source_target_pairs={{0,4},{1,5},{2,6},{3,7},{4,0},{6,2},{8,12},{9,13},{10,14},{11,15},... | collective-permute-start | bytes 1572872 | tf_op jit(solution)/shard_map/ppermute | solution.py:217
  11.5 14.5 %collective-permute-start.8 = (bf16[256,1024]{1,0:T(8,128)(2,1)S(1)}, bf16[256,1024]{1,0:T(8,128)(2,1)S(1)}, u32[]{:S(2)}, u32[]{:S(2)}) collective-permute-start(bf16[256,1024]{1,0:T(8,128)(2,1)S(1)} %constant_dynamic-update-slice_fusion.refs_9_), channel_id=1, source_target_pairs={{0,8},{2,10},{4,12},{6,14},{9,17},{11,19},{13,21},{15,23},{16,24},... | collective-permute-start | bytes 1572872 | tf_op jit(solution)/shard_map/ppermute | solution.py:217
  16.4 14.1 %collective-permute-start.2 = (bf16[16,512]{1,0:T(8,128)(2,1)S(1)}, bf16[16,512]{1,0:T(8,128)(2,1)S(1)}, u32[]{:S(2)}, u32[]{:S(2)}) collective-permute-start(bf16[16,512]{1,0:T(8,128)(2,1)S(1)} %pad_maximum_fusion.2.refs_5_), channel_id=1, source_target_pairs={{0,4},{1,5},{2,6},{3,7},{4,0},{5,1},{6,2},{7,3},{8,12},{9,13},{10,... | collective-permute-start | bytes 49160 | tf_op jit(solution)/shard_map/ppermute | solution.py:217
  16.4 14.8 %collective-permute-start.3 = (bf16[16,512]{1,0:T(8,128)(2,1)S(1)}, bf16[16,512]{1,0:T(8,128)(2,1)S(1)}, u32[]{:S(2)}, u32[]{:S(2)}) collective-permute-start(bf16[16,512]{1,0:T(8,128)(2,1)S(1)} %pad_maximum_fusion.2.refs_5_), channel_id=1, source_target_pairs={{0,8},{2,10},{4,12},{6,14},{9,17},{11,19},{13,21},{15,23},{16,24},... | collective-permute-start | bytes 49160 | tf_op jit(solution)/shard_map/ppermute | solution.py:217
  17.7 13.6 %collective-permute-start.4 = (bf16[16,512]{1,0:T(8,128)(2,1)S(1)}, bf16[16,512]{1,0:T(8,128)(2,1)S(1)}, u32[]{:S(2)}, u32[]{:S(2)}) collective-permute-start(bf16[16,512]{1,0:T(8,128)(2,1)S(1)} %pad_maximum_fusion.2.refs_5_), channel_id=1, source_target_pairs={{0,12},{2,14},{4,8},{6,10},{9,21},{11,23},{13,17},{15,19},{16,28},... | collective-permute-start | bytes 49160 | tf_op jit(solution)/shard_map/ppermute | solution.py:217
  23.6 11.2 %collective-permute-start.5 = (bf16[256,1024]{1,0:T(8,128)(2,1)S(1)}, bf16[256,1024]{1,0:T(8,128)(2,1)S(1)}, u32[]{:S(2)}, u32[]{:S(2)}) collective-permute-start(bf16[256,1024]{1,0:T(8,128)(2,1)S(1)} %constant_dynamic-update-slice_fusion.refs_9_), channel_id=1, source_target_pairs={{0,2},{1,3},{2,0},{3,1},{4,6},{5,7},{6,4},{7,5},{8,10},{9,11},{10,... | collective-permute-start | bytes 1572872 | tf_op jit(solution)/shard_map/ppermute | solution.py:217
  26.0 8.3 %collective-permute-start.10 = (bf16[128,1024]{1,0:T(8,128)(2,1)S(1)}, bf16[128,1024]{1,0:T(8,128)(2,1)S(1)}, u32[]{:S(2)}, u32[]{:S(2)}) collective-permute-start(bf16[128,1024]{1,0:T(8,128)(2,1)S(1)} %slice.66), channel_id=1, source_target_pairs={{0,8},{2,10},{4,12},{6,14},{9,17},{11,19},{13,21},{15,23},{16,24},... | collective-permute-start | bytes 786440 | tf_op jit(solution)/shard_map/ppermute | solution.py:217
  30.5 3.8 %collective-permute-start.11 = (bf16[128,1024]{1,0:T(8,128)(2,1)S(1)}, bf16[128,1024]{1,0:T(8,128)(2,1)S(1)}, u32[]{:S(2)}, u32[]{:S(2)}) collective-permute-start(bf16[128,1024]{1,0:T(8,128)(2,1)S(1)} %slice.67), channel_id=1, source_target_pairs={{1,5},{3,7},{5,1},{7,3},{8,12},{10,14},{12,8},{14,10},{17,21},{19,... | collective-permute-start | bytes 786440 | tf_op jit(solution)/shard_map/ppermute | solution.py:217
  31.2 5.0 %collective-permute-start.7 = (bf16[256,1024]{1,0:T(8,128)(2,1)S(1)}, bf16[256,1024]{1,0:T(8,128)(2,1)S(1)}, u32[]{:S(2)}, u32[]{:S(2)}) collective-permute-start(bf16[256,1024]{1,0:T(8,128)(2,1)S(1)} %collective-permute-done.6.refs_11_), channel_id=1, source_target_pairs={{0,2},{1,3},{2,0},{3,1},{4,6},{5,7},{6,4},{7,5},{8,10},{9,11},{10,... | collective-permute-start | bytes 1572872 | tf_op jit(solution)/shard_map/ppermute | solution.py:217
  31.2 5.0 %collective-permute-start.9 = (bf16[256,1024]{1,0:T(8,128)(2,1)S(1)}, bf16[256,1024]{1,0:T(8,128)(2,1)S(1)}, u32[]{:S(2)}, u32[]{:S(2)}) collective-permute-start(bf16[256,1024]{1,0:T(8,128)(2,1)S(1)} %collective-permute-done.8.refs_13_), channel_id=1, source_target_pairs={{0,2},{1,3},{2,0},{3,1},{4,6},{5,7},{6,4},{7,5},{8,10},{9,11},{10,... | collective-permute-start | bytes 1572872 | tf_op jit(solution)/shard_map/ppermute | solution.py:217
  34.3 1.9 %collective-permute-start.13 = (bf16[128,1024]{1,0:T(8,128)(2,1)S(1)}, bf16[128,1024]{1,0:T(8,128)(2,1)S(1)}, u32[]{:S(2)}, u32[]{:S(2)}) collective-permute-start(bf16[128,1024]{1,0:T(8,128)(2,1)S(1)} %collective-permute-done.11.refs_16_), channel_id=1, source_target_pairs={{0,2},{1,3},{2,0},{3,1},{4,6},{5,7},{6,4},{7,5},{8,10},{9,11},{10,... | collective-permute-start | bytes 786440 | tf_op jit(solution)/shard_map/ppermute | solution.py:217
  60.0 11.8 %collective-permute-start.15 = (f32[16,2,256]{2,0,1:T(8,128)S(1)}, f32[16,2,256]{2,0,1:T(8,128)S(1)}, u32[]{:S(2)}, u32[]{:S(2)}) collective-permute-start(f32[16,2,256]{2,0,1:T(8,128)S(1)} %copy.17), channel_id=1, source_target_pairs={{0,4},{1,5},{2,6},{3,7},{4,0},{5,1},{6,2},{7,3},{8,12},{9,13},{10,... | collective-permute-start | bytes 98312 | tf_op jit(solution)/shard_map/ppermute | solution.py:217
  71.8 25.7 %collective-permute-start.16 = (f32[16,256]{1,0:T(8,128)S(1)}, f32[16,256]{1,0:T(8,128)S(1)}, u32[]{:S(2)}, u32[]{:S(2)}) collective-permute-start(f32[16,256]{1,0:T(8,128)S(1)} %slice_bitcast_fusion.2), channel_id=1, source_target_pairs={{1,25},{3,27},{5,29},{7,31},{8,0},{10,2},{12,4},{14,6},{17,9},{19,... | collective-permute-start | bytes 49160 | tf_op jit(solution)/shard_map/ppermute | solution.py:217
  73.1 25.3 %collective-permute-start.23 = (bf16[16,2304]{1,0:T(8,128)(2,1)S(1)}, bf16[16,2304]{1,0:T(8,128)(2,1)S(1)}, u32[]{:S(2)}, u32[]{:S(2)}) collective-permute-start(bf16[16,2304]{1,0:T(8,128)(2,1)S(1)} %broadcast_select_fusion.5), channel_id=1, source_target_pairs={{0,2},{2,0},{4,6},{6,4},{8,10},{10,8},{12,14},{14,12},{16,18},{18,... | collective-permute-start | bytes 221192 | tf_op jit(solution)/shard_map/ppermute | solution.py:272
  97.6 4.0 %collective-permute-start.17 = (f32[32,256]{1,0:T(8,128)S(1)}, f32[32,256]{1,0:T(8,128)S(1)}, u32[]{:S(2)}, u32[]{:S(2)}) collective-permute-start(f32[32,256]{1,0:T(8,128)S(1)} %pad_maximum_fusion.1), channel_id=1, source_target_pairs={{0,1},{1,0},{2,3},{3,2},{4,5},{5,4},{6,7},{7,6},{8,9},{9,8},{10,11... | collective-permute-start | bytes 98312 | tf_op jit(solution)/shard_map/ppermute | solution.py:266
  98.5 4.4 %collective-permute-start.24 = (bf16[16,2304]{1,0:T(8,128)(2,1)S(1)}, bf16[16,2304]{1,0:T(8,128)(2,1)S(1)}, u32[]{:S(2)}, u32[]{:S(2)}) collective-permute-start(bf16[16,2304]{1,0:T(8,128)(2,1)S(1)} %add_convert_fusion.7), channel_id=1, source_target_pairs={{0,4},{2,6},{4,0},{6,2},{8,12},{10,14},{12,8},{14,10},{16,20},{18,... | collective-permute-start | bytes 221192 | tf_op jit(solution)/shard_map/ppermute | solution.py:272
  102.0 2.3 %collective-permute-start.18 = (bf16[16,4096]{1,0:T(8,128)(2,1)S(1)}, bf16[16,4096]{1,0:T(8,128)(2,1)S(1)}, u32[]{:S(2)}, u32[]{:S(2)}) collective-permute-start(bf16[16,4096]{1,0:T(8,128)(2,1)S(1)} %broadcast_select_fusion.2), channel_id=1, source_target_pairs={{0,2},{2,0},{4,6},{6,4},{8,10},{10,8},{12,14},{14,12},{16,18},{18,... | collective-permute-start | bytes 393224 | tf_op jit(solution)/shard_map/ppermute | solution.py:272
  102.9 4.4 %collective-permute-start.25 = (bf16[16,2304]{1,0:T(8,128)(2,1)S(1)}, bf16[16,2304]{1,0:T(8,128)(2,1)S(1)}, u32[]{:S(2)}, u32[]{:S(2)}) collective-permute-start(bf16[16,2304]{1,0:T(8,128)(2,1)S(1)} %add_convert_fusion.6), channel_id=1, source_target_pairs={{0,8},{2,10},{4,12},{6,14},{8,0},{10,2},{12,4},{14,6},{16,24},{18,... | collective-permute-start | bytes 221192 | tf_op jit(solution)/shard_map/ppermute | solution.py:272
  104.4 5.7 %collective-permute-start.19 = (bf16[16,4096]{1,0:T(8,128)(2,1)S(1)}, bf16[16,4096]{1,0:T(8,128)(2,1)S(1)}, u32[]{:S(2)}, u32[]{:S(2)}) collective-permute-start(bf16[16,4096]{1,0:T(8,128)(2,1)S(1)} %add_convert_fusion.3), channel_id=1, source_target_pairs={{0,4},{2,6},{4,0},{6,2},{8,12},{10,14},{12,8},{14,10},{16,20},{18,... | collective-permute-start | bytes 393224 | tf_op jit(solution)/shard_map/ppermute | solution.py:272
  107.4 5.4 %collective-permute-start.26 = (bf16[16,2304]{1,0:T(8,128)(2,1)S(1)}, bf16[16,2304]{1,0:T(8,128)(2,1)S(1)}, u32[]{:S(2)}, u32[]{:S(2)}) collective-permute-start(bf16[16,2304]{1,0:T(8,128)(2,1)S(1)} %add_convert_fusion.5), channel_id=1, source_target_pairs={{0,16},{2,18},{4,20},{6,22},{8,24},{10,26},{12,28},{14,30},{16,0},... | collective-permute-start | bytes 221192 | tf_op jit(solution)/shard_map/ppermute | solution.py:272
  110.1 5.0 %collective-permute-start.20 = (bf16[16,4096]{1,0:T(8,128)(2,1)S(1)}, bf16[16,4096]{1,0:T(8,128)(2,1)S(1)}, u32[]{:S(2)}, u32[]{:S(2)}) collective-permute-start(bf16[16,4096]{1,0:T(8,128)(2,1)S(1)} %add_convert_fusion.2), channel_id=1, source_target_pairs={{0,8},{2,10},{4,12},{6,14},{8,0},{10,2},{12,4},{14,6},{16,24},{18,... | collective-permute-start | bytes 393224 | tf_op jit(solution)/shard_map/ppermute | solution.py:272
  112.8 5.1 %collective-permute-start.27 = (bf16[16,2304]{1,0:T(8,128)(2,1)S(1)}, bf16[16,2304]{1,0:T(8,128)(2,1)S(1)}, u32[]{:S(2)}, u32[]{:S(2)}) collective-permute-start(bf16[16,2304]{1,0:T(8,128)(2,1)S(1)} %add_convert_fusion.4), channel_id=1, source_target_pairs={{0,2},{2,0},{4,6},{6,4},{8,10},{10,8},{12,14},{14,12},{16,18},{18,... | collective-permute-start | bytes 221192 | tf_op jit(solution)/shard_map/ppermute | solution.py:272
  115.2 7.8 %collective-permute-start.21 = (bf16[16,4096]{1,0:T(8,128)(2,1)S(1)}, bf16[16,4096]{1,0:T(8,128)(2,1)S(1)}, u32[]{:S(2)}, u32[]{:S(2)}) collective-permute-start(bf16[16,4096]{1,0:T(8,128)(2,1)S(1)} %add_convert_fusion.1), channel_id=1, source_target_pairs={{0,16},{2,18},{4,20},{6,22},{8,24},{10,26},{12,28},{14,30},{16,0},... | collective-permute-start | bytes 393224 | tf_op jit(solution)/shard_map/ppermute | solution.py:272
  (10 other events, 154.1 us)

commit v5 on v4

--- a/solution.py
+++ b/solution.py
@@ -79,17 +79,14 @@
                 grad_v[at, :] = jnp.zeros((count, width_kv), F32)
 
     def finish(blocks):
-        for g in range(kv):
-            cols = slice(g * HD, (g + 1) * HD)
-            total = None
-            for slot, j in enumerate(blocks):
-                rounded = grad_v[slot * rows : (slot + 1) * rows, cols].astype(BF16)
-                at = slice(j // 2 * rows, (j // 2 + 1) * rows)
-                target = back_v_sibling if j % 2 else back_v
-                target[:, at] += ADAPTER_SCALE * dot(up_v[:, cols], rounded, NT)
-                term = dot(low_v[j // 2][:, j % 2 * rows : (j % 2 + 1) * rows], rounded, NN)
-                total = term if total is None else total + term
-            grad_up_v[:, cols] = (ADAPTER_SCALE * total).astype(BF16)
+        length = len(blocks) * rows
+        rounded = grad_v[:length, :].astype(BF16)
+        back = ADAPTER_SCALE * dot(up_v[...], rounded, NT)
+        for slot, j in enumerate(blocks):
+            target = back_v_sibling if j % 2 else back_v
+            target[:, j // 2 * rows : (j // 2 + 1) * rows] = back[:, slot * rows : (slot + 1) * rows]
+        low = jnp.concatenate([low_v[j // 2][...] for j in blocks[::2]], axis=1)
+        grad_up_v[...] = (ADAPTER_SCALE * dot(low, rounded, NN)).astype(BF16)
 
     def attend(length):
         def wide(i):
@@ -117,9 +114,9 @@
                 top = jnp.maximum(top, jnp.max(rest, axis=0, keepdims=True))
             return top * to_log2
 
-        def one_step(i, top):
+        def one_step(i, top, last=False):
             probs[:length, :] = jnp.exp2(scores[:length, :] * to_log2 - top).astype(BF16)
-            later = score(jnp.minimum(i + 1, steps - 1))
+            later = top if last else score(i + 1)
             attended = dot(values_t[i // steps_per_kv, :, :length], probs[:length, :], NN)
             inverse = 1.0 / attended[HD : HD + 1, :]
             attended = (attended[:HD] * inverse).astype(BF16)
@@ -144,7 +141,8 @@
 
             return later
 
-        lax.fori_loop(0, steps, one_step, score(0))
+        top = lax.fori_loop(0, steps - 1, one_step, score(0))
+        one_step(jnp.int32(steps - 1), top, last=True)
 
     for y in (0, 1):
         for z in (0, 1):
@@ -289,14 +287,11 @@
     return (mine.astype(F32) + got.astype(F32)).astype(BF16)
 
 
-def sum_over_seq(part):
-    kept, sent = split_for_core(part)
-    total = add_up(kept, swap(sent, 1))
-    step = 2
+def sum_over_chips(total, step):
     while step < lax.axis_size("seq"):
         total = add_up(total, swap(total, step))
         step *= 2
-    return join_cores(total)
+    return total
 
 
 def per_device(
@@ -334,19 +329,25 @@
         given,
     )
 
-    grad_up = sum_over_seq(jnp.concatenate((grad_up_q, grad_up_v), axis=1)).astype(F32)
     back_v = (back_v + routes.core(back_v_sibling)).reshape(rank, 4, rows)
     back_v = back_v[:, 0::2] + routes.across_y(back_v[:, 1::2])
     back_v = back_v[:, 0] + routes.down(back_v[:, 1])
     back = sum_over_tensor(jnp.concatenate((back_q, back_v), axis=0)).astype(BF16)
     grad_down = dot(back, hidden_in, NN).astype(BF16)
-    grad_down = sum_over_seq(jnp.concatenate((grad_down[:rank], grad_down[rank:]), axis=1))
-    grad_down = grad_down.astype(F32)
+    odd = lax.axis_index("seq") % 2 == 1
+    of_query, of_value = grad_down[:rank], grad_down[rank:]
+    total = add_up(jnp.where(odd, of_value, of_query), swap(jnp.where(odd, of_query, of_value), 1))
+    kept, sent = split_for_core(jnp.concatenate((grad_up_q, grad_up_v), axis=1))
+    grad_up = sum_over_chips(add_up(kept, swap(sent, 1)), 2)
+    total, grad_up = lax.optimization_barrier((add_up(total, swap(total, 2)), grad_up))
+    total = sum_over_chips(total, 4)
+    grad_up = join_cores(grad_up).astype(F32)
+    got = swap(total, 1)
     return (
         attention,
-        grad_down[:, :width_here].T,
+        jnp.where(odd, got, total).astype(F32).T,
         grad_up[:, :-kv_width],
-        grad_down[:, width_here:].T,
+        jnp.where(odd, total, got).astype(F32).T,
         grad_up[:, -kv_width:],
     )
 

time: 126 us -> 125 us (level)
  starting transfers between devices: 45.7 us -> 43.9 us
    ppermute x10, waiting for transfers between devices: 9.62 us -> 12.2 us  [swap(): lax.ppermute(block, 'seq', [(i, i ^ step) for i in range(lax.axis_size('s...]
    ppermute x10, starting transfers between devices: 13.3 us -> 10.8 us  [swap(): lax.ppermute(block, 'seq', [(i, i ^ step) for i in range(lax.axis_size('s...]
    ppermute x16, waiting for transfers between devices: 38 us -> 35.7 us  [send(): return lax.ppermute(block, AXES, route)]
where the time goes in v5:
time: 125 us; the launch traced here: 124 us
  waiting for transfers between devices  49.1 us (39%)
  starting transfers between devices  43.9 us (35%)
  Pallas kernels  21.8 us (17%)
  local copies, waits for them, and re-layouts  3.6 us (3%)
  matrix products  2.32 us (2%)
  other arithmetic  1.8 us (1%)
    ppermute x16, waiting for transfers between devices, send(): return lax.ppermute(block, AXES, route)  35.7 us
    ppermute x16, starting transfers between devices, send(): return lax.ppermute(block, AXES, route)  28.5 us
    pallas_call x1, Pallas kernels, attention_call(): pl.pallas_call(functools.partial(attention_body, rows, per_head, kv, stac...  21.8 us
    ppermute x10, waiting for transfers between devices, swap(): lax.ppermute(block, 'seq', [(i, i ^ step) for i in range(lax.axis_size('s...  12.2 us
    ppermute x10, starting transfers between devices, swap(): lax.ppermute(block, 'seq', [(i, i ^ step) for i in range(lax.axis_size('s...  10.8 us
    ppermute x2, starting transfers between devices, sum_over_tensor(): lax.ppermute(part, 'tensor', [(i, i ^ step) for i in range(size)])  4.61 us
  transfers between devices with their start and end apart: 28, of which 15 were waited for; matrix products, arithmetic and copies ran while one was open for 3% of the time, Pallas kernels for 0%

profile of v5, /device:TPU:0, one launch (start us, length us, event | category | flops | bytes accessed | tf_op | source)
XLA Modules:
  0.0 123.5 jit_solution(11186228153963415942)
XLA Ops:
  0.7 1.5 %copy-done = bf16[256,4096]{1,0:T(8,128)(2,1)S(1)} copy-done((bf16[256,4096]{1,0:T(8,128)(2,1)S(1)}, bf16[256,4096]{1,0:T(8,128)(2,1)}, u32[]{:S(2)}) %copy-start) | copy-done | bytes 2097176
  2.2 1.8 %fusion = f32[32,256]{1,0:T(8,128)S(1)} fusion(bf16[256,4096]{1,0:T(8,128)(2,1)S(1)} %copy-done, bf16[4096,16]{0,1:T(8,128)(2,1)} %param.15, bf16[4096,16]{0,1:T(8,128)(2,1)} %param.13), kind=kOutput, calls=%fused_computation.1 | convolution fusion | flops 67633152 | bytes 2392064 | tf_op jit(solution)/shard_map/dot_general | solution.py:317
  4.1 3.0 %collective-permute-start = (f32[32,256]{1,0:T(8,128)S(1)}, f32[32,256]{1,0:T(8,128)S(1)}, u32[]{:S(2)}, u32[]{:S(2)}) collective-permute-start(f32[32,256]{1,0:T(8,128)S(1)} %fusion), channel_id=1, source_target_pairs={{0,1},{1,0},{2,3},{3,2},{4,5},{5,4},{6,7},{7,6},{8,9},{9,8},{10,11... | collective-permute-start | bytes 98312 | tf_op jit(solution)/shard_map/ppermute | solution.py:264
  8.1 3.4 %collective-permute-start.6 = (bf16[256,1024]{1,0:T(8,128)(2,1)S(1)}, bf16[256,1024]{1,0:T(8,128)(2,1)S(1)}, u32[]{:S(2)}, u32[]{:S(2)}) collective-permute-start(bf16[256,1024]{1,0:T(8,128)(2,1)S(1)} %constant_dynamic-update-slice_fusion.refs_9_), channel_id=1, source_target_pairs={{0,4},{1,5},{2,6},{3,7},{4,0},{6,2},{8,12},{9,13},{10,14},{11,15},... | collective-permute-start | bytes 1572872 | tf_op jit(solution)/shard_map/ppermute | solution.py:215
  11.5 3.5 %collective-permute-start.8 = (bf16[256,1024]{1,0:T(8,128)(2,1)S(1)}, bf16[256,1024]{1,0:T(8,128)(2,1)S(1)}, u32[]{:S(2)}, u32[]{:S(2)}) collective-permute-start(bf16[256,1024]{1,0:T(8,128)(2,1)S(1)} %constant_dynamic-update-slice_fusion.refs_9_), channel_id=1, source_target_pairs={{0,8},{2,10},{4,12},{6,14},{9,17},{11,19},{13,21},{15,23},{16,24},... | collective-permute-start | bytes 1572872 | tf_op jit(solution)/shard_map/ppermute | solution.py:215
  17.7 2.7 %collective-permute-start.4 = (bf16[16,512]{1,0:T(8,128)(2,1)S(1)}, bf16[16,512]{1,0:T(8,128)(2,1)S(1)}, u32[]{:S(2)}, u32[]{:S(2)}) collective-permute-start(bf16[16,512]{1,0:T(8,128)(2,1)S(1)} %pad_maximum_fusion.2.refs_5_), channel_id=1, source_target_pairs={{0,12},{2,14},{4,8},{6,10},{9,21},{11,23},{13,17},{15,19},{16,28},... | collective-permute-start | bytes 49160 | tf_op jit(solution)/shard_map/ppermute | solution.py:215
  20.4 3.2 %collective-permute-done.6.refs_11_ = bf16[256,1024]{1,0:T(8,128)(2,1)S(1)} collective-permute-done((bf16[256,1024]{1,0:T(8,128)(2,1)S(1)}, bf16[256,1024]{1,0:T(8,128)(2,1)S(1)}, u32[]{:S(2)}, u32[]{:S(2)}) %collective-permute-start.6) | collective-permute-done | bytes 524320 | tf_op jit(solution)/shard_map/ppermute | solution.py:215
  23.6 2.4 %collective-permute-done.8.refs_13_ = bf16[256,1024]{1,0:T(8,128)(2,1)S(1)} collective-permute-done((bf16[256,1024]{1,0:T(8,128)(2,1)S(1)}, bf16[256,1024]{1,0:T(8,128)(2,1)S(1)}, u32[]{:S(2)}, u32[]{:S(2)}) %collective-permute-start.8) | collective-permute-done | bytes 524320 | tf_op jit(solution)/shard_map/ppermute | solution.py:215
  26.0 4.4 %collective-permute-start.10 = (bf16[128,1024]{1,0:T(8,128)(2,1)S(1)}, bf16[128,1024]{1,0:T(8,128)(2,1)S(1)}, u32[]{:S(2)}, u32[]{:S(2)}) collective-permute-start(bf16[128,1024]{1,0:T(8,128)(2,1)S(1)} %slice.58), channel_id=1, source_target_pairs={{0,8},{2,10},{4,12},{6,14},{9,17},{11,19},{13,21},{15,23},{16,24},... | collective-permute-start | bytes 786440 | tf_op jit(solution)/shard_map/ppermute | solution.py:215
  31.7 2.5 %collective-permute-done.10.refs_15_ = bf16[128,1024]{1,0:T(8,128)(2,1)S(1)} collective-permute-done((bf16[128,1024]{1,0:T(8,128)(2,1)S(1)}, bf16[128,1024]{1,0:T(8,128)(2,1)S(1)}, u32[]{:S(2)}, u32[]{:S(2)}) %collective-permute-start.10) | collective-permute-done | bytes 262176 | tf_op jit(solution)/shard_map/ppermute | solution.py:215
  36.2 21.8 %shard_map.128 = (bf16[256,4096]{1,0:T(8,128)(2,1)}, bf16[16,4096]{1,0:T(8,128)(2,1)S(1)}, f32[16,256]{1,0:T(8,128)S(1)}, f32[16,1024]{1,0:T(8,128)S(1)}, f32[16...) custom-call(bf16[256,4096]{1,0:T(8,128)(2,1)S(1)} %copy-done.1, bf16[16,256]{1,0:T(8,128)(2,1)S(1)} %get-tuple-element.26.refs_1_, ...), custom_call_target="tpu_custom_call" | custom-call | flops 21474836480 | bytes 16777216 | tf_op jit(solution)/shard_map/pallas_call | solution.py:167
  59.5 9.9 %collective-permute-start.15 = (f32[16,2,256]{2,0,1:T(8,128)S(1)}, f32[16,2,256]{2,0,1:T(8,128)S(1)}, u32[]{:S(2)}, u32[]{:S(2)}) collective-permute-start(f32[16,2,256]{2,0,1:T(8,128)S(1)} %copy.17), channel_id=1, source_target_pairs={{0,4},{1,5},{2,6},{3,7},{4,0},{5,1},{6,2},{7,3},{8,12},{9,13},{10,... | collective-permute-start | bytes 98312 | tf_op jit(solution)/shard_map/ppermute | solution.py:215
  69.6 1.7 %collective-permute-done.15 = f32[16,2,256]{2,0,1:T(8,128)S(1)} collective-permute-done((f32[16,2,256]{2,0,1:T(8,128)S(1)}, f32[16,2,256]{2,0,1:T(8,128)S(1)}, u32[]{:S(2)}, u32[]{:S(2)}) %collective-permute-start.15) | collective-permute-done | bytes 32800 | tf_op jit(solution)/shard_map/ppermute | solution.py:215
  71.3 1.3 %collective-permute-start.16 = (f32[16,256]{1,0:T(8,128)S(1)}, f32[16,256]{1,0:T(8,128)S(1)}, u32[]{:S(2)}, u32[]{:S(2)}) collective-permute-start(f32[16,256]{1,0:T(8,128)S(1)} %slice_bitcast_fusion), channel_id=1, source_target_pairs={{1,25},{3,27},{5,29},{7,31},{8,0},{10,2},{12,4},{14,6},{17,9},{19,... | collective-permute-start | bytes 49160 | tf_op jit(solution)/shard_map/ppermute | solution.py:215
  72.6 2.1 %collective-permute-start.21 = (bf16[16,2304]{1,0:T(8,128)(2,1)S(1)}, bf16[16,2304]{1,0:T(8,128)(2,1)S(1)}, u32[]{:S(2)}, u32[]{:S(2)}) collective-permute-start(bf16[16,2304]{1,0:T(8,128)(2,1)S(1)} %add_convert_fusion.7), channel_id=1, source_target_pairs={{0,4},{2,6},{4,0},{6,2},{8,12},{10,14},{12,8},{14,10},{16,20},{18,... | collective-permute-start | bytes 221192 | tf_op jit(solution)/shard_map/ppermute | solution.py:270
  74.7 22.2 %collective-permute-done.16 = f32[16,256]{1,0:T(8,128)S(1)} collective-permute-done((f32[16,256]{1,0:T(8,128)S(1)}, f32[16,256]{1,0:T(8,128)S(1)}, u32[]{:S(2)}, u32[]{:S(2)}) %collective-permute-start.16) | collective-permute-done | bytes 16416 | tf_op jit(solution)/shard_map/ppermute | solution.py:215
  96.9 1.6 %collective-permute-start.17 = (f32[32,256]{1,0:T(8,128)S(1)}, f32[32,256]{1,0:T(8,128)S(1)}, u32[]{:S(2)}, u32[]{:S(2)}) collective-permute-start(f32[32,256]{1,0:T(8,128)S(1)} %pad_maximum_fusion.1), channel_id=1, source_target_pairs={{0,1},{1,0},{2,3},{3,2},{4,5},{5,4},{6,7},{7,6},{8,9},{9,8},{10,11... | collective-permute-start | bytes 98312 | tf_op jit(solution)/shard_map/ppermute | solution.py:264
  101.5 1.5 %collective-permute-done.22 = bf16[16,2304]{1,0:T(8,128)(2,1)S(1)} collective-permute-done((bf16[16,2304]{1,0:T(8,128)(2,1)S(1)}, bf16[16,2304]{1,0:T(8,128)(2,1)S(1)}, u32[]{:S(2)}, u32[]{:S(2)}) %collective-permute-start.22) | collective-permute-done | bytes 73760 | tf_op jit(solution)/shard_map/ppermute | solution.py:270
  103.0 2.0 %collective-permute-start.23 = (bf16[16,2304]{1,0:T(8,128)(2,1)S(1)}, bf16[16,2304]{1,0:T(8,128)(2,1)S(1)}, u32[]{:S(2)}, u32[]{:S(2)}) collective-permute-start(bf16[16,2304]{1,0:T(8,128)(2,1)S(1)} %add_convert_fusion.5), channel_id=1, source_target_pairs={{0,16},{2,18},{4,20},{6,22},{8,24},{10,26},{12,28},{14,30},{16,0},... | collective-permute-start | bytes 221192 | tf_op jit(solution)/shard_map/ppermute | solution.py:270
  105.0 2.1 %collective-permute-start.19 = (bf16[16,4096]{1,0:T(8,128)(2,1)S(1)}, bf16[16,4096]{1,0:T(8,128)(2,1)S(1)}, u32[]{:S(2)}, u32[]{:S(2)}) collective-permute-start(bf16[16,4096]{1,0:T(8,128)(2,1)S(1)} %add_convert_fusion.3), channel_id=1, source_target_pairs={{0,4},{2,6},{4,0},{6,2},{8,12},{10,14},{12,8},{14,10},{16,20},{18,... | collective-permute-start | bytes 393224 | tf_op jit(solution)/shard_map/ppermute | solution.py:270
  107.1 2.0 %collective-permute-done.23 = bf16[16,2304]{1,0:T(8,128)(2,1)S(1)} collective-permute-done((bf16[16,2304]{1,0:T(8,128)(2,1)S(1)}, bf16[16,2304]{1,0:T(8,128)(2,1)S(1)}, u32[]{:S(2)}, u32[]{:S(2)}) %collective-permute-start.23) | collective-permute-done | bytes 73760 | tf_op jit(solution)/shard_map/ppermute | solution.py:270
  110.2 2.0 %collective-permute-start.24 = (bf16[16,4096]{1,0:T(8,128)(2,1)S(1)}, bf16[16,4096]{1,0:T(8,128)(2,1)S(1)}, u32[]{:S(2)}, u32[]{:S(2)}) collective-permute-start(bf16[16,4096]{1,0:T(8,128)(2,1)S(1)} %add_convert_fusion.2), channel_id=1, source_target_pairs={{0,8},{2,10},{4,12},{6,14},{8,0},{10,2},{12,4},{14,6},{16,24},{18,... | collective-permute-start | bytes 393224 | tf_op jit(solution)/shard_map/ppermute | solution.py:270
  112.2 3.0 %collective-permute-done.24 = bf16[16,4096]{1,0:T(8,128)(2,1)S(1)} collective-permute-done((bf16[16,4096]{1,0:T(8,128)(2,1)S(1)}, bf16[16,4096]{1,0:T(8,128)(2,1)S(1)}, u32[]{:S(2)}, u32[]{:S(2)}) %collective-permute-start.24) | collective-permute-done | bytes 131104 | tf_op jit(solution)/shard_map/ppermute | solution.py:270
  116.5 4.7 %collective-permute-done.25 = bf16[16,4096]{1,0:T(8,128)(2,1)S(1)} collective-permute-done((bf16[16,4096]{1,0:T(8,128)(2,1)S(1)}, bf16[16,4096]{1,0:T(8,128)(2,1)S(1)}, u32[]{:S(2)}, u32[]{:S(2)}) %collective-permute-start.25) | collective-permute-done | bytes 131104 | tf_op jit(solution)/shard_map/ppermute | solution.py:270
  (78 shorter events, 16.1 us)
Async XLA Ops:
  4.1 11.0 %collective-permute-start = (f32[32,256]{1,0:T(8,128)S(1)}, f32[32,256]{1,0:T(8,128)S(1)}, u32[]{:S(2)}, u32[]{:S(2)}) collective-permute-start(f32[32,256]{1,0:T(8,128)S(1)} %fusion), channel_id=1, source_target_pairs={{0,1},{1,0},{2,3},{3,2},{4,5},{5,4},{6,7},{7,6},{8,9},{9,8},{10,11... | collective-permute-start | bytes 98312 | tf_op jit(solution)/shard_map/ppermute | solution.py:264
  8.1 15.5 %collective-permute-start.6 = (bf16[256,1024]{1,0:T(8,128)(2,1)S(1)}, bf16[256,1024]{1,0:T(8,128)(2,1)S(1)}, u32[]{:S(2)}, u32[]{:S(2)}) collective-permute-start(bf16[256,1024]{1,0:T(8,128)(2,1)S(1)} %constant_dynamic-update-slice_fusion.refs_9_), channel_id=1, source_target_pairs={{0,4},{1,5},{2,6},{3,7},{4,0},{6,2},{8,12},{9,13},{10,14},{11,15},... | collective-permute-start | bytes 1572872 | tf_op jit(solution)/shard_map/ppermute | solution.py:215
  11.5 14.5 %collective-permute-start.8 = (bf16[256,1024]{1,0:T(8,128)(2,1)S(1)}, bf16[256,1024]{1,0:T(8,128)(2,1)S(1)}, u32[]{:S(2)}, u32[]{:S(2)}) collective-permute-start(bf16[256,1024]{1,0:T(8,128)(2,1)S(1)} %constant_dynamic-update-slice_fusion.refs_9_), channel_id=1, source_target_pairs={{0,8},{2,10},{4,12},{6,14},{9,17},{11,19},{13,21},{15,23},{16,24},... | collective-permute-start | bytes 1572872 | tf_op jit(solution)/shard_map/ppermute | solution.py:215
  16.4 14.1 %collective-permute-start.2 = (bf16[16,512]{1,0:T(8,128)(2,1)S(1)}, bf16[16,512]{1,0:T(8,128)(2,1)S(1)}, u32[]{:S(2)}, u32[]{:S(2)}) collective-permute-start(bf16[16,512]{1,0:T(8,128)(2,1)S(1)} %pad_maximum_fusion.2.refs_5_), channel_id=1, source_target_pairs={{0,4},{1,5},{2,6},{3,7},{4,0},{5,1},{6,2},{7,3},{8,12},{9,13},{10,... | collective-permute-start | bytes 49160 | tf_op jit(solution)/shard_map/ppermute | solution.py:215
  16.4 14.8 %collective-permute-start.3 = (bf16[16,512]{1,0:T(8,128)(2,1)S(1)}, bf16[16,512]{1,0:T(8,128)(2,1)S(1)}, u32[]{:S(2)}, u32[]{:S(2)}) collective-permute-start(bf16[16,512]{1,0:T(8,128)(2,1)S(1)} %pad_maximum_fusion.2.refs_5_), channel_id=1, source_target_pairs={{0,8},{2,10},{4,12},{6,14},{9,17},{11,19},{13,21},{15,23},{16,24},... | collective-permute-start | bytes 49160 | tf_op jit(solution)/shard_map/ppermute | solution.py:215
  17.7 13.6 %collective-permute-start.4 = (bf16[16,512]{1,0:T(8,128)(2,1)S(1)}, bf16[16,512]{1,0:T(8,128)(2,1)S(1)}, u32[]{:S(2)}, u32[]{:S(2)}) collective-permute-start(bf16[16,512]{1,0:T(8,128)(2,1)S(1)} %pad_maximum_fusion.2.refs_5_), channel_id=1, source_target_pairs={{0,12},{2,14},{4,8},{6,10},{9,21},{11,23},{13,17},{15,19},{16,28},... | collective-permute-start | bytes 49160 | tf_op jit(solution)/shard_map/ppermute | solution.py:215
  23.6 11.2 %collective-permute-start.5 = (bf16[256,1024]{1,0:T(8,128)(2,1)S(1)}, bf16[256,1024]{1,0:T(8,128)(2,1)S(1)}, u32[]{:S(2)}, u32[]{:S(2)}) collective-permute-start(bf16[256,1024]{1,0:T(8,128)(2,1)S(1)} %constant_dynamic-update-slice_fusion.refs_9_), channel_id=1, source_target_pairs={{0,2},{1,3},{2,0},{3,1},{4,6},{5,7},{6,4},{7,5},{8,10},{9,11},{10,... | collective-permute-start | bytes 1572872 | tf_op jit(solution)/shard_map/ppermute | solution.py:215
  26.0 8.3 %collective-permute-start.10 = (bf16[128,1024]{1,0:T(8,128)(2,1)S(1)}, bf16[128,1024]{1,0:T(8,128)(2,1)S(1)}, u32[]{:S(2)}, u32[]{:S(2)}) collective-permute-start(bf16[128,1024]{1,0:T(8,128)(2,1)S(1)} %slice.58), channel_id=1, source_target_pairs={{0,8},{2,10},{4,12},{6,14},{9,17},{11,19},{13,21},{15,23},{16,24},... | collective-permute-start | bytes 786440 | tf_op jit(solution)/shard_map/ppermute | solution.py:215
  30.5 3.8 %collective-permute-start.11 = (bf16[128,1024]{1,0:T(8,128)(2,1)S(1)}, bf16[128,1024]{1,0:T(8,128)(2,1)S(1)}, u32[]{:S(2)}, u32[]{:S(2)}) collective-permute-start(bf16[128,1024]{1,0:T(8,128)(2,1)S(1)} %slice.59), channel_id=1, source_target_pairs={{1,5},{3,7},{5,1},{7,3},{8,12},{10,14},{12,8},{14,10},{17,21},{19,... | collective-permute-start | bytes 786440 | tf_op jit(solution)/shard_map/ppermute | solution.py:215
  31.2 5.0 %collective-permute-start.7 = (bf16[256,1024]{1,0:T(8,128)(2,1)S(1)}, bf16[256,1024]{1,0:T(8,128)(2,1)S(1)}, u32[]{:S(2)}, u32[]{:S(2)}) collective-permute-start(bf16[256,1024]{1,0:T(8,128)(2,1)S(1)} %collective-permute-done.6.refs_11_), channel_id=1, source_target_pairs={{0,2},{1,3},{2,0},{3,1},{4,6},{5,7},{6,4},{7,5},{8,10},{9,11},{10,... | collective-permute-start | bytes 1572872 | tf_op jit(solution)/shard_map/ppermute | solution.py:215
  31.2 5.0 %collective-permute-start.9 = (bf16[256,1024]{1,0:T(8,128)(2,1)S(1)}, bf16[256,1024]{1,0:T(8,128)(2,1)S(1)}, u32[]{:S(2)}, u32[]{:S(2)}) collective-permute-start(bf16[256,1024]{1,0:T(8,128)(2,1)S(1)} %collective-permute-done.8.refs_13_), channel_id=1, source_target_pairs={{0,2},{1,3},{2,0},{3,1},{4,6},{5,7},{6,4},{7,5},{8,10},{9,11},{10,... | collective-permute-start | bytes 1572872 | tf_op jit(solution)/shard_map/ppermute | solution.py:215
  34.3 1.9 %collective-permute-start.13 = (bf16[128,1024]{1,0:T(8,128)(2,1)S(1)}, bf16[128,1024]{1,0:T(8,128)(2,1)S(1)}, u32[]{:S(2)}, u32[]{:S(2)}) collective-permute-start(bf16[128,1024]{1,0:T(8,128)(2,1)S(1)} %collective-permute-done.11.refs_16_), channel_id=1, source_target_pairs={{0,2},{1,3},{2,0},{3,1},{4,6},{5,7},{6,4},{7,5},{8,10},{9,11},{10,... | collective-permute-start | bytes 786440 | tf_op jit(solution)/shard_map/ppermute | solution.py:215
  59.5 11.8 %collective-permute-start.15 = (f32[16,2,256]{2,0,1:T(8,128)S(1)}, f32[16,2,256]{2,0,1:T(8,128)S(1)}, u32[]{:S(2)}, u32[]{:S(2)}) collective-permute-start(f32[16,2,256]{2,0,1:T(8,128)S(1)} %copy.17), channel_id=1, source_target_pairs={{0,4},{1,5},{2,6},{3,7},{4,0},{5,1},{6,2},{7,3},{8,12},{9,13},{10,... | collective-permute-start | bytes 98312 | tf_op jit(solution)/shard_map/ppermute | solution.py:215
  69.4 3.2 %collective-permute-start.20 = (bf16[16,2304]{1,0:T(8,128)(2,1)S(1)}, bf16[16,2304]{1,0:T(8,128)(2,1)S(1)}, u32[]{:S(2)}, u32[]{:S(2)}) collective-permute-start(bf16[16,2304]{1,0:T(8,128)(2,1)S(1)} %broadcast_select_fusion.3), channel_id=1, source_target_pairs={{0,2},{2,0},{4,6},{6,4},{8,10},{10,8},{12,14},{14,12},{16,18},{18,... | collective-permute-start | bytes 221192 | tf_op jit(solution)/shard_map/ppermute | solution.py:270
  71.3 25.6 %collective-permute-start.16 = (f32[16,256]{1,0:T(8,128)S(1)}, f32[16,256]{1,0:T(8,128)S(1)}, u32[]{:S(2)}, u32[]{:S(2)}) collective-permute-start(f32[16,256]{1,0:T(8,128)S(1)} %slice_bitcast_fusion), channel_id=1, source_target_pairs={{1,25},{3,27},{5,29},{7,31},{8,0},{10,2},{12,4},{14,6},{17,9},{19,... | collective-permute-start | bytes 49160 | tf_op jit(solution)/shard_map/ppermute | solution.py:215
  72.6 25.9 %collective-permute-start.21 = (bf16[16,2304]{1,0:T(8,128)(2,1)S(1)}, bf16[16,2304]{1,0:T(8,128)(2,1)S(1)}, u32[]{:S(2)}, u32[]{:S(2)}) collective-permute-start(bf16[16,2304]{1,0:T(8,128)(2,1)S(1)} %add_convert_fusion.7), channel_id=1, source_target_pairs={{0,4},{2,6},{4,0},{6,2},{8,12},{10,14},{12,8},{14,10},{16,20},{18,... | collective-permute-start | bytes 221192 | tf_op jit(solution)/shard_map/ppermute | solution.py:270
  96.9 4.0 %collective-permute-start.17 = (f32[32,256]{1,0:T(8,128)S(1)}, f32[32,256]{1,0:T(8,128)S(1)}, u32[]{:S(2)}, u32[]{:S(2)}) collective-permute-start(f32[32,256]{1,0:T(8,128)S(1)} %pad_maximum_fusion.1), channel_id=1, source_target_pairs={{0,1},{1,0},{2,3},{3,2},{4,5},{5,4},{6,7},{7,6},{8,9},{9,8},{10,11... | collective-permute-start | bytes 98312 | tf_op jit(solution)/shard_map/ppermute | solution.py:264
  98.5 4.4 %collective-permute-start.22 = (bf16[16,2304]{1,0:T(8,128)(2,1)S(1)}, bf16[16,2304]{1,0:T(8,128)(2,1)S(1)}, u32[]{:S(2)}, u32[]{:S(2)}) collective-permute-start(bf16[16,2304]{1,0:T(8,128)(2,1)S(1)} %add_convert_fusion.6), channel_id=1, source_target_pairs={{0,8},{2,10},{4,12},{6,14},{8,0},{10,2},{12,4},{14,6},{16,24},{18,... | collective-permute-start | bytes 221192 | tf_op jit(solution)/shard_map/ppermute | solution.py:270
  101.4 3.6 %collective-permute-start.18 = (bf16[16,4096]{1,0:T(8,128)(2,1)S(1)}, bf16[16,4096]{1,0:T(8,128)(2,1)S(1)}, u32[]{:S(2)}, u32[]{:S(2)}) collective-permute-start(bf16[16,4096]{1,0:T(8,128)(2,1)S(1)} %broadcast_select_fusion), channel_id=1, source_target_pairs={{0,2},{2,0},{4,6},{6,4},{8,10},{10,8},{12,14},{14,12},{16,18},{18,... | collective-permute-start | bytes 393224 | tf_op jit(solution)/shard_map/ppermute | solution.py:270
  103.0 6.1 %collective-permute-start.23 = (bf16[16,2304]{1,0:T(8,128)(2,1)S(1)}, bf16[16,2304]{1,0:T(8,128)(2,1)S(1)}, u32[]{:S(2)}, u32[]{:S(2)}) collective-permute-start(bf16[16,2304]{1,0:T(8,128)(2,1)S(1)} %add_convert_fusion.5), channel_id=1, source_target_pairs={{0,16},{2,18},{4,20},{6,22},{8,24},{10,26},{12,28},{14,30},{16,0},... | collective-permute-start | bytes 221192 | tf_op jit(solution)/shard_map/ppermute | solution.py:270
  105.0 5.1 %collective-permute-start.19 = (bf16[16,4096]{1,0:T(8,128)(2,1)S(1)}, bf16[16,4096]{1,0:T(8,128)(2,1)S(1)}, u32[]{:S(2)}, u32[]{:S(2)}) collective-permute-start(bf16[16,4096]{1,0:T(8,128)(2,1)S(1)} %add_convert_fusion.3), channel_id=1, source_target_pairs={{0,4},{2,6},{4,0},{6,2},{8,12},{10,14},{12,8},{14,10},{16,20},{18,... | collective-permute-start | bytes 393224 | tf_op jit(solution)/shard_map/ppermute | solution.py:270
  110.2 5.0 %collective-permute-start.24 = (bf16[16,4096]{1,0:T(8,128)(2,1)S(1)}, bf16[16,4096]{1,0:T(8,128)(2,1)S(1)}, u32[]{:S(2)}, u32[]{:S(2)}) collective-permute-start(bf16[16,4096]{1,0:T(8,128)(2,1)S(1)} %add_convert_fusion.2), channel_id=1, source_target_pairs={{0,8},{2,10},{4,12},{6,14},{8,0},{10,2},{12,4},{14,6},{16,24},{18,... | collective-permute-start | bytes 393224 | tf_op jit(solution)/shard_map/ppermute | solution.py:270
  112.2 4.3 %collective-permute-start.27 = (bf16[16,2304]{1,0:T(8,128)(2,1)S(1)}, bf16[16,2304]{1,0:T(8,128)(2,1)S(1)}, u32[]{:S(2)}, u32[]{:S(2)}) collective-permute-start(bf16[16,2304]{1,0:T(8,128)(2,1)S(1)} %add_convert_fusion.4), channel_id=1, source_target_pairs={{0,2},{2,0},{4,6},{6,4},{8,10},{10,8},{12,14},{14,12},{16,18},{18,... | collective-permute-start | bytes 221192 | tf_op jit(solution)/shard_map/ppermute | solution.py:270
  115.3 5.9 %collective-permute-start.25 = (bf16[16,4096]{1,0:T(8,128)(2,1)S(1)}, bf16[16,4096]{1,0:T(8,128)(2,1)S(1)}, u32[]{:S(2)}, u32[]{:S(2)}) collective-permute-start(bf16[16,4096]{1,0:T(8,128)(2,1)S(1)} %add_convert_fusion.1), channel_id=1, source_target_pairs={{0,16},{2,18},{4,20},{6,22},{8,24},{10,26},{12,28},{14,30},{16,0},... | collective-permute-start | bytes 393224 | tf_op jit(solution)/shard_map/ppermute | solution.py:270
  (10 other events, 154.1 us)

commit v6 on v5

--- a/solution.py
+++ b/solution.py
@@ -35,11 +35,11 @@
 
 
 def attention_body(rows, per_head, kv, stacked, blocks_in_group, *refs):
-    frozen, low_q_t, up_q, up_v, grad_out = refs[:5]
+    queries, low_q_t, up_q, up_v, grad_out = refs[:5]
     low_v = refs[5:9]
     given = refs[9:19]
     out, grad_up_q, back_q, back_v, back_v_sibling, grad_up_v = refs[19:25]
-    low_q, scores, probs, grad_s, keys, keys_t, values, values_t, grad_v = refs[25:]
+    scores, probs, grad_s, keys, keys_t, values, values_t, grad_v, grad_q = refs[25:]
     scale = float(HD) ** -0.5
     to_log2 = scale * LOG2E
     place = place_in_group(blocks_in_group)
@@ -52,10 +52,8 @@
     columns = stacked * rows
     steps = kv * per_head // stacked
     steps_per_kv = per_head // stacked
-    back_q[...] = jnp.zeros_like(back_q)
     back_v[...] = jnp.zeros_like(back_v)
     back_v_sibling[...] = jnp.zeros_like(back_v)
-    low_q[...] = low_q_t[...].T
     key_at = lax.broadcasted_iota(jnp.int32, (rows, columns), 0)
     query_at = lax.broadcasted_iota(jnp.int32, (rows, columns), 1) % rows
 
@@ -79,6 +77,8 @@
                 grad_v[at, :] = jnp.zeros((count, width_kv), F32)
 
     def finish(blocks):
+        grad_up_q[...] = (ADAPTER_SCALE * dot(low_q_t[...], grad_q[...], NT)).astype(BF16)
+        back_q[...] = ADAPTER_SCALE * dot(up_q[...], grad_q[...], NN)
         length = len(blocks) * rows
         rounded = grad_v[:length, :].astype(BF16)
         back = ADAPTER_SCALE * dot(up_v[...], rounded, NT)
@@ -99,8 +99,7 @@
             return pl.ds(pl.multiple_of((i // steps_per_kv) * HD, HD), HD)
 
         def score(i):
-            query = frozen[:, wide(i)].astype(F32) + ADAPTER_SCALE * dot(low_q[...], up_q[:, wide(i)], NN)
-            query = query.astype(BF16)
+            query = queries[:, wide(i)]
             query = jnp.concatenate([query[:, a * HD : (a + 1) * HD] for a in range(stacked)], axis=0)
             s = dot(keys[:length, kv_cols(i)], query, NT)
             own = jnp.where(key_at <= query_at, s[:rows], MASKED)
@@ -131,14 +130,8 @@
             grad_v[:length, kv_cols(i)] += dot(probs[:length, :], normed, NT)
             grad_query = dot(keys_t[kv_cols(i), :length], grad_s[:length, :], NN)
             grad_query = (grad_query * (inverse * scale)).astype(BF16)
-            back = None
             for a in range(stacked):
-                one = grad_query[:, a * rows : (a + 1) * rows]
-                grad_up_q[:, narrow(i, a)] = (ADAPTER_SCALE * dot(low_q_t[...], one, NT)).astype(BF16)
-                term = dot(up_q[:, narrow(i, a)], one, NN)
-                back = term if back is None else back + term
-            back_q[...] += ADAPTER_SCALE * back
-
+                grad_q[narrow(i, a), :] = grad_query[:, a * rows : (a + 1) * rows]
             return later
 
         top = lax.fori_loop(0, steps - 1, one_step, score(0))
@@ -155,8 +148,8 @@
                 finish(blocks)
 
 
-def attention_call(frozen, low_q_t, up_q, up_v, grad_out, low_v, given):
-    rows, width = frozen.shape
+def attention_call(queries, low_q_t, up_q, up_v, grad_out, low_v, given):
+    rows, width = queries.shape
     kv = up_v.shape[1] // HD
     rank = up_q.shape[0]
     per_head = width // HD // kv
@@ -169,7 +162,6 @@
         in_specs=[vmem] * (5 + len(low_v) + len(given)),
         out_specs=[vmem] * 6,
         scratch_shapes=[
-            pltpu.VMEM((rows, rank), BF16),
             pltpu.VMEM((reach, stacked * rows), F32),
             pltpu.VMEM((reach, stacked * rows), BF16),
             pltpu.VMEM((reach, stacked * rows), BF16),
@@ -178,6 +170,7 @@
             pltpu.VMEM((reach, kv * HD), BF16),
             pltpu.VMEM((kv, HD + ONES, reach), BF16),
             pltpu.VMEM((reach, kv * HD), F32),
+            pltpu.VMEM((width, rows), BF16),
         ],
         out_shape=[
             jax.ShapeDtypeStruct((rows, width), BF16),
@@ -191,7 +184,7 @@
         cost_estimate=pl.CostEstimate(
             flops=10 * pairs * HD, bytes_accessed=16 * rows * width, transcendentals=pairs
         ),
-    )(frozen, low_q_t, up_q, up_v, grad_out, *low_v, *given)
+    )(queries, low_q_t, up_q, up_v, grad_out, *low_v, *given)
 
 
 class Routes:
@@ -240,10 +233,12 @@
         return self.send(block, lambda s, t: s - self.half if self.upper(s, t) else None)
 
 
-def gather_blocks(routes, own):
+def gather_near(routes, own):
+    return routes.own_across_y(own), routes.up(own)
+
+
+def gather_far(routes, own, from_y, from_z):
     cut = own.shape[0] // 2
-    from_y = routes.own_across_y(own)
-    from_z = routes.up(own)
     first = routes.up(from_y[:cut])
     second = routes.within_upper(from_z[cut:])
     found = []
@@ -312,15 +307,25 @@
     blocks = GROUP // rows
     assert blocks == 8 and rows % 32 == 0
     routes = Routes(blocks)
-    given = gather_blocks(routes, jnp.concatenate((key_base, frozen_value), axis=1))
+    own = jnp.concatenate((key_base, frozen_value), axis=1)
+    near = gather_near(routes, own)
     down = jnp.concatenate((down_query, down_value), axis=1)
     part_t = lax.dot_general(down, hidden_in, (((0,), (1,)), ((), ())), preferred_element_type=F32)
     low_t = sum_over_tensor(part_t).astype(BF16)
     low_q_t = low_t[:rank]
     low_v = gather_low(routes, low_t[rank:])
+    near, low_v = lax.optimization_barrier((near, low_v))
+    given = gather_far(routes, own, *near)
+    queries = (
+        frozen_query.astype(F32)
+        + ADAPTER_SCALE
+        * lax.dot_general(
+            low_q_t, query_upper_factor, (((0,), (0,)), ((), ())), preferred_element_type=F32
+        )
+    ).astype(BF16)
 
     attention, grad_up_q, back_q, back_v, back_v_sibling, grad_up_v = attention_call(
-        frozen_query,
+        queries,
         low_q_t,
         query_upper_factor,
         value_upper_factor,

time: 125 us -> 122 us (0.976)
  Pallas kernels: 21.8 us -> 18.2 us
    pallas_call x1, Pallas kernels: 21.8 us -> 18.2 us  [attention_call(): pl.pallas_call(functools.partial(attention_body, rows, per_head, kv, stac...]
  transfers between devices with their start and end apart: 28 -> 28, of which waited for: 15 -> 16; matrix products, arithmetic and copies ran while one was open for 3% -> 2% of each run, Pallas kernels for 0% -> 0%
where the time goes in v6:
time: 122 us; the launch traced here: 121 us
  waiting for transfers between devices  49.8 us (41%)
  starting transfers between devices  44.4 us (36%)
  Pallas kernels  18.2 us (15%)
  matrix products  2.9 us (2%)
  local copies, waits for them, and re-layouts  2.65 us (2%)
  other arithmetic  1.8 us (1%)
    ppermute x16, waiting for transfers between devices, send(): return lax.ppermute(block, AXES, route)  35.3 us
    ppermute x16, starting transfers between devices, send(): return lax.ppermute(block, AXES, route)  29.5 us
    pallas_call x1, Pallas kernels, attention_call(): pl.pallas_call(functools.partial(attention_body, rows, per_head, kv, stac...  18.2 us
    ppermute x10, waiting for transfers between devices, swap(): lax.ppermute(block, 'seq', [(i, i ^ step) for i in range(lax.axis_size('s...  13.4 us
    ppermute x10, starting transfers between devices, swap(): lax.ppermute(block, 'seq', [(i, i ^ step) for i in range(lax.axis_size('s...  10 us
    ppermute x2, starting transfers between devices, sum_over_tensor(): lax.ppermute(part, 'tensor', [(i, i ^ step) for i in range(size)])  4.93 us
  transfers between devices with their start and end apart: 28, of which 16 were waited for; matrix products, arithmetic and copies ran while one was open for 2% of the time, Pallas kernels for 0%

profile of v6, /device:TPU:0, one launch (start us, length us, event | category | flops | bytes accessed | tf_op | source)
XLA Modules:
  0.0 120.9 jit_solution(3629710625527902490)
XLA Ops:
  0.7 1.5 %copy-done = bf16[256,4096]{1,0:T(8,128)(2,1)S(1)} copy-done((bf16[256,4096]{1,0:T(8,128)(2,1)S(1)}, bf16[256,4096]{1,0:T(8,128)(2,1)}, u32[]{:S(2)}) %copy-start) | copy-done | bytes 2097176
  2.2 1.7 %fusion.2 = f32[32,256]{1,0:T(8,128)S(1)} fusion(bf16[256,4096]{1,0:T(8,128)(2,1)S(1)} %copy-done, bf16[4096,16]{0,1:T(8,128)(2,1)} %param.15, bf16[4096,16]{0,1:T(8,128)(2,1)} %param.13), kind=kOutput, calls=%fused_computation.4 | convolution fusion | flops 67633152 | bytes 2392064 | tf_op jit(solution)/shard_map/dot_general | solution.py:313
  3.9 3.0 %collective-permute-start = (f32[32,256]{1,0:T(8,128)S(1)}, f32[32,256]{1,0:T(8,128)S(1)}, u32[]{:S(2)}, u32[]{:S(2)}) collective-permute-start(f32[32,256]{1,0:T(8,128)S(1)} %fusion.2), channel_id=1, source_target_pairs={{0,1},{1,0},{2,3},{3,2},{4,5},{5,4},{6,7},{7,6},{8,9},{9,8},{10,11... | collective-permute-start | bytes 98312 | tf_op jit(solution)/shard_map/ppermute | solution.py:259
  7.0 3.4 %collective-permute-start.1 = (bf16[256,1024]{1,0:T(8,128)(2,1)S(1)}, bf16[256,1024]{1,0:T(8,128)(2,1)S(1)}, u32[]{:S(2)}, u32[]{:S(2)}) collective-permute-start(bf16[256,1024]{1,0:T(8,128)(2,1)S(1)} %constant_dynamic-update-slice_fusion.refs_9_), channel_id=1, source_target_pairs={{0,4},{1,5},{2,6},{3,7},{4,0},{6,2},{8,12},{9,13},{10,14},{11,15},... | collective-permute-start | bytes 1572872 | tf_op jit(solution)/shard_map/ppermute | solution.py:208
  10.5 3.5 %collective-permute-start.2 = (bf16[256,1024]{1,0:T(8,128)(2,1)S(1)}, bf16[256,1024]{1,0:T(8,128)(2,1)S(1)}, u32[]{:S(2)}, u32[]{:S(2)}) collective-permute-start(bf16[256,1024]{1,0:T(8,128)(2,1)S(1)} %constant_dynamic-update-slice_fusion.refs_9_), channel_id=1, source_target_pairs={{0,8},{2,10},{4,12},{6,14},{9,17},{11,19},{13,21},{15,23},{16,24},... | collective-permute-start | bytes 1572872 | tf_op jit(solution)/shard_map/ppermute | solution.py:208
  16.6 2.7 %collective-permute-start.6 = (bf16[16,512]{1,0:T(8,128)(2,1)S(1)}, bf16[16,512]{1,0:T(8,128)(2,1)S(1)}, u32[]{:S(2)}, u32[]{:S(2)}) collective-permute-start(bf16[16,512]{1,0:T(8,128)(2,1)S(1)} %pad_maximum_fusion.2.refs_5_), channel_id=1, source_target_pairs={{0,12},{2,14},{4,8},{6,10},{9,21},{11,23},{13,17},{15,19},{16,28},... | collective-permute-start | bytes 49160 | tf_op jit(solution)/shard_map/ppermute | solution.py:208
  19.3 3.3 %collective-permute-done.4.refs_6_ = bf16[16,512]{1,0:T(8,128)(2,1)S(1)} collective-permute-done((bf16[16,512]{1,0:T(8,128)(2,1)S(1)}, bf16[16,512]{1,0:T(8,128)(2,1)S(1)}, u32[]{:S(2)}, u32[]{:S(2)}) %collective-permute-start.4) | collective-permute-done | bytes 16416 | tf_op jit(solution)/shard_map/ppermute | solution.py:208
  22.6 2.5 %collective-permute-done.5.refs_7_ = bf16[16,512]{1,0:T(8,128)(2,1)S(1)} collective-permute-done((bf16[16,512]{1,0:T(8,128)(2,1)S(1)}, bf16[16,512]{1,0:T(8,128)(2,1)S(1)}, u32[]{:S(2)}, u32[]{:S(2)}) %collective-permute-start.5) | collective-permute-done | bytes 16416 | tf_op jit(solution)/shard_map/ppermute | solution.py:208
  25.3 4.2 %collective-permute-start.10 = (bf16[128,1024]{1,0:T(8,128)(2,1)S(1)}, bf16[128,1024]{1,0:T(8,128)(2,1)S(1)}, u32[]{:S(2)}, u32[]{:S(2)}) collective-permute-start(bf16[128,1024]{1,0:T(8,128)(2,1)S(1)} %slice.44), channel_id=1, source_target_pairs={{0,8},{2,10},{4,12},{6,14},{9,17},{11,19},{13,21},{15,23},{16,24},... | collective-permute-start | bytes 786440 | tf_op jit(solution)/shard_map/ppermute | solution.py:208
  31.1 2.3 %collective-permute-done.10.refs_15_ = bf16[128,1024]{1,0:T(8,128)(2,1)S(1)} collective-permute-done((bf16[128,1024]{1,0:T(8,128)(2,1)S(1)}, bf16[128,1024]{1,0:T(8,128)(2,1)S(1)}, u32[]{:S(2)}, u32[]{:S(2)}) %collective-permute-start.10) | collective-permute-done | bytes 262176 | tf_op jit(solution)/shard_map/ppermute | solution.py:208
  35.4 18.2 %shard_map.128 = (bf16[256,4096]{1,0:T(8,128)(2,1)}, bf16[16,4096]{1,0:T(8,128)(2,1)S(1)}, f32[16,256]{1,0:T(8,128)S(1)}, f32[16,1024]{1,0:T(8,128)S(1)}, f32[16...) custom-call(bf16[256,4096]{1,0:T(8,128)(2,1)S(1)} %fusion.1.refs_0_, bf16[16,256]{1,0:T(8,128)(2,1)S(1)} %get-tuple-element.38.refs_1_, ...), custom_call_target="tpu_custom_call" | custom-call | flops 21474836480 | bytes 16777216 | tf_op jit(solution)/shard_map/pallas_call | solution.py:160
  55.0 10.8 %collective-permute-start.15 = (f32[16,2,256]{2,0,1:T(8,128)S(1)}, f32[16,2,256]{2,0,1:T(8,128)S(1)}, u32[]{:S(2)}, u32[]{:S(2)}) collective-permute-start(f32[16,2,256]{2,0,1:T(8,128)S(1)} %copy.17), channel_id=1, source_target_pairs={{0,4},{1,5},{2,6},{3,7},{4,0},{5,1},{6,2},{7,3},{8,12},{9,13},{10,... | collective-permute-start | bytes 98312 | tf_op jit(solution)/shard_map/ppermute | solution.py:208
  66.1 1.7 %collective-permute-done.15 = f32[16,2,256]{2,0,1:T(8,128)S(1)} collective-permute-done((f32[16,2,256]{2,0,1:T(8,128)S(1)}, f32[16,2,256]{2,0,1:T(8,128)S(1)}, u32[]{:S(2)}, u32[]{:S(2)}) %collective-permute-start.15) | collective-permute-done | bytes 32800 | tf_op jit(solution)/shard_map/ppermute | solution.py:208
  67.7 1.3 %collective-permute-start.16 = (f32[16,256]{1,0:T(8,128)S(1)}, f32[16,256]{1,0:T(8,128)S(1)}, u32[]{:S(2)}, u32[]{:S(2)}) collective-permute-start(f32[16,256]{1,0:T(8,128)S(1)} %slice_bitcast_fusion), channel_id=1, source_target_pairs={{1,25},{3,27},{5,29},{7,31},{8,0},{10,2},{12,4},{14,6},{17,9},{19,... | collective-permute-start | bytes 49160 | tf_op jit(solution)/shard_map/ppermute | solution.py:208
  69.1 2.1 %collective-permute-start.21 = (bf16[16,2304]{1,0:T(8,128)(2,1)S(1)}, bf16[16,2304]{1,0:T(8,128)(2,1)S(1)}, u32[]{:S(2)}, u32[]{:S(2)}) collective-permute-start(bf16[16,2304]{1,0:T(8,128)(2,1)S(1)} %add_convert_fusion.7), channel_id=1, source_target_pairs={{0,4},{2,6},{4,0},{6,2},{8,12},{10,14},{12,8},{14,10},{16,20},{18,... | collective-permute-start | bytes 221192 | tf_op jit(solution)/shard_map/ppermute | solution.py:265
  71.2 22.4 %collective-permute-done.16 = f32[16,256]{1,0:T(8,128)S(1)} collective-permute-done((f32[16,256]{1,0:T(8,128)S(1)}, f32[16,256]{1,0:T(8,128)S(1)}, u32[]{:S(2)}, u32[]{:S(2)}) %collective-permute-start.16) | collective-permute-done | bytes 16416 | tf_op jit(solution)/shard_map/ppermute | solution.py:208
  93.6 1.9 %collective-permute-start.17 = (f32[32,256]{1,0:T(8,128)S(1)}, f32[32,256]{1,0:T(8,128)S(1)}, u32[]{:S(2)}, u32[]{:S(2)}) collective-permute-start(f32[32,256]{1,0:T(8,128)S(1)} %pad_maximum_fusion.1), channel_id=1, source_target_pairs={{0,1},{1,0},{2,3},{3,2},{4,5},{5,4},{6,7},{7,6},{8,9},{9,8},{10,11... | collective-permute-start | bytes 98312 | tf_op jit(solution)/shard_map/ppermute | solution.py:259
  98.2 1.8 %collective-permute-done.22 = bf16[16,2304]{1,0:T(8,128)(2,1)S(1)} collective-permute-done((bf16[16,2304]{1,0:T(8,128)(2,1)S(1)}, bf16[16,2304]{1,0:T(8,128)(2,1)S(1)}, u32[]{:S(2)}, u32[]{:S(2)}) %collective-permute-start.22) | collective-permute-done | bytes 73760 | tf_op jit(solution)/shard_map/ppermute | solution.py:265
  100.0 2.0 %collective-permute-start.23 = (bf16[16,2304]{1,0:T(8,128)(2,1)S(1)}, bf16[16,2304]{1,0:T(8,128)(2,1)S(1)}, u32[]{:S(2)}, u32[]{:S(2)}) collective-permute-start(bf16[16,2304]{1,0:T(8,128)(2,1)S(1)} %add_convert_fusion.5), channel_id=1, source_target_pairs={{0,16},{2,18},{4,20},{6,22},{8,24},{10,26},{12,28},{14,30},{16,0},... | collective-permute-start | bytes 221192 | tf_op jit(solution)/shard_map/ppermute | solution.py:265
  102.1 2.1 %collective-permute-start.19 = (bf16[16,4096]{1,0:T(8,128)(2,1)S(1)}, bf16[16,4096]{1,0:T(8,128)(2,1)S(1)}, u32[]{:S(2)}, u32[]{:S(2)}) collective-permute-start(bf16[16,4096]{1,0:T(8,128)(2,1)S(1)} %add_convert_fusion.3), channel_id=1, source_target_pairs={{0,4},{2,6},{4,0},{6,2},{8,12},{10,14},{12,8},{14,10},{16,20},{18,... | collective-permute-start | bytes 393224 | tf_op jit(solution)/shard_map/ppermute | solution.py:265
  104.1 2.0 %collective-permute-done.23 = bf16[16,2304]{1,0:T(8,128)(2,1)S(1)} collective-permute-done((bf16[16,2304]{1,0:T(8,128)(2,1)S(1)}, bf16[16,2304]{1,0:T(8,128)(2,1)S(1)}, u32[]{:S(2)}, u32[]{:S(2)}) %collective-permute-start.23) | collective-permute-done | bytes 73760 | tf_op jit(solution)/shard_map/ppermute | solution.py:265
  107.1 2.1 %collective-permute-start.24 = (bf16[16,4096]{1,0:T(8,128)(2,1)S(1)}, bf16[16,4096]{1,0:T(8,128)(2,1)S(1)}, u32[]{:S(2)}, u32[]{:S(2)}) collective-permute-start(bf16[16,4096]{1,0:T(8,128)(2,1)S(1)} %add_convert_fusion.2), channel_id=1, source_target_pairs={{0,8},{2,10},{4,12},{6,14},{8,0},{10,2},{12,4},{14,6},{16,24},{18,... | collective-permute-start | bytes 393224 | tf_op jit(solution)/shard_map/ppermute | solution.py:265
  109.2 3.4 %collective-permute-done.24 = bf16[16,4096]{1,0:T(8,128)(2,1)S(1)} collective-permute-done((bf16[16,4096]{1,0:T(8,128)(2,1)S(1)}, bf16[16,4096]{1,0:T(8,128)(2,1)S(1)}, u32[]{:S(2)}, u32[]{:S(2)}) %collective-permute-start.24) | collective-permute-done | bytes 131104 | tf_op jit(solution)/shard_map/ppermute | solution.py:265
  113.3 5.3 %collective-permute-done.25 = bf16[16,4096]{1,0:T(8,128)(2,1)S(1)} collective-permute-done((bf16[16,4096]{1,0:T(8,128)(2,1)S(1)}, bf16[16,4096]{1,0:T(8,128)(2,1)S(1)}, u32[]{:S(2)}, u32[]{:S(2)}) %collective-permute-start.25) | collective-permute-done | bytes 131104 | tf_op jit(solution)/shard_map/ppermute | solution.py:265
  (81 shorter events, 14.5 us)
Async XLA Ops:
  3.9 10.1 %collective-permute-start = (f32[32,256]{1,0:T(8,128)S(1)}, f32[32,256]{1,0:T(8,128)S(1)}, u32[]{:S(2)}, u32[]{:S(2)}) collective-permute-start(f32[32,256]{1,0:T(8,128)S(1)} %fusion.2), channel_id=1, source_target_pairs={{0,1},{1,0},{2,3},{3,2},{4,5},{5,4},{6,7},{7,6},{8,9},{9,8},{10,11... | collective-permute-start | bytes 98312 | tf_op jit(solution)/shard_map/ppermute | solution.py:259
  7.0 18.3 %collective-permute-start.1 = (bf16[256,1024]{1,0:T(8,128)(2,1)S(1)}, bf16[256,1024]{1,0:T(8,128)(2,1)S(1)}, u32[]{:S(2)}, u32[]{:S(2)}) collective-permute-start(bf16[256,1024]{1,0:T(8,128)(2,1)S(1)} %constant_dynamic-update-slice_fusion.refs_9_), channel_id=1, source_target_pairs={{0,4},{1,5},{2,6},{3,7},{4,0},{6,2},{8,12},{9,13},{10,14},{11,15},... | collective-permute-start | bytes 1572872 | tf_op jit(solution)/shard_map/ppermute | solution.py:208
  10.5 14.8 %collective-permute-start.2 = (bf16[256,1024]{1,0:T(8,128)(2,1)S(1)}, bf16[256,1024]{1,0:T(8,128)(2,1)S(1)}, u32[]{:S(2)}, u32[]{:S(2)}) collective-permute-start(bf16[256,1024]{1,0:T(8,128)(2,1)S(1)} %constant_dynamic-update-slice_fusion.refs_9_), channel_id=1, source_target_pairs={{0,8},{2,10},{4,12},{6,14},{9,17},{11,19},{13,21},{15,23},{16,24},... | collective-permute-start | bytes 1572872 | tf_op jit(solution)/shard_map/ppermute | solution.py:208
  15.3 7.4 %collective-permute-start.4 = (bf16[16,512]{1,0:T(8,128)(2,1)S(1)}, bf16[16,512]{1,0:T(8,128)(2,1)S(1)}, u32[]{:S(2)}, u32[]{:S(2)}) collective-permute-start(bf16[16,512]{1,0:T(8,128)(2,1)S(1)} %pad_maximum_fusion.2.refs_5_), channel_id=1, source_target_pairs={{0,4},{1,5},{2,6},{3,7},{4,0},{5,1},{6,2},{7,3},{8,12},{9,13},{10,... | collective-permute-start | bytes 49160 | tf_op jit(solution)/shard_map/ppermute | solution.py:208
  15.3 9.8 %collective-permute-start.5 = (bf16[16,512]{1,0:T(8,128)(2,1)S(1)}, bf16[16,512]{1,0:T(8,128)(2,1)S(1)}, u32[]{:S(2)}, u32[]{:S(2)}) collective-permute-start(bf16[16,512]{1,0:T(8,128)(2,1)S(1)} %pad_maximum_fusion.2.refs_5_), channel_id=1, source_target_pairs={{0,8},{2,10},{4,12},{6,14},{9,17},{11,19},{13,21},{15,23},{16,24},... | collective-permute-start | bytes 49160 | tf_op jit(solution)/shard_map/ppermute | solution.py:208
  16.6 8.7 %collective-permute-start.6 = (bf16[16,512]{1,0:T(8,128)(2,1)S(1)}, bf16[16,512]{1,0:T(8,128)(2,1)S(1)}, u32[]{:S(2)}, u32[]{:S(2)}) collective-permute-start(bf16[16,512]{1,0:T(8,128)(2,1)S(1)} %pad_maximum_fusion.2.refs_5_), channel_id=1, source_target_pairs={{0,12},{2,14},{4,8},{6,10},{9,21},{11,23},{13,17},{15,19},{16,28},... | collective-permute-start | bytes 49160 | tf_op jit(solution)/shard_map/ppermute | solution.py:208
  25.3 8.1 %collective-permute-start.10 = (bf16[128,1024]{1,0:T(8,128)(2,1)S(1)}, bf16[128,1024]{1,0:T(8,128)(2,1)S(1)}, u32[]{:S(2)}, u32[]{:S(2)}) collective-permute-start(bf16[128,1024]{1,0:T(8,128)(2,1)S(1)} %slice.44), channel_id=1, source_target_pairs={{0,8},{2,10},{4,12},{6,14},{9,17},{11,19},{13,21},{15,23},{16,24},... | collective-permute-start | bytes 786440 | tf_op jit(solution)/shard_map/ppermute | solution.py:208
  29.6 3.8 %collective-permute-start.11 = (bf16[128,1024]{1,0:T(8,128)(2,1)S(1)}, bf16[128,1024]{1,0:T(8,128)(2,1)S(1)}, u32[]{:S(2)}, u32[]{:S(2)}) collective-permute-start(bf16[128,1024]{1,0:T(8,128)(2,1)S(1)} %slice.45), channel_id=1, source_target_pairs={{1,5},{3,7},{5,1},{7,3},{8,12},{10,14},{12,8},{14,10},{17,21},{19,... | collective-permute-start | bytes 786440 | tf_op jit(solution)/shard_map/ppermute | solution.py:208
  30.4 4.3 %collective-permute-start.7 = (bf16[256,1024]{1,0:T(8,128)(2,1)S(1)}, bf16[256,1024]{1,0:T(8,128)(2,1)S(1)}, u32[]{:S(2)}, u32[]{:S(2)}) collective-permute-start(bf16[256,1024]{1,0:T(8,128)(2,1)S(1)} %constant_dynamic-update-slice_fusion.refs_9_), channel_id=1, source_target_pairs={{0,2},{1,3},{2,0},{3,1},{4,6},{5,7},{6,4},{7,5},{8,10},{9,11},{10,... | collective-permute-start | bytes 1572872 | tf_op jit(solution)/shard_map/ppermute | solution.py:208
  30.5 4.8 %collective-permute-start.8 = (bf16[256,1024]{1,0:T(8,128)(2,1)S(1)}, bf16[256,1024]{1,0:T(8,128)(2,1)S(1)}, u32[]{:S(2)}, u32[]{:S(2)}) collective-permute-start(bf16[256,1024]{1,0:T(8,128)(2,1)S(1)} %collective-permute-done.1.refs_11_), channel_id=1, source_target_pairs={{0,2},{1,3},{2,0},{3,1},{4,6},{5,7},{6,4},{7,5},{8,10},{9,11},{10,... | collective-permute-start | bytes 1572872 | tf_op jit(solution)/shard_map/ppermute | solution.py:208
  31.0 4.3 %collective-permute-start.9 = (bf16[256,1024]{1,0:T(8,128)(2,1)S(1)}, bf16[256,1024]{1,0:T(8,128)(2,1)S(1)}, u32[]{:S(2)}, u32[]{:S(2)}) collective-permute-start(bf16[256,1024]{1,0:T(8,128)(2,1)S(1)} %collective-permute-done.2.refs_13_), channel_id=1, source_target_pairs={{0,2},{1,3},{2,0},{3,1},{4,6},{5,7},{6,4},{7,5},{8,10},{9,11},{10,... | collective-permute-start | bytes 1572872 | tf_op jit(solution)/shard_map/ppermute | solution.py:208
  33.4 1.9 %collective-permute-start.13 = (bf16[128,1024]{1,0:T(8,128)(2,1)S(1)}, bf16[128,1024]{1,0:T(8,128)(2,1)S(1)}, u32[]{:S(2)}, u32[]{:S(2)}) collective-permute-start(bf16[128,1024]{1,0:T(8,128)(2,1)S(1)} %collective-permute-done.11.refs_16_), channel_id=1, source_target_pairs={{0,2},{1,3},{2,0},{3,1},{4,6},{5,7},{6,4},{7,5},{8,10},{9,11},{10,... | collective-permute-start | bytes 786440 | tf_op jit(solution)/shard_map/ppermute | solution.py:208
  55.0 12.7 %collective-permute-start.15 = (f32[16,2,256]{2,0,1:T(8,128)S(1)}, f32[16,2,256]{2,0,1:T(8,128)S(1)}, u32[]{:S(2)}, u32[]{:S(2)}) collective-permute-start(f32[16,2,256]{2,0,1:T(8,128)S(1)} %copy.17), channel_id=1, source_target_pairs={{0,4},{1,5},{2,6},{3,7},{4,0},{5,1},{6,2},{7,3},{8,12},{9,13},{10,... | collective-permute-start | bytes 98312 | tf_op jit(solution)/shard_map/ppermute | solution.py:208
  65.9 3.2 %collective-permute-start.20 = (bf16[16,2304]{1,0:T(8,128)(2,1)S(1)}, bf16[16,2304]{1,0:T(8,128)(2,1)S(1)}, u32[]{:S(2)}, u32[]{:S(2)}) collective-permute-start(bf16[16,2304]{1,0:T(8,128)(2,1)S(1)} %broadcast_select_fusion.3), channel_id=1, source_target_pairs={{0,2},{2,0},{4,6},{6,4},{8,10},{10,8},{12,14},{14,12},{16,18},{18,... | collective-permute-start | bytes 221192 | tf_op jit(solution)/shard_map/ppermute | solution.py:265
  67.7 25.8 %collective-permute-start.16 = (f32[16,256]{1,0:T(8,128)S(1)}, f32[16,256]{1,0:T(8,128)S(1)}, u32[]{:S(2)}, u32[]{:S(2)}) collective-permute-start(f32[16,256]{1,0:T(8,128)S(1)} %slice_bitcast_fusion), channel_id=1, source_target_pairs={{1,25},{3,27},{5,29},{7,31},{8,0},{10,2},{12,4},{14,6},{17,9},{19,... | collective-permute-start | bytes 49160 | tf_op jit(solution)/shard_map/ppermute | solution.py:208
  69.1 26.4 %collective-permute-start.21 = (bf16[16,2304]{1,0:T(8,128)(2,1)S(1)}, bf16[16,2304]{1,0:T(8,128)(2,1)S(1)}, u32[]{:S(2)}, u32[]{:S(2)}) collective-permute-start(bf16[16,2304]{1,0:T(8,128)(2,1)S(1)} %add_convert_fusion.7), channel_id=1, source_target_pairs={{0,4},{2,6},{4,0},{6,2},{8,12},{10,14},{12,8},{14,10},{16,20},{18,... | collective-permute-start | bytes 221192 | tf_op jit(solution)/shard_map/ppermute | solution.py:265
  93.6 4.0 %collective-permute-start.17 = (f32[32,256]{1,0:T(8,128)S(1)}, f32[32,256]{1,0:T(8,128)S(1)}, u32[]{:S(2)}, u32[]{:S(2)}) collective-permute-start(f32[32,256]{1,0:T(8,128)S(1)} %pad_maximum_fusion.1), channel_id=1, source_target_pairs={{0,1},{1,0},{2,3},{3,2},{4,5},{5,4},{6,7},{7,6},{8,9},{9,8},{10,11... | collective-permute-start | bytes 98312 | tf_op jit(solution)/shard_map/ppermute | solution.py:259
  95.6 4.4 %collective-permute-start.22 = (bf16[16,2304]{1,0:T(8,128)(2,1)S(1)}, bf16[16,2304]{1,0:T(8,128)(2,1)S(1)}, u32[]{:S(2)}, u32[]{:S(2)}) collective-permute-start(bf16[16,2304]{1,0:T(8,128)(2,1)S(1)} %add_convert_fusion.6), channel_id=1, source_target_pairs={{0,8},{2,10},{4,12},{6,14},{8,0},{10,2},{12,4},{14,6},{16,24},{18,... | collective-permute-start | bytes 221192 | tf_op jit(solution)/shard_map/ppermute | solution.py:265
  98.1 3.9 %collective-permute-start.18 = (bf16[16,4096]{1,0:T(8,128)(2,1)S(1)}, bf16[16,4096]{1,0:T(8,128)(2,1)S(1)}, u32[]{:S(2)}, u32[]{:S(2)}) collective-permute-start(bf16[16,4096]{1,0:T(8,128)(2,1)S(1)} %broadcast_select_fusion), channel_id=1, source_target_pairs={{0,2},{2,0},{4,6},{6,4},{8,10},{10,8},{12,14},{14,12},{16,18},{18,... | collective-permute-start | bytes 393224 | tf_op jit(solution)/shard_map/ppermute | solution.py:265
  100.0 6.1 %collective-permute-start.23 = (bf16[16,2304]{1,0:T(8,128)(2,1)S(1)}, bf16[16,2304]{1,0:T(8,128)(2,1)S(1)}, u32[]{:S(2)}, u32[]{:S(2)}) collective-permute-start(bf16[16,2304]{1,0:T(8,128)(2,1)S(1)} %add_convert_fusion.5), channel_id=1, source_target_pairs={{0,16},{2,18},{4,20},{6,22},{8,24},{10,26},{12,28},{14,30},{16,0},... | collective-permute-start | bytes 221192 | tf_op jit(solution)/shard_map/ppermute | solution.py:265
  102.1 5.0 %collective-permute-start.19 = (bf16[16,4096]{1,0:T(8,128)(2,1)S(1)}, bf16[16,4096]{1,0:T(8,128)(2,1)S(1)}, u32[]{:S(2)}, u32[]{:S(2)}) collective-permute-start(bf16[16,4096]{1,0:T(8,128)(2,1)S(1)} %add_convert_fusion.3), channel_id=1, source_target_pairs={{0,4},{2,6},{4,0},{6,2},{8,12},{10,14},{12,8},{14,10},{16,20},{18,... | collective-permute-start | bytes 393224 | tf_op jit(solution)/shard_map/ppermute | solution.py:265
  107.1 5.4 %collective-permute-start.24 = (bf16[16,4096]{1,0:T(8,128)(2,1)S(1)}, bf16[16,4096]{1,0:T(8,128)(2,1)S(1)}, u32[]{:S(2)}, u32[]{:S(2)}) collective-permute-start(bf16[16,4096]{1,0:T(8,128)(2,1)S(1)} %add_convert_fusion.2), channel_id=1, source_target_pairs={{0,8},{2,10},{4,12},{6,14},{8,0},{10,2},{12,4},{14,6},{16,24},{18,... | collective-permute-start | bytes 393224 | tf_op jit(solution)/shard_map/ppermute | solution.py:265
  109.2 4.1 %collective-permute-start.27 = (bf16[16,2304]{1,0:T(8,128)(2,1)S(1)}, bf16[16,2304]{1,0:T(8,128)(2,1)S(1)}, u32[]{:S(2)}, u32[]{:S(2)}) collective-permute-start(bf16[16,2304]{1,0:T(8,128)(2,1)S(1)} %add_convert_fusion.4), channel_id=1, source_target_pairs={{0,2},{2,0},{4,6},{6,4},{8,10},{10,8},{12,14},{14,12},{16,18},{18,... | collective-permute-start | bytes 221192 | tf_op jit(solution)/shard_map/ppermute | solution.py:265
  112.6 5.9 %collective-permute-start.25 = (bf16[16,4096]{1,0:T(8,128)(2,1)S(1)}, bf16[16,4096]{1,0:T(8,128)(2,1)S(1)}, u32[]{:S(2)}, u32[]{:S(2)}) collective-permute-start(bf16[16,4096]{1,0:T(8,128)(2,1)S(1)} %add_convert_fusion.1), channel_id=1, source_target_pairs={{0,16},{2,18},{4,20},{6,22},{8,24},{10,26},{12,28},{14,30},{16,0},... | collective-permute-start | bytes 393224 | tf_op jit(solution)/shard_map/ppermute | solution.py:265
  (11 other events, 97.7 us)

commit v7 on v6

--- a/solution.py
+++ b/solution.py
@@ -314,8 +314,6 @@
     low_t = sum_over_tensor(part_t).astype(BF16)
     low_q_t = low_t[:rank]
     low_v = gather_low(routes, low_t[rank:])
-    near, low_v = lax.optimization_barrier((near, low_v))
-    given = gather_far(routes, own, *near)
     queries = (
         frozen_query.astype(F32)
         + ADAPTER_SCALE
@@ -323,6 +321,8 @@
             low_q_t, query_upper_factor, (((0,), (0,)), ((), ())), preferred_element_type=F32
         )
     ).astype(BF16)
+    near, low_v, queries = lax.optimization_barrier((near, low_v, queries))
+    given = gather_far(routes, own, *near)
 
     attention, grad_up_q, back_q, back_v, back_v_sibling, grad_up_v = attention_call(
         queries,

time: 122 us -> 122 us (level)
  no operation moved by 1% of the time
where the time goes in v7:
time: 122 us; the launch traced here: 121 us
  waiting for transfers between devices  50.9 us (42%)
  starting transfers between devices  43.8 us (36%)
  Pallas kernels  18.2 us (15%)
  matrix products  2.89 us (2%)
  local copies, waits for them, and re-layouts  2.65 us (2%)
  other arithmetic  1.8 us (1%)
    ppermute x16, waiting for transfers between devices, send(): return lax.ppermute(block, AXES, route)  35.4 us
    ppermute x16, starting transfers between devices, send(): return lax.ppermute(block, AXES, route)  29.3 us
    pallas_call x1, Pallas kernels, attention_call(): pl.pallas_call(functools.partial(attention_body, rows, per_head, kv, stac...  18.2 us
    ppermute x10, waiting for transfers between devices, swap(): lax.ppermute(block, 'seq', [(i, i ^ step) for i in range(lax.axis_size('s...  14.3 us
    ppermute x10, starting transfers between devices, swap(): lax.ppermute(block, 'seq', [(i, i ^ step) for i in range(lax.axis_size('s...  9.47 us
    ppermute x2, starting transfers between devices, sum_over_tensor(): lax.ppermute(part, 'tensor', [(i, i ^ step) for i in range(size)])  5.06 us
  transfers between devices with their start and end apart: 28, of which 16 were waited for; matrix products, arithmetic and copies ran while one was open for 2% of the time, Pallas kernels for 0%

profile of v7, /device:TPU:0, one launch (start us, length us, event | category | flops | bytes accessed | tf_op | source)
XLA Modules:
  0.0 121.3 jit_solution(17027917695814625288)
XLA Ops:
  0.7 1.5 %copy-done = bf16[256,4096]{1,0:T(8,128)(2,1)S(1)} copy-done((bf16[256,4096]{1,0:T(8,128)(2,1)S(1)}, bf16[256,4096]{1,0:T(8,128)(2,1)}, u32[]{:S(2)}) %copy-start) | copy-done | bytes 2097176
  2.2 1.7 %fusion.2 = f32[32,256]{1,0:T(8,128)S(1)} fusion(bf16[256,4096]{1,0:T(8,128)(2,1)S(1)} %copy-done, bf16[4096,16]{0,1:T(8,128)(2,1)} %param.15, bf16[4096,16]{0,1:T(8,128)(2,1)} %param.13), kind=kOutput, calls=%fused_computation.4 | convolution fusion | flops 67633152 | bytes 2392064 | tf_op jit(solution)/shard_map/dot_general | solution.py:313
  3.9 3.0 %collective-permute-start.2 = (f32[32,256]{1,0:T(8,128)S(1)}, f32[32,256]{1,0:T(8,128)S(1)}, u32[]{:S(2)}, u32[]{:S(2)}) collective-permute-start(f32[32,256]{1,0:T(8,128)S(1)} %fusion.2), channel_id=1, source_target_pairs={{0,1},{1,0},{2,3},{3,2},{4,5},{5,4},{6,7},{7,6},{8,9},{9,8},{10,11... | collective-permute-start | bytes 98312 | tf_op jit(solution)/shard_map/ppermute | solution.py:259
  7.0 3.4 %collective-permute-start = (bf16[256,1024]{1,0:T(8,128)(2,1)S(1)}, bf16[256,1024]{1,0:T(8,128)(2,1)S(1)}, u32[]{:S(2)}, u32[]{:S(2)}) collective-permute-start(bf16[256,1024]{1,0:T(8,128)(2,1)S(1)} %constant_dynamic-update-slice_fusion.refs_9_), channel_id=1, source_target_pairs={{0,4},{1,5},{2,6},{3,7},{4,0},{6,2},{8,12},{9,13},{10,14},{11,15},... | collective-permute-start | bytes 1572872 | tf_op jit(solution)/shard_map/ppermute | solution.py:208
  10.5 3.5 %collective-permute-start.1 = (bf16[256,1024]{1,0:T(8,128)(2,1)S(1)}, bf16[256,1024]{1,0:T(8,128)(2,1)S(1)}, u32[]{:S(2)}, u32[]{:S(2)}) collective-permute-start(bf16[256,1024]{1,0:T(8,128)(2,1)S(1)} %constant_dynamic-update-slice_fusion.refs_9_), channel_id=1, source_target_pairs={{0,8},{2,10},{4,12},{6,14},{9,17},{11,19},{13,21},{15,23},{16,24},... | collective-permute-start | bytes 1572872 | tf_op jit(solution)/shard_map/ppermute | solution.py:208
  15.3 1.4 %collective-permute-start.5 = (bf16[16,512]{1,0:T(8,128)(2,1)S(1)}, bf16[16,512]{1,0:T(8,128)(2,1)S(1)}, u32[]{:S(2)}, u32[]{:S(2)}) collective-permute-start(bf16[16,512]{1,0:T(8,128)(2,1)S(1)} %pad_maximum_fusion.2.refs_5_), channel_id=1, source_target_pairs={{0,8},{2,10},{4,12},{6,14},{9,17},{11,19},{13,21},{15,23},{16,24},... | collective-permute-start | bytes 49160 | tf_op jit(solution)/shard_map/ppermute | solution.py:208
  16.7 2.6 %collective-permute-start.6 = (bf16[16,512]{1,0:T(8,128)(2,1)S(1)}, bf16[16,512]{1,0:T(8,128)(2,1)S(1)}, u32[]{:S(2)}, u32[]{:S(2)}) collective-permute-start(bf16[16,512]{1,0:T(8,128)(2,1)S(1)} %pad_maximum_fusion.2.refs_5_), channel_id=1, source_target_pairs={{0,12},{2,14},{4,8},{6,10},{9,21},{11,23},{13,17},{15,19},{16,28},... | collective-permute-start | bytes 49160 | tf_op jit(solution)/shard_map/ppermute | solution.py:208
  20.1 2.6 %collective-permute-done.4.refs_6_ = bf16[16,512]{1,0:T(8,128)(2,1)S(1)} collective-permute-done((bf16[16,512]{1,0:T(8,128)(2,1)S(1)}, bf16[16,512]{1,0:T(8,128)(2,1)S(1)}, u32[]{:S(2)}, u32[]{:S(2)}) %collective-permute-start.4) | collective-permute-done | bytes 16416 | tf_op jit(solution)/shard_map/ppermute | solution.py:208
  22.6 2.5 %collective-permute-done.5.refs_7_ = bf16[16,512]{1,0:T(8,128)(2,1)S(1)} collective-permute-done((bf16[16,512]{1,0:T(8,128)(2,1)S(1)}, bf16[16,512]{1,0:T(8,128)(2,1)S(1)}, u32[]{:S(2)}, u32[]{:S(2)}) %collective-permute-start.5) | collective-permute-done | bytes 16416 | tf_op jit(solution)/shard_map/ppermute | solution.py:208
  25.3 4.2 %collective-permute-start.10 = (bf16[128,1024]{1,0:T(8,128)(2,1)S(1)}, bf16[128,1024]{1,0:T(8,128)(2,1)S(1)}, u32[]{:S(2)}, u32[]{:S(2)}) collective-permute-start(bf16[128,1024]{1,0:T(8,128)(2,1)S(1)} %slice.44), channel_id=1, source_target_pairs={{0,8},{2,10},{4,12},{6,14},{9,17},{11,19},{13,21},{15,23},{16,24},... | collective-permute-start | bytes 786440 | tf_op jit(solution)/shard_map/ppermute | solution.py:208
  30.8 2.6 %collective-permute-done.10.refs_15_ = bf16[128,1024]{1,0:T(8,128)(2,1)S(1)} collective-permute-done((bf16[128,1024]{1,0:T(8,128)(2,1)S(1)}, bf16[128,1024]{1,0:T(8,128)(2,1)S(1)}, u32[]{:S(2)}, u32[]{:S(2)}) %collective-permute-start.10) | collective-permute-done | bytes 262176 | tf_op jit(solution)/shard_map/ppermute | solution.py:208
  35.4 18.2 %shard_map.128 = (bf16[256,4096]{1,0:T(8,128)(2,1)}, bf16[16,4096]{1,0:T(8,128)(2,1)S(1)}, f32[16,256]{1,0:T(8,128)S(1)}, f32[16,1024]{1,0:T(8,128)S(1)}, f32[16...) custom-call(bf16[256,4096]{1,0:T(8,128)(2,1)S(1)} %fusion.1.refs_0_, bf16[16,256]{1,0:T(8,128)(2,1)S(1)} %get-tuple-element.39.refs_1_, ...), custom_call_target="tpu_custom_call" | custom-call | flops 21474836480 | bytes 16777216 | tf_op jit(solution)/shard_map/pallas_call | solution.py:160
  55.0 10.8 %collective-permute-start.15 = (f32[16,2,256]{2,0,1:T(8,128)S(1)}, f32[16,2,256]{2,0,1:T(8,128)S(1)}, u32[]{:S(2)}, u32[]{:S(2)}) collective-permute-start(f32[16,2,256]{2,0,1:T(8,128)S(1)} %copy.17), channel_id=1, source_target_pairs={{0,4},{1,5},{2,6},{3,7},{4,0},{5,1},{6,2},{7,3},{8,12},{9,13},{10,... | collective-permute-start | bytes 98312 | tf_op jit(solution)/shard_map/ppermute | solution.py:208
  66.1 1.7 %collective-permute-done.15 = f32[16,2,256]{2,0,1:T(8,128)S(1)} collective-permute-done((f32[16,2,256]{2,0,1:T(8,128)S(1)}, f32[16,2,256]{2,0,1:T(8,128)S(1)}, u32[]{:S(2)}, u32[]{:S(2)}) %collective-permute-start.15) | collective-permute-done | bytes 32800 | tf_op jit(solution)/shard_map/ppermute | solution.py:208
  69.1 2.1 %collective-permute-start.21 = (bf16[16,2304]{1,0:T(8,128)(2,1)S(1)}, bf16[16,2304]{1,0:T(8,128)(2,1)S(1)}, u32[]{:S(2)}, u32[]{:S(2)}) collective-permute-start(bf16[16,2304]{1,0:T(8,128)(2,1)S(1)} %add_convert_fusion.7), channel_id=1, source_target_pairs={{0,4},{2,6},{4,0},{6,2},{8,12},{10,14},{12,8},{14,10},{16,20},{18,... | collective-permute-start | bytes 221192 | tf_op jit(solution)/shard_map/ppermute | solution.py:265
  71.2 22.3 %collective-permute-done.16 = f32[16,256]{1,0:T(8,128)S(1)} collective-permute-done((f32[16,256]{1,0:T(8,128)S(1)}, f32[16,256]{1,0:T(8,128)S(1)}, u32[]{:S(2)}, u32[]{:S(2)}) %collective-permute-start.16) | collective-permute-done | bytes 16416 | tf_op jit(solution)/shard_map/ppermute | solution.py:208
  93.5 2.1 %collective-permute-start.17 = (f32[32,256]{1,0:T(8,128)S(1)}, f32[32,256]{1,0:T(8,128)S(1)}, u32[]{:S(2)}, u32[]{:S(2)}) collective-permute-start(f32[32,256]{1,0:T(8,128)S(1)} %pad_maximum_fusion.1), channel_id=1, source_target_pairs={{0,1},{1,0},{2,3},{3,2},{4,5},{5,4},{6,7},{7,6},{8,9},{9,8},{10,11... | collective-permute-start | bytes 98312 | tf_op jit(solution)/shard_map/ppermute | solution.py:259
  98.0 1.9 %collective-permute-done.22 = bf16[16,2304]{1,0:T(8,128)(2,1)S(1)} collective-permute-done((bf16[16,2304]{1,0:T(8,128)(2,1)S(1)}, bf16[16,2304]{1,0:T(8,128)(2,1)S(1)}, u32[]{:S(2)}, u32[]{:S(2)}) %collective-permute-start.22) | collective-permute-done | bytes 73760 | tf_op jit(solution)/shard_map/ppermute | solution.py:265
  100.0 2.0 %collective-permute-start.23 = (bf16[16,2304]{1,0:T(8,128)(2,1)S(1)}, bf16[16,2304]{1,0:T(8,128)(2,1)S(1)}, u32[]{:S(2)}, u32[]{:S(2)}) collective-permute-start(bf16[16,2304]{1,0:T(8,128)(2,1)S(1)} %add_convert_fusion.5), channel_id=1, source_target_pairs={{0,16},{2,18},{4,20},{6,22},{8,24},{10,26},{12,28},{14,30},{16,0},... | collective-permute-start | bytes 221192 | tf_op jit(solution)/shard_map/ppermute | solution.py:265
  102.1 2.1 %collective-permute-start.19 = (bf16[16,4096]{1,0:T(8,128)(2,1)S(1)}, bf16[16,4096]{1,0:T(8,128)(2,1)S(1)}, u32[]{:S(2)}, u32[]{:S(2)}) collective-permute-start(bf16[16,4096]{1,0:T(8,128)(2,1)S(1)} %add_convert_fusion.3), channel_id=1, source_target_pairs={{0,4},{2,6},{4,0},{6,2},{8,12},{10,14},{12,8},{14,10},{16,20},{18,... | collective-permute-start | bytes 393224 | tf_op jit(solution)/shard_map/ppermute | solution.py:265
  104.1 2.0 %collective-permute-done.23 = bf16[16,2304]{1,0:T(8,128)(2,1)S(1)} collective-permute-done((bf16[16,2304]{1,0:T(8,128)(2,1)S(1)}, bf16[16,2304]{1,0:T(8,128)(2,1)S(1)}, u32[]{:S(2)}, u32[]{:S(2)}) %collective-permute-start.23) | collective-permute-done | bytes 73760 | tf_op jit(solution)/shard_map/ppermute | solution.py:265
  107.1 2.1 %collective-permute-start.24 = (bf16[16,4096]{1,0:T(8,128)(2,1)S(1)}, bf16[16,4096]{1,0:T(8,128)(2,1)S(1)}, u32[]{:S(2)}, u32[]{:S(2)}) collective-permute-start(bf16[16,4096]{1,0:T(8,128)(2,1)S(1)} %add_convert_fusion.2), channel_id=1, source_target_pairs={{0,8},{2,10},{4,12},{6,14},{8,0},{10,2},{12,4},{14,6},{16,24},{18,... | collective-permute-start | bytes 393224 | tf_op jit(solution)/shard_map/ppermute | solution.py:265
  109.2 3.8 %collective-permute-done.24 = bf16[16,4096]{1,0:T(8,128)(2,1)S(1)} collective-permute-done((bf16[16,4096]{1,0:T(8,128)(2,1)S(1)}, bf16[16,4096]{1,0:T(8,128)(2,1)S(1)}, u32[]{:S(2)}, u32[]{:S(2)}) %collective-permute-start.24) | collective-permute-done | bytes 131104 | tf_op jit(solution)/shard_map/ppermute | solution.py:265
  113.3 5.7 %collective-permute-done.25 = bf16[16,4096]{1,0:T(8,128)(2,1)S(1)} collective-permute-done((bf16[16,4096]{1,0:T(8,128)(2,1)S(1)}, bf16[16,4096]{1,0:T(8,128)(2,1)S(1)}, u32[]{:S(2)}, u32[]{:S(2)}) %collective-permute-start.25) | collective-permute-done | bytes 131104 | tf_op jit(solution)/shard_map/ppermute | solution.py:265
  (81 shorter events, 14.5 us)
Async XLA Ops:
  3.9 10.1 %collective-permute-start.2 = (f32[32,256]{1,0:T(8,128)S(1)}, f32[32,256]{1,0:T(8,128)S(1)}, u32[]{:S(2)}, u32[]{:S(2)}) collective-permute-start(f32[32,256]{1,0:T(8,128)S(1)} %fusion.2), channel_id=1, source_target_pairs={{0,1},{1,0},{2,3},{3,2},{4,5},{5,4},{6,7},{7,6},{8,9},{9,8},{10,11... | collective-permute-start | bytes 98312 | tf_op jit(solution)/shard_map/ppermute | solution.py:259
  7.0 18.3 %collective-permute-start = (bf16[256,1024]{1,0:T(8,128)(2,1)S(1)}, bf16[256,1024]{1,0:T(8,128)(2,1)S(1)}, u32[]{:S(2)}, u32[]{:S(2)}) collective-permute-start(bf16[256,1024]{1,0:T(8,128)(2,1)S(1)} %constant_dynamic-update-slice_fusion.refs_9_), channel_id=1, source_target_pairs={{0,4},{1,5},{2,6},{3,7},{4,0},{6,2},{8,12},{9,13},{10,14},{11,15},... | collective-permute-start | bytes 1572872 | tf_op jit(solution)/shard_map/ppermute | solution.py:208
  10.5 14.8 %collective-permute-start.1 = (bf16[256,1024]{1,0:T(8,128)(2,1)S(1)}, bf16[256,1024]{1,0:T(8,128)(2,1)S(1)}, u32[]{:S(2)}, u32[]{:S(2)}) collective-permute-start(bf16[256,1024]{1,0:T(8,128)(2,1)S(1)} %constant_dynamic-update-slice_fusion.refs_9_), channel_id=1, source_target_pairs={{0,8},{2,10},{4,12},{6,14},{9,17},{11,19},{13,21},{15,23},{16,24},... | collective-permute-start | bytes 1572872 | tf_op jit(solution)/shard_map/ppermute | solution.py:208
  15.3 7.4 %collective-permute-start.4 = (bf16[16,512]{1,0:T(8,128)(2,1)S(1)}, bf16[16,512]{1,0:T(8,128)(2,1)S(1)}, u32[]{:S(2)}, u32[]{:S(2)}) collective-permute-start(bf16[16,512]{1,0:T(8,128)(2,1)S(1)} %pad_maximum_fusion.2.refs_5_), channel_id=1, source_target_pairs={{0,4},{1,5},{2,6},{3,7},{4,0},{5,1},{6,2},{7,3},{8,12},{9,13},{10,... | collective-permute-start | bytes 49160 | tf_op jit(solution)/shard_map/ppermute | solution.py:208
  15.3 9.8 %collective-permute-start.5 = (bf16[16,512]{1,0:T(8,128)(2,1)S(1)}, bf16[16,512]{1,0:T(8,128)(2,1)S(1)}, u32[]{:S(2)}, u32[]{:S(2)}) collective-permute-start(bf16[16,512]{1,0:T(8,128)(2,1)S(1)} %pad_maximum_fusion.2.refs_5_), channel_id=1, source_target_pairs={{0,8},{2,10},{4,12},{6,14},{9,17},{11,19},{13,21},{15,23},{16,24},... | collective-permute-start | bytes 49160 | tf_op jit(solution)/shard_map/ppermute | solution.py:208
  16.7 8.6 %collective-permute-start.6 = (bf16[16,512]{1,0:T(8,128)(2,1)S(1)}, bf16[16,512]{1,0:T(8,128)(2,1)S(1)}, u32[]{:S(2)}, u32[]{:S(2)}) collective-permute-start(bf16[16,512]{1,0:T(8,128)(2,1)S(1)} %pad_maximum_fusion.2.refs_5_), channel_id=1, source_target_pairs={{0,12},{2,14},{4,8},{6,10},{9,21},{11,23},{13,17},{15,19},{16,28},... | collective-permute-start | bytes 49160 | tf_op jit(solution)/shard_map/ppermute | solution.py:208
  22.6 11.3 %collective-permute-start.7 = (bf16[256,1024]{1,0:T(8,128)(2,1)S(1)}, bf16[256,1024]{1,0:T(8,128)(2,1)S(1)}, u32[]{:S(2)}, u32[]{:S(2)}) collective-permute-start(bf16[256,1024]{1,0:T(8,128)(2,1)S(1)} %constant_dynamic-update-slice_fusion.refs_9_), channel_id=1, source_target_pairs={{0,2},{1,3},{2,0},{3,1},{4,6},{5,7},{6,4},{7,5},{8,10},{9,11},{10,... | collective-permute-start | bytes 1572872 | tf_op jit(solution)/shard_map/ppermute | solution.py:208
  25.3 8.1 %collective-permute-start.10 = (bf16[128,1024]{1,0:T(8,128)(2,1)S(1)}, bf16[128,1024]{1,0:T(8,128)(2,1)S(1)}, u32[]{:S(2)}, u32[]{:S(2)}) collective-permute-start(bf16[128,1024]{1,0:T(8,128)(2,1)S(1)} %slice.44), channel_id=1, source_target_pairs={{0,8},{2,10},{4,12},{6,14},{9,17},{11,19},{13,21},{15,23},{16,24},... | collective-permute-start | bytes 786440 | tf_op jit(solution)/shard_map/ppermute | solution.py:208
  29.6 3.8 %collective-permute-start.11 = (bf16[128,1024]{1,0:T(8,128)(2,1)S(1)}, bf16[128,1024]{1,0:T(8,128)(2,1)S(1)}, u32[]{:S(2)}, u32[]{:S(2)}) collective-permute-start(bf16[128,1024]{1,0:T(8,128)(2,1)S(1)} %slice.45), channel_id=1, source_target_pairs={{1,5},{3,7},{5,1},{7,3},{8,12},{10,14},{12,8},{14,10},{17,21},{19,... | collective-permute-start | bytes 786440 | tf_op jit(solution)/shard_map/ppermute | solution.py:208
  30.3 5.1 %collective-permute-start.8 = (bf16[256,1024]{1,0:T(8,128)(2,1)S(1)}, bf16[256,1024]{1,0:T(8,128)(2,1)S(1)}, u32[]{:S(2)}, u32[]{:S(2)}) collective-permute-start(bf16[256,1024]{1,0:T(8,128)(2,1)S(1)} %collective-permute-done.refs_11_), channel_id=1, source_target_pairs={{0,2},{1,3},{2,0},{3,1},{4,6},{5,7},{6,4},{7,5},{8,10},{9,11},{10,... | collective-permute-start | bytes 1572872 | tf_op jit(solution)/shard_map/ppermute | solution.py:208
  30.3 5.0 %collective-permute-start.9 = (bf16[256,1024]{1,0:T(8,128)(2,1)S(1)}, bf16[256,1024]{1,0:T(8,128)(2,1)S(1)}, u32[]{:S(2)}, u32[]{:S(2)}) collective-permute-start(bf16[256,1024]{1,0:T(8,128)(2,1)S(1)} %collective-permute-done.1.refs_13_), channel_id=1, source_target_pairs={{0,2},{1,3},{2,0},{3,1},{4,6},{5,7},{6,4},{7,5},{8,10},{9,11},{10,... | collective-permute-start | bytes 1572872 | tf_op jit(solution)/shard_map/ppermute | solution.py:208
  33.4 1.9 %collective-permute-start.13 = (bf16[128,1024]{1,0:T(8,128)(2,1)S(1)}, bf16[128,1024]{1,0:T(8,128)(2,1)S(1)}, u32[]{:S(2)}, u32[]{:S(2)}) collective-permute-start(bf16[128,1024]{1,0:T(8,128)(2,1)S(1)} %collective-permute-done.11.refs_16_), channel_id=1, source_target_pairs={{0,2},{1,3},{2,0},{3,1},{4,6},{5,7},{6,4},{7,5},{8,10},{9,11},{10,... | collective-permute-start | bytes 786440 | tf_op jit(solution)/shard_map/ppermute | solution.py:208
  55.0 12.7 %collective-permute-start.15 = (f32[16,2,256]{2,0,1:T(8,128)S(1)}, f32[16,2,256]{2,0,1:T(8,128)S(1)}, u32[]{:S(2)}, u32[]{:S(2)}) collective-permute-start(f32[16,2,256]{2,0,1:T(8,128)S(1)} %copy.17), channel_id=1, source_target_pairs={{0,4},{1,5},{2,6},{3,7},{4,0},{5,1},{6,2},{7,3},{8,12},{9,13},{10,... | collective-permute-start | bytes 98312 | tf_op jit(solution)/shard_map/ppermute | solution.py:208
  65.9 3.2 %collective-permute-start.20 = (bf16[16,2304]{1,0:T(8,128)(2,1)S(1)}, bf16[16,2304]{1,0:T(8,128)(2,1)S(1)}, u32[]{:S(2)}, u32[]{:S(2)}) collective-permute-start(bf16[16,2304]{1,0:T(8,128)(2,1)S(1)} %broadcast_select_fusion.3), channel_id=1, source_target_pairs={{0,2},{2,0},{4,6},{6,4},{8,10},{10,8},{12,14},{14,12},{16,18},{18,... | collective-permute-start | bytes 221192 | tf_op jit(solution)/shard_map/ppermute | solution.py:265
  67.7 25.7 %collective-permute-start.16 = (f32[16,256]{1,0:T(8,128)S(1)}, f32[16,256]{1,0:T(8,128)S(1)}, u32[]{:S(2)}, u32[]{:S(2)}) collective-permute-start(f32[16,256]{1,0:T(8,128)S(1)} %slice_bitcast_fusion), channel_id=1, source_target_pairs={{1,25},{3,27},{5,29},{7,31},{8,0},{10,2},{12,4},{14,6},{17,9},{19,... | collective-permute-start | bytes 49160 | tf_op jit(solution)/shard_map/ppermute | solution.py:208
  69.1 26.4 %collective-permute-start.21 = (bf16[16,2304]{1,0:T(8,128)(2,1)S(1)}, bf16[16,2304]{1,0:T(8,128)(2,1)S(1)}, u32[]{:S(2)}, u32[]{:S(2)}) collective-permute-start(bf16[16,2304]{1,0:T(8,128)(2,1)S(1)} %add_convert_fusion.7), channel_id=1, source_target_pairs={{0,4},{2,6},{4,0},{6,2},{8,12},{10,14},{12,8},{14,10},{16,20},{18,... | collective-permute-start | bytes 221192 | tf_op jit(solution)/shard_map/ppermute | solution.py:265
  93.5 4.0 %collective-permute-start.17 = (f32[32,256]{1,0:T(8,128)S(1)}, f32[32,256]{1,0:T(8,128)S(1)}, u32[]{:S(2)}, u32[]{:S(2)}) collective-permute-start(f32[32,256]{1,0:T(8,128)S(1)} %pad_maximum_fusion.1), channel_id=1, source_target_pairs={{0,1},{1,0},{2,3},{3,2},{4,5},{5,4},{6,7},{7,6},{8,9},{9,8},{10,11... | collective-permute-start | bytes 98312 | tf_op jit(solution)/shard_map/ppermute | solution.py:259
  95.6 4.4 %collective-permute-start.22 = (bf16[16,2304]{1,0:T(8,128)(2,1)S(1)}, bf16[16,2304]{1,0:T(8,128)(2,1)S(1)}, u32[]{:S(2)}, u32[]{:S(2)}) collective-permute-start(bf16[16,2304]{1,0:T(8,128)(2,1)S(1)} %add_convert_fusion.6), channel_id=1, source_target_pairs={{0,8},{2,10},{4,12},{6,14},{8,0},{10,2},{12,4},{14,6},{16,24},{18,... | collective-permute-start | bytes 221192 | tf_op jit(solution)/shard_map/ppermute | solution.py:265
  98.0 4.0 %collective-permute-start.18 = (bf16[16,4096]{1,0:T(8,128)(2,1)S(1)}, bf16[16,4096]{1,0:T(8,128)(2,1)S(1)}, u32[]{:S(2)}, u32[]{:S(2)}) collective-permute-start(bf16[16,4096]{1,0:T(8,128)(2,1)S(1)} %broadcast_select_fusion), channel_id=1, source_target_pairs={{0,2},{2,0},{4,6},{6,4},{8,10},{10,8},{12,14},{14,12},{16,18},{18,... | collective-permute-start | bytes 393224 | tf_op jit(solution)/shard_map/ppermute | solution.py:265
  100.0 6.1 %collective-permute-start.23 = (bf16[16,2304]{1,0:T(8,128)(2,1)S(1)}, bf16[16,2304]{1,0:T(8,128)(2,1)S(1)}, u32[]{:S(2)}, u32[]{:S(2)}) collective-permute-start(bf16[16,2304]{1,0:T(8,128)(2,1)S(1)} %add_convert_fusion.5), channel_id=1, source_target_pairs={{0,16},{2,18},{4,20},{6,22},{8,24},{10,26},{12,28},{14,30},{16,0},... | collective-permute-start | bytes 221192 | tf_op jit(solution)/shard_map/ppermute | solution.py:265
  102.1 5.0 %collective-permute-start.19 = (bf16[16,4096]{1,0:T(8,128)(2,1)S(1)}, bf16[16,4096]{1,0:T(8,128)(2,1)S(1)}, u32[]{:S(2)}, u32[]{:S(2)}) collective-permute-start(bf16[16,4096]{1,0:T(8,128)(2,1)S(1)} %add_convert_fusion.3), channel_id=1, source_target_pairs={{0,4},{2,6},{4,0},{6,2},{8,12},{10,14},{12,8},{14,10},{16,20},{18,... | collective-permute-start | bytes 393224 | tf_op jit(solution)/shard_map/ppermute | solution.py:265
  107.1 5.9 %collective-permute-start.24 = (bf16[16,4096]{1,0:T(8,128)(2,1)S(1)}, bf16[16,4096]{1,0:T(8,128)(2,1)S(1)}, u32[]{:S(2)}, u32[]{:S(2)}) collective-permute-start(bf16[16,4096]{1,0:T(8,128)(2,1)S(1)} %add_convert_fusion.2), channel_id=1, source_target_pairs={{0,8},{2,10},{4,12},{6,14},{8,0},{10,2},{12,4},{14,6},{16,24},{18,... | collective-permute-start | bytes 393224 | tf_op jit(solution)/shard_map/ppermute | solution.py:265
  109.2 4.1 %collective-permute-start.27 = (bf16[16,2304]{1,0:T(8,128)(2,1)S(1)}, bf16[16,2304]{1,0:T(8,128)(2,1)S(1)}, u32[]{:S(2)}, u32[]{:S(2)}) collective-permute-start(bf16[16,2304]{1,0:T(8,128)(2,1)S(1)} %add_convert_fusion.4), channel_id=1, source_target_pairs={{0,2},{2,0},{4,6},{6,4},{8,10},{10,8},{12,14},{14,12},{16,18},{18,... | collective-permute-start | bytes 221192 | tf_op jit(solution)/shard_map/ppermute | solution.py:265
  113.0 5.9 %collective-permute-start.25 = (bf16[16,4096]{1,0:T(8,128)(2,1)S(1)}, bf16[16,4096]{1,0:T(8,128)(2,1)S(1)}, u32[]{:S(2)}, u32[]{:S(2)}) collective-permute-start(bf16[16,4096]{1,0:T(8,128)(2,1)S(1)} %add_convert_fusion.1), channel_id=1, source_target_pairs={{0,16},{2,18},{4,20},{6,22},{8,24},{10,26},{12,28},{14,30},{16,0},... | collective-permute-start | bytes 393224 | tf_op jit(solution)/shard_map/ppermute | solution.py:265
  (11 other events, 97.1 us)
